TPU v7x, 32 devices: a whole 2x2x4 slice. The times are simulated.
32 devices in a mesh: col: 4 (over y, x), row: 8 (over z, core).
Axes of the slice: x: 2, y: 2, z: 4, core: 2. Of those that a mesh axis runs over, the one named last changes fastest.
Arguments:
- lengths: int32 [2, 32], P(None, ('col', 'row')), may hold values from 2 to 1024, as said below
- items: int32 [2, 32, 1024], P(None, ('col', 'row')), may hold values from 0 to 25599, as said below
- negatives: int32 [512], replicated, may hold values from 0 to 25599, as said below
- time_buckets: int32 [2, 32, 1024], P(None, ('col', 'row')), may hold values from 0 to 63, as said below
- table: float32 [25600, 512], P('row', 'col'), may hold values from -0.6 to 0.6
- table_m: float32 [25600, 512], P('row', 'col'), may hold values from -1.4305115e-06 to 1.4305115e-06
- table_v: float32 [25600, 512], P('row', 'col'), may hold values from 4.7683716e-15 to 1.9073486e-14
- w_in: float32 [512, 2048], P(('col', 'row')), may hold values from -0.25 to 0.25
- w_in_m: float32 [512, 2048], P(('col', 'row')), may hold values from -2.670288e-05 to 2.670288e-05
- w_in_v: float32 [512, 2048], P(('col', 'row')), may hold values from 1.5449524e-12 to 6.1798097e-12
- w_out: float32 [512, 512], P(('col', 'row')), may hold values from -0.0390625 to 0.0390625
- w_out_m: float32 [512, 512], P(('col', 'row')), may hold values from -2.670288e-05 to 2.670288e-05
- w_out_v: float32 [512, 512], P(('col', 'row')), may hold values from 1.5449524e-12 to 6.1798097e-12
- gains: float32 [3, 512], P(None, ('col', 'row')), may hold values from 0.28 to 2.6
- gains_m: float32 [3, 512], P(None, ('col', 'row')), may hold values from -5.340576e-05 to 5.340576e-05
- gains_v: float32 [3, 512], P(None, ('col', 'row')), may hold values from 6.1798097e-12 to 2.4719239e-11
- rab: float32 [8, 32], replicated, may hold values from -4 to 4
- rab_m: float32 [8, 32], replicated, may hold values from -7.6293945e-06 to 7.6293945e-06
- rab_v: float32 [8, 32], replicated, may hold values from 1.7166138e-13 to 6.866455e-13
Outputs:
- loss_sum: float32 [], replicated
- loss_count: float32 [], replicated
- grad_norm: float32 [], replicated
- table_new: float32 [25600, 512], P('row', 'col')
- table_m_new: float32 [25600, 512], P('row', 'col')
- table_v_new: float32 [25600, 512], P('row', 'col')
- table_low: bfloat16 [25600, 512], P('row', 'col')
- w_in_new: float32 [512, 2048], P(('col', 'row'))
- w_in_m_new: float32 [512, 2048], P(('col', 'row'))
- w_in_v_new: float32 [512, 2048], P(('col', 'row'))
- w_in_low: bfloat16 [512, 2048], P(('col', 'row'))
- w_out_new: float32 [512, 512], P(('col', 'row'))
- w_out_m_new: float32 [512, 512], P(('col', 'row'))
- w_out_v_new: float32 [512, 512], P(('col', 'row'))
- w_out_low: bfloat16 [512, 512], P(('col', 'row'))
- gains_new: float32 [3, 512], P(None, ('col', 'row'))
- gains_m_new: float32 [3, 512], P(None, ('col', 'row'))
- gains_v_new: float32 [3, 512], P(None, ('col', 'row'))
- rab_new: float32 [8, 32], replicated
- rab_m_new: float32 [8, 32], replicated
- rab_v_new: float32 [8, 32], replicated
Inputs may be any that keep to these rules, and one draw needn't show every extreme that they name: lengths reach 1024 in every draw. In each history, exactly 128 events name items of each block of 3200 rows. negatives[j] lies in the block of 3200 rows number j // 64. `time_buckets`: nondecreasing along each history, 0 at its first slot.
All inputs are finite; a program needn't handle non-finite values.
Results may differ from a plain program's by a relative error of at most 0.0081.
Values may be sent and summed in bfloat16 or wider, within the bound.
No kernel may reach another device: no remote copies, remote signals or barrier semaphores. Data moves between devices by JAX's collectives and lax.ppermute only.
A program may use at most 192 MiB of HBM per device.

v0:
```python
import jax
import jax.numpy as jnp
from jax import lax
from jax.sharding import PartitionSpec as P

SEQ = 1024
NB = 32
NBT = 64
STEP = 10


BETA_ONE = 0.9
BETA_TWO = 0.999
EPS_ADAM = 1e-08
EPS_NORM = 1e-06
WEIGHT_DECAY = 0.01
CLIP_NORM = 0.05
RATE_TABLE = 0.06
RATE_DENSE = 0.01
RATE_SMALL = 0.5
SCORE_SCALE = 0.5


def silu_parts(values):
    sigmoid = jax.nn.sigmoid(values)
    return (values * sigmoid, sigmoid * (1.0 + values * (1.0 - sigmoid)))


def rms_scale(values):
    return lax.rsqrt(jnp.mean(values * values, axis=-1, keepdims=True) + EPS_NORM)


def rms_back(values, norm_scale, grad_normed):
    cubed = norm_scale * norm_scale * norm_scale
    return norm_scale * grad_normed - values * cubed * jnp.mean(
        grad_normed * values, axis=-1, keepdims=True
    )


def to_heads(values, head_count):
    return values.reshape(values.shape[0], head_count, values.shape[1] // head_count).transpose(
        1, 0, 2
    )


def from_heads(values):
    return values.transpose(1, 0, 2).reshape(values.shape[1], values.shape[0] * values.shape[2])


def head_scores(head_query, head_keys, bias_row, relative, visible):
    scores = (
        SCORE_SCALE
        * jnp.einsum("id,jd->ij", head_query, head_keys, preferred_element_type=jnp.float32)
        + bias_row[relative]
    )
    active, grad_slope = silu_parts(scores)
    attend = (jnp.where(visible, active, 0.0) / SEQ).astype(jnp.bfloat16)
    return (attend, grad_slope)


def head_forward(head_parts, relative, visible):
    head_query, head_keys, head_value, bias_row = head_parts
    attend, _ = head_scores(head_query, head_keys, bias_row, relative, visible)
    return jnp.dot(attend, head_value, preferred_element_type=jnp.float32)


def head_backward(head_parts, relative, visible, bucket_low, bucket_full):
    head_query, head_keys, head_value, grad_out, bias_row = head_parts
    attend, grad_slope = head_scores(head_query, head_keys, bias_row, relative, visible)
    grad_attend = jnp.einsum("id,jd->ij", grad_out, head_value, preferred_element_type=jnp.float32)
    grad_value = jnp.einsum("ij,id->jd", attend, grad_out, preferred_element_type=jnp.float32)
    grad_scores = jnp.where(visible, grad_attend / SEQ * grad_slope, 0.0).astype(jnp.bfloat16)
    grad_query = SCORE_SCALE * jnp.einsum(
        "ij,jd->id", grad_scores, head_keys, preferred_element_type=jnp.float32
    )
    grad_keys = SCORE_SCALE * jnp.einsum(
        "ij,id->jd", grad_scores, head_query, preferred_element_type=jnp.float32
    )
    bucket_rows = jnp.einsum(
        "ia,ij->aj", bucket_low, grad_scores, preferred_element_type=jnp.float32
    )
    bucket_pairs = jnp.dot(bucket_rows, bucket_full, precision=lax.Precision.HIGHEST)
    return (grad_query, grad_keys, grad_value, bucket_pairs)


def layer_forward(embedded, w_big, w_small, gain_all, bias_table, neg_rows, buckets, length):
    seq_len, model_width = embedded.shape
    head_count = bias_table.shape[0]
    embed_f = embedded.astype(jnp.float32)
    scale_in = rms_scale(embed_f)
    normed = (embed_f * scale_in * gain_all[0]).astype(jnp.bfloat16)
    project = jnp.dot(normed, w_big, preferred_element_type=jnp.float32)
    active, _ = silu_parts(project)
    gate_part = active[:, :model_width]
    rounded = active[:, model_width:].astype(jnp.bfloat16)
    value_heads = to_heads(rounded[:, :model_width], head_count)
    query_heads = to_heads(rounded[:, model_width : 2 * model_width], head_count)
    keys_heads = to_heads(rounded[:, 2 * model_width :], head_count)
    relative = jnp.clip(buckets[:, None] - buckets[None, :], 0, NB - 1)
    places = jnp.arange(seq_len)
    visible = (places[None, :] <= places[:, None]) & (places[None, :] < length)
    bucket_full = (buckets[:, None] == jnp.arange(NBT)[None, :]).astype(jnp.float32)
    attended = lax.map(
        lambda head_parts: head_forward(head_parts, relative, visible),
        (query_heads, keys_heads, value_heads, bias_table),
    )
    merged = from_heads(attended)
    scale_mid = rms_scale(merged)
    mixed_low = (merged * scale_mid * gain_all[1] * gate_part).astype(jnp.bfloat16)
    hidden = embed_f + jnp.dot(mixed_low, w_small, preferred_element_type=jnp.float32)
    scale_out = rms_scale(hidden)
    final_out = (hidden * scale_out * gain_all[2]).astype(jnp.bfloat16)
    target = jnp.concatenate([embed_f[1:], jnp.zeros((1, model_width), jnp.float32)], axis=0)
    positive = jnp.sum(final_out.astype(jnp.float32) * target, axis=-1)
    negative = jnp.einsum("id,nd->in", final_out, neg_rows, preferred_element_type=jnp.float32)
    highest = jnp.maximum(jnp.max(negative, axis=-1), positive)
    neg_exp = jnp.exp(negative - highest[:, None])
    pos_exp = jnp.exp(positive - highest)
    totals = pos_exp + jnp.sum(neg_exp, axis=-1)
    valid_rows = places < length - 1
    loss_local = jnp.sum(jnp.where(valid_rows, highest + jnp.log(totals) - positive, 0.0))
    kept = (
        embed_f,
        scale_in,
        normed,
        project,
        gate_part,
        query_heads,
        keys_heads,
        value_heads,
        relative,
        visible,
        bucket_full,
        merged,
        scale_mid,
        mixed_low,
        hidden,
        scale_out,
        final_out,
        target,
        neg_exp,
        pos_exp,
        totals,
        valid_rows,
    )
    return (loss_local, kept)


def layer_backward(kept, w_big, w_small, gain_all, bias_table, neg_rows):
    (
        embed_f,
        scale_in,
        normed,
        project,
        gate_part,
        query_heads,
        keys_heads,
        value_heads,
        relative,
        visible,
        bucket_full,
        merged,
        scale_mid,
        mixed_low,
        hidden,
        scale_out,
        final_out,
        target,
        neg_exp,
        pos_exp,
        totals,
        valid_rows,
    ) = kept
    head_count = bias_table.shape[0]
    model_width = embed_f.shape[1]
    counted = jnp.where(valid_rows, 1.0, 0.0)
    grad_neg = (counted[:, None] * neg_exp / totals[:, None]).astype(jnp.bfloat16)
    grad_pos = counted * (pos_exp / totals - 1.0)
    final_f = final_out.astype(jnp.float32)
    grad_final = (
        jnp.dot(grad_neg, neg_rows, preferred_element_type=jnp.float32) + grad_pos[:, None] * target
    )
    grad_negrows = jnp.einsum("in,id->nd", grad_neg, final_out, preferred_element_type=jnp.float32)
    grad_embed = jnp.concatenate(
        [jnp.zeros((1, model_width), jnp.float32), grad_pos[:-1, None] * final_f[:-1]], axis=0
    )
    grad_gain_out = jnp.sum(grad_final * hidden * scale_out, axis=0)
    grad_hidden = rms_back(hidden, scale_out, grad_final * gain_all[2])
    grad_branch = grad_hidden.astype(jnp.bfloat16)
    grad_small = jnp.einsum("id,ie->de", mixed_low, grad_branch, preferred_element_type=jnp.float32)
    grad_mixed = jnp.einsum("ie,de->id", grad_branch, w_small, preferred_element_type=jnp.float32)
    normed_mid = merged * scale_mid
    grad_gain_mid = jnp.sum(grad_mixed * normed_mid * gate_part, axis=0)
    grad_gate = grad_mixed * normed_mid * gain_all[1]
    grad_merged = rms_back(merged, scale_mid, grad_mixed * gain_all[1] * gate_part)
    grad_heads = to_heads(grad_merged.astype(jnp.bfloat16), head_count)
    bucket_low = bucket_full.astype(jnp.bfloat16)
    grad_query, grad_keys, grad_value, bucket_pairs = lax.map(
        lambda head_parts: head_backward(head_parts, relative, visible, bucket_low, bucket_full),
        (query_heads, keys_heads, value_heads, grad_heads, bias_table),
    )
    first_bucket = jnp.arange(NBT)[:, None, None]
    second_bucket = jnp.arange(NBT)[None, :, None]
    fold_table = (
        jnp.clip(first_bucket - second_bucket, 0, NB - 1) == jnp.arange(NB)[None, None, :]
    ).astype(jnp.float32)
    grad_rab = jnp.einsum("hab,abr->hr", bucket_pairs, fold_table, precision=lax.Precision.HIGHEST)
    grad_active = jnp.concatenate(
        [grad_gate, from_heads(grad_value), from_heads(grad_query), from_heads(grad_keys)], axis=1
    )
    _, project_slope = silu_parts(project)
    grad_project = (grad_active * project_slope).astype(jnp.bfloat16)
    grad_big = jnp.einsum("id,ie->de", normed, grad_project, preferred_element_type=jnp.float32)
    grad_normed = jnp.einsum("ie,de->id", grad_project, w_big, preferred_element_type=jnp.float32)
    grad_gain_in = jnp.sum(grad_normed * embed_f * scale_in, axis=0)
    grad_embed = grad_embed + grad_hidden + rms_back(embed_f, scale_in, grad_normed * gain_all[0])
    grad_gain = jnp.stack([grad_gain_in, grad_gain_mid, grad_gain_out])
    return (grad_embed, grad_big, grad_small, grad_gain, grad_rab, grad_negrows)


def adamw_update(weight, first, second, grad, rate):
    first = BETA_ONE * first + (1.0 - BETA_ONE) * grad
    second = BETA_TWO * second + (1.0 - BETA_TWO) * grad * grad
    fixed_first = first / (1.0 - BETA_ONE**STEP)
    fixed_second = second / (1.0 - BETA_TWO**STEP)
    weight = weight - rate * (
        fixed_first / (jnp.sqrt(fixed_second) + EPS_ADAM) + WEIGHT_DECAY * weight
    )
    return (weight, first, second)


def local(
    lengths,
    items,
    negatives,
    time_buckets,
    table,
    table_m,
    table_v,
    w_in,
    w_in_m,
    w_in_v,
    w_out,
    w_out_m,
    w_out_v,
    gains,
    gains_m,
    gains_v,
    rab,
    rab_m,
    rab_v,
):
    col_count = lax.axis_size("col")
    row_count = lax.axis_size("row")
    row_place = lax.axis_index("row")
    rows_dev, col_piece = table.shape
    model_width = w_in.shape[1] // 4
    seq_len = items.shape[2]
    neg_total = negatives.shape[0]
    neg_own = neg_total // row_count
    table_b = table.astype(jnp.bfloat16)
    own_negs = (
        lax.dynamic_slice_in_dim(negatives, row_place * neg_own, neg_own) - row_place * rows_dev
    )
    neg_gathered = lax.all_gather(table_b[own_negs], ("col", "row"), axis=0, tiled=True)
    neg_rows = (
        neg_gathered.reshape(col_count, row_count, neg_own, col_piece)
        .transpose(1, 2, 0, 3)
        .reshape(neg_total, model_width)
    )
    shard_big = jnp.zeros(w_in.shape, jnp.float32)
    shard_small = jnp.zeros(w_out.shape, jnp.float32)
    shard_gain = jnp.zeros(gains.shape, jnp.float32)
    table_grad = jnp.zeros(table.shape, jnp.float32)
    negs_grad = jnp.zeros((neg_total, model_width), jnp.float32)
    rab_grad = jnp.zeros(rab.shape, jnp.float32)
    loss_total = jnp.zeros((), jnp.float32)
    count_total = jnp.zeros((), jnp.float32)
    for micro_batch in range(items.shape[0]):
        w_big, w_small, gain_all = (
            lax.all_gather(w_in.astype(jnp.bfloat16), ("col", "row"), axis=0, tiled=True),
            lax.all_gather(w_out.astype(jnp.bfloat16), ("col", "row"), axis=0, tiled=True),
            lax.all_gather(gains.astype(jnp.bfloat16), ("col", "row"), axis=1, tiled=True),
        )
        length = lengths[micro_batch, 0]
        group_ids = lax.all_gather(items[micro_batch, 0][None], "col", axis=0, tiled=True).reshape(
            -1
        )
        owner_order = jnp.argsort(group_ids // rows_dev, stable=True)
        inverse = jnp.argsort(owner_order, stable=True)
        requests = group_ids[owner_order].reshape(row_count, -1)
        incoming = lax.all_to_all(requests, "row", split_axis=0, concat_axis=0, tiled=True)
        found_rows = table_b[incoming - row_place * rows_dev]
        returned = lax.all_to_all(found_rows, "row", split_axis=0, concat_axis=0, tiled=True)
        event_rows = returned.reshape(-1, col_piece)[inverse].reshape(col_count, seq_len, col_piece)
        embedded = lax.all_to_all(event_rows, "col", split_axis=0, concat_axis=2, tiled=True)[0]
        loss_local, kept = layer_forward(
            embedded, w_big, w_small, gain_all, rab, neg_rows, time_buckets[micro_batch, 0], length
        )
        grad_embed, grad_big, grad_small, grad_gain, grad_bias, grad_negrows = layer_backward(
            kept, w_big, w_small, gain_all, rab, neg_rows
        )
        grad_low = grad_embed.astype(jnp.bfloat16)
        grad_pieces = lax.all_to_all(grad_low[None], "col", split_axis=2, concat_axis=0, tiled=True)
        sorted_grads = grad_pieces.reshape(-1, col_piece)[owner_order].reshape(
            row_count, -1, col_piece
        )
        arriving = lax.all_to_all(sorted_grads, "row", split_axis=0, concat_axis=0, tiled=True)
        local_rows = (incoming - row_place * rows_dev).reshape(-1)
        table_grad = table_grad.at[local_rows].add(
            arriving.reshape(-1, col_piece).astype(jnp.float32)
        )
        negs_grad = negs_grad + grad_negrows
        rab_grad = rab_grad + grad_bias
        loss_total = loss_total + loss_local
        count_total = count_total + jnp.maximum(length - 1, 0).astype(jnp.float32)
        shard_big = shard_big + lax.psum_scatter(
            grad_big, ("col", "row"), scatter_dimension=0, tiled=True
        )
        shard_small = shard_small + lax.psum_scatter(
            grad_small, ("col", "row"), scatter_dimension=0, tiled=True
        )
        shard_gain = shard_gain + lax.psum_scatter(
            grad_gain, ("col", "row"), scatter_dimension=1, tiled=True
        )
    rab_sum, loss_sum, loss_count = lax.psum((rab_grad, loss_total, count_total), ("col", "row"))
    neg_layout = (
        negs_grad.reshape(row_count, neg_own, col_count, col_piece)
        .transpose(2, 0, 1, 3)
        .reshape(-1, col_piece)
    )
    neg_share = lax.psum_scatter(neg_layout, ("col", "row"), scatter_dimension=0, tiled=True)
    table_grad = table_grad.at[own_negs].add(neg_share)
    grad_table = table_grad / loss_count
    grad_big = shard_big / loss_count
    grad_small = shard_small / loss_count
    grad_gain = shard_gain / loss_count
    grad_rab = rab_sum / loss_count
    local_squares = (
        jnp.sum(grad_table * grad_table)
        + jnp.sum(grad_big * grad_big)
        + jnp.sum(grad_small * grad_small)
        + jnp.sum(grad_gain * grad_gain)
    )
    grad_norm = jnp.sqrt(lax.psum(local_squares, ("col", "row")) + jnp.sum(grad_rab * grad_rab))
    factor = jnp.minimum(1.0, CLIP_NORM / grad_norm)
    table_new, table_m_new, table_v_new = adamw_update(
        table, table_m, table_v, grad_table * factor, RATE_TABLE
    )
    w_in_new, w_in_m_new, w_in_v_new = adamw_update(
        w_in, w_in_m, w_in_v, grad_big * factor, RATE_DENSE
    )
    w_out_new, w_out_m_new, w_out_v_new = adamw_update(
        w_out, w_out_m, w_out_v, grad_small * factor, RATE_DENSE
    )
    gains_new, gains_m_new, gains_v_new = adamw_update(
        gains, gains_m, gains_v, grad_gain * factor, RATE_SMALL
    )
    rab_new, rab_m_new, rab_v_new = adamw_update(rab, rab_m, rab_v, grad_rab * factor, RATE_SMALL)
    return (
        loss_sum,
        loss_count,
        grad_norm,
        table_new,
        table_m_new,
        table_v_new,
        table_new.astype(jnp.bfloat16),
        w_in_new,
        w_in_m_new,
        w_in_v_new,
        w_in_new.astype(jnp.bfloat16),
        w_out_new,
        w_out_m_new,
        w_out_v_new,
        w_out_new.astype(jnp.bfloat16),
        gains_new,
        gains_m_new,
        gains_v_new,
        rab_new,
        rab_m_new,
        rab_v_new,
    )


def solution(mesh):
    placed = (
        P(None, ("col", "row")),
        P(None, ("col", "row"), None),
        P(),
        P(None, ("col", "row"), None),
        P("row", "col"),
        P("row", "col"),
        P("row", "col"),
        P(("col", "row"), None),
        P(("col", "row"), None),
        P(("col", "row"), None),
        P(("col", "row"), None),
        P(("col", "row"), None),
        P(("col", "row"), None),
        P(None, ("col", "row")),
        P(None, ("col", "row")),
        P(None, ("col", "row")),
        P(),
        P(),
        P(),
    )
    return jax.shard_map(
        local,
        mesh=mesh,
        in_specs=placed,
        out_specs=(
            P(),
            P(),
            P(),
            P("row", "col"),
            P("row", "col"),
            P("row", "col"),
            P("row", "col"),
            P(("col", "row"), None),
            P(("col", "row"), None),
            P(("col", "row"), None),
            P(("col", "row"), None),
            P(("col", "row"), None),
            P(("col", "row"), None),
            P(("col", "row"), None),
            P(("col", "row"), None),
            P(None, ("col", "row")),
            P(None, ("col", "row")),
            P(None, ("col", "row")),
            P(),
            P(),
            P(),
        ),
        check_vma=False,
    )
```

profile of v0, /device:TPU:0, one launch (start us, length us, event | category | flops | bytes accessed | tf_op | source)
XLA Modules:
  0.0 2330.9 jit_solution(3270868495967650146)
XLA Ops:
  23.3 40.6 %gather_fusion = s32[4096]{0:T(1024)} fusion(s32[4096]{0:T(1024)S(1)} %bitcast.2620, s32[4096]{0:T(1024)S(1)} %fusion.554), kind=kCustom, calls=%fused_computation | custom fusion | bytes 49152 | tf_op jit(solution)/shard_map/gather | solution.py:291
  82.7 40.6 %gather_fusion.4 = s32[4096]{0:T(1024)} fusion(s32[4096]{0:T(1024)S(1)} %bitcast.2622, s32[4096]{0:T(1024)S(1)} %fusion.556), kind=kCustom, calls=%fused_computation.4 | custom fusion | bytes 49152 | tf_op jit(solution)/shard_map/gather | solution.py:291
  195.7 44.6 %all-gather.3 = bf16[32,16,3]{1,2,0:T(4,128)(2,1)S(1)} all-gather(bf16[1,16,3]{1,2,0:T(4,128)(2,1)S(1)} %convert_bitcast_fusion.2), channel_id=1, replica_groups=mesh['col'=4,'row'=8] {'col','row'}, dimensions={0}, use_global_device_ids=true | all-gather | bytes 3168 | tf_op jit(solution)/shard_map/all_gather | solution.py:283
  263.2 41.7 %all-gather.1 = bf16[2048,128]{1,0:T(8,128)(2,1)} all-gather(bf16[64,128]{1,0:T(8,128)(2,1)S(1)} %gather_fusion.3), channel_id=3, replica_groups=mesh['col'=4,'row'=8] {'col','row'}, dimensions={0}, use_global_device_ids=true | all-gather | bytes 540672 | tf_op jit(solution)/shard_map/all_gather | solution.py:265
  336.7 43.5 %all_gather.24 = bf16[512,512]{1,0:T(8,128)(2,1)} all-gather(bf16[16,512]{1,0:T(8,128)(2,1)S(1)} %convert_element_type.193), channel_id=1, replica_groups=mesh['col'=4,'row'=8] {'col','row'}, dimensions={0}, use_global_device_ids=true | all-gather | bytes 540672 | tf_op jit(solution)/shard_map/all_gather | solution.py:282
  407.3 233.0 %while.59 = (s32[]{:T(128)}, f32[8,1024,64]{1,2,0:T(8,128)S(1)}, bf16[8,1024,64]{2,1,0:T(8,128)(2,1)}, bf16[8,1024,64]{2,1,0:T(8,128)(2,1)}, f32[8,32]{1,0:T(8,1...) while((s32[]{:T(128)}, f32[8,1024,64]{1,2,0:T(8,128)S(1)}, ...), condition=%wide.region_15.16_spmd.clone, body=%wide.region_14.15_spmd.clone.sunk | while | flops 350224384 | bytes 1076833 | solution.py:103
  673.0 234.1 %while.58 = (s32[]{:T(128)}, f32[8,1024,64]{1,2,0:T(8,128)S(1)}, bf16[8,1024,64]{2,1,0:T(8,128)(2,1)}, bf16[8,1024,64]{2,1,0:T(8,128)(2,1)}, f32[8,32]{1,0:T(8,1...) while((s32[]{:T(128)}, f32[8,1024,64]{1,2,0:T(8,128)S(1)}, ...), condition=%wide.region_4.5_spmd.clone, body=%wide.region_3.4_spmd.clone.sunk | while | flops 350224384 | bytes 1076833 | solution.py:103
  941.1 363.0 %while.61 = (s32[]{:T(128)}, f32[8,1024,64]{1,2,0:T(8,128)}, f32[8,1024,64]{1,2,0:T(8,128)}, f32[8,1024,64]{1,2,0:T(8,128)}, f32[8,64,64]{2,0,1:T(8,128)S(1)}, /...) while((s32[]{:T(128)}, f32[8,1024,64]{1,2,0:T(8,128)}, ...), condition=%wide.region_33.34_spmd.clone.clone, body=%wide.region_32.33_spmd.clone.clone.sunk | while | flops 951517184 | bytes 40722088 | solution.py:198
  942.7 31.3 %select_add_fusion.7 = f32[1024,1024]{1,0:T(8,128)S(1)} fusion(s32[1024]{0:T(1024)S(1)} %get-tuple-element.1516, f32[]{:T(128)} %bitcast.2586, f32[]{:T(128)} %bitcast.2587, f32[]{:T(128)} %bitcast.2588, f32[]{:T(128)} %bitcast.2589, f32[]{:T(128)} %bitcast.2590, f32[]{:T(128)} %bitcast.2591, f32[]{:T(128)} %bitcast.2592, f32[]{:T(128)} %bitcast.2593, ...), kind=kOutput, calls=%fused_computation.455.clone.1 | convolution fusion | flops 206569472 | bytes 4744192 | tf_op jit(solution)/shard_map/while/body/eval_jaxpr/id,jd->ij/dot_general | solution.py:53
  988.1 31.3 %select_add_fusion.7 = f32[1024,1024]{1,0:T(8,128)S(1)} fusion(s32[1024]{0:T(1024)S(1)} %get-tuple-element.1516, f32[]{:T(128)} %bitcast.2586, f32[]{:T(128)} %bitcast.2587, f32[]{:T(128)} %bitcast.2588, f32[]{:T(128)} %bitcast.2589, f32[]{:T(128)} %bitcast.2590, f32[]{:T(128)} %bitcast.2591, f32[]{:T(128)} %bitcast.2592, f32[]{:T(128)} %bitcast.2593, ...), kind=kOutput, calls=%fused_computation.455.clone.1 | convolution fusion | flops 206569472 | bytes 4744192 | tf_op jit(solution)/shard_map/while/body/eval_jaxpr/id,jd->ij/dot_general | solution.py:53
  1033.4 31.3 %select_add_fusion.7 = f32[1024,1024]{1,0:T(8,128)S(1)} fusion(s32[1024]{0:T(1024)S(1)} %get-tuple-element.1516, f32[]{:T(128)} %bitcast.2586, f32[]{:T(128)} %bitcast.2587, f32[]{:T(128)} %bitcast.2588, f32[]{:T(128)} %bitcast.2589, f32[]{:T(128)} %bitcast.2590, f32[]{:T(128)} %bitcast.2591, f32[]{:T(128)} %bitcast.2592, f32[]{:T(128)} %bitcast.2593, ...), kind=kOutput, calls=%fused_computation.455.clone.1 | convolution fusion | flops 206569472 | bytes 4744192 | tf_op jit(solution)/shard_map/while/body/eval_jaxpr/id,jd->ij/dot_general | solution.py:53
  1078.8 31.3 %select_add_fusion.7 = f32[1024,1024]{1,0:T(8,128)S(1)} fusion(s32[1024]{0:T(1024)S(1)} %get-tuple-element.1516, f32[]{:T(128)} %bitcast.2586, f32[]{:T(128)} %bitcast.2587, f32[]{:T(128)} %bitcast.2588, f32[]{:T(128)} %bitcast.2589, f32[]{:T(128)} %bitcast.2590, f32[]{:T(128)} %bitcast.2591, f32[]{:T(128)} %bitcast.2592, f32[]{:T(128)} %bitcast.2593, ...), kind=kOutput, calls=%fused_computation.455.clone.1 | convolution fusion | flops 206569472 | bytes 4744192 | tf_op jit(solution)/shard_map/while/body/eval_jaxpr/id,jd->ij/dot_general | solution.py:53
  1124.1 31.3 %select_add_fusion.7 = f32[1024,1024]{1,0:T(8,128)S(1)} fusion(s32[1024]{0:T(1024)S(1)} %get-tuple-element.1516, f32[]{:T(128)} %bitcast.2586, f32[]{:T(128)} %bitcast.2587, f32[]{:T(128)} %bitcast.2588, f32[]{:T(128)} %bitcast.2589, f32[]{:T(128)} %bitcast.2590, f32[]{:T(128)} %bitcast.2591, f32[]{:T(128)} %bitcast.2592, f32[]{:T(128)} %bitcast.2593, ...), kind=kOutput, calls=%fused_computation.455.clone.1 | convolution fusion | flops 206569472 | bytes 4744192 | tf_op jit(solution)/shard_map/while/body/eval_jaxpr/id,jd->ij/dot_general | solution.py:53
  1169.5 31.3 %select_add_fusion.7 = f32[1024,1024]{1,0:T(8,128)S(1)} fusion(s32[1024]{0:T(1024)S(1)} %get-tuple-element.1516, f32[]{:T(128)} %bitcast.2586, f32[]{:T(128)} %bitcast.2587, f32[]{:T(128)} %bitcast.2588, f32[]{:T(128)} %bitcast.2589, f32[]{:T(128)} %bitcast.2590, f32[]{:T(128)} %bitcast.2591, f32[]{:T(128)} %bitcast.2592, f32[]{:T(128)} %bitcast.2593, ...), kind=kOutput, calls=%fused_computation.455.clone.1 | convolution fusion | flops 206569472 | bytes 4744192 | tf_op jit(solution)/shard_map/while/body/eval_jaxpr/id,jd->ij/dot_general | solution.py:53
  1214.8 31.3 %select_add_fusion.7 = f32[1024,1024]{1,0:T(8,128)S(1)} fusion(s32[1024]{0:T(1024)S(1)} %get-tuple-element.1516, f32[]{:T(128)} %bitcast.2586, f32[]{:T(128)} %bitcast.2587, f32[]{:T(128)} %bitcast.2588, f32[]{:T(128)} %bitcast.2589, f32[]{:T(128)} %bitcast.2590, f32[]{:T(128)} %bitcast.2591, f32[]{:T(128)} %bitcast.2592, f32[]{:T(128)} %bitcast.2593, ...), kind=kOutput, calls=%fused_computation.455.clone.1 | convolution fusion | flops 206569472 | bytes 4744192 | tf_op jit(solution)/shard_map/while/body/eval_jaxpr/id,jd->ij/dot_general | solution.py:53
  1260.2 31.3 %select_add_fusion.7 = f32[1024,1024]{1,0:T(8,128)S(1)} fusion(s32[1024]{0:T(1024)S(1)} %get-tuple-element.1516, f32[]{:T(128)} %bitcast.2586, f32[]{:T(128)} %bitcast.2587, f32[]{:T(128)} %bitcast.2588, f32[]{:T(128)} %bitcast.2589, f32[]{:T(128)} %bitcast.2590, f32[]{:T(128)} %bitcast.2591, f32[]{:T(128)} %bitcast.2592, f32[]{:T(128)} %bitcast.2593, ...), kind=kOutput, calls=%fused_computation.455.clone.1 | convolution fusion | flops 206569472 | bytes 4744192 | tf_op jit(solution)/shard_map/while/body/eval_jaxpr/id,jd->ij/dot_general | solution.py:53
  1312.8 371.3 %while.60 = (s32[]{:T(128)}, f32[8,1024,64]{1,2,0:T(8,128)}, f32[8,1024,64]{1,2,0:T(8,128)}, f32[8,1024,64]{1,2,0:T(8,128)}, f32[8,64,64]{2,0,1:T(8,128)S(1)}, /...) while((s32[]{:T(128)}, f32[8,1024,64]{1,2,0:T(8,128)}, ...), condition=%wide.region_27.28_spmd.clone.clone, body=%wide.region_26.27_spmd.clone.clone.sunk | while | flops 951517184 | bytes 40722088 | solution.py:198
  1314.6 31.3 %select_add_fusion.6 = f32[1024,1024]{1,0:T(8,128)S(1)} fusion(s32[1024]{0:T(1024)S(1)} %get-tuple-element.1474, f32[]{:T(128)} %bitcast.2512, f32[]{:T(128)} %bitcast.2513, f32[]{:T(128)} %bitcast.2514, f32[]{:T(128)} %bitcast.2515, f32[]{:T(128)} %bitcast.2516, f32[]{:T(128)} %bitcast.2517, f32[]{:T(128)} %bitcast.2518, f32[]{:T(128)} %bitcast.2519, ...), kind=kOutput, calls=%fused_computation.333.clone.1 | convolution fusion | flops 206569472 | bytes 4744192 | tf_op jit(solution)/shard_map/while/body/eval_jaxpr/id,jd->ij/dot_general | solution.py:53
  1639.1 31.3 %select_add_fusion.6 = f32[1024,1024]{1,0:T(8,128)S(1)} fusion(s32[1024]{0:T(1024)S(1)} %get-tuple-element.1474, f32[]{:T(128)} %bitcast.2512, f32[]{:T(128)} %bitcast.2513, f32[]{:T(128)} %bitcast.2514, f32[]{:T(128)} %bitcast.2515, f32[]{:T(128)} %bitcast.2516, f32[]{:T(128)} %bitcast.2517, f32[]{:T(128)} %bitcast.2518, f32[]{:T(128)} %bitcast.2519, ...), kind=kOutput, calls=%fused_computation.333.clone.1 | convolution fusion | flops 206569472 | bytes 4744192 | tf_op jit(solution)/shard_map/while/body/eval_jaxpr/id,jd->ij/dot_general | solution.py:53
  1818.4 47.7 %psum.29 = f32[]{:T(128)} all-reduce(f32[]{:T(128)S(6)} %add.454), channel_id=1, replica_groups=mesh['col'=4,'row'=8] {'col','row'}, use_global_device_ids=true, to_apply=%region_23.24 | all-reduce | flops 1 | bytes 8 | tf_op jit(solution)/shard_map/psum | solution.py:326
  1893.5 99.5 %reduce-scatter.11.cloned.1.call-done = f32[16,512]{1,0:T(8,128)} async-done(((f32[512,512]{1,0:T(8,128)}), f32[16,512]{1,0:T(8,128)}) %reduce-scatter.11.cloned.1.call-update) | async-done | bytes 32784 | tf_op jit(solution)/shard_map/reduce_scatter | solution.py:320
  2041.6 84.7 %reduce-scatter.7.cloned.1.call-done = f32[64,128]{1,0:T(8,128)} async-done(((f32[2048,128]{1,0:T(8,128)}), f32[64,128]{1,0:T(8,128)}) %reduce-scatter.7.cloned.1.call-update) | async-done | bytes 32784 | tf_op jit(solution)/shard_map/reduce_scatter | solution.py:332
  2129.7 137.4 %reduce-scatter.9.cloned.1.call-done = f32[16,2048]{1,0:T(8,128)} async-done(((f32[512,2048]{1,0:T(8,128)}), f32[16,2048]{1,0:T(8,128)}) %reduce-scatter.9.cloned.1.call-update) | async-done | bytes 131088 | tf_op jit(solution)/shard_map/reduce_scatter | solution.py:317
  2271.9 37.0 %all-reduce.4 = (f32[]{:T(128)}, f32[]{:T(128)}, f32[8,32]{1,0:T(8,128)S(1)}) all-reduce(f32[]{:T(128)S(6)} %add.453, f32[]{:T(128)S(6)} %add.471, f32[8,32]{1,0:T(8,128)S(1)} %fusion.531), channel_id=1, replica_groups=mesh['col'=4,'row'=8] {'col','row'}, use_global_device_ids=true, to_apply=%region_22.23 | all-reduce | flops 258 | bytes 2064 | tf_op jit(solution)/shard_map/psum | solution.py:326
  (720 shorter events, 1374.4 us)
Async XLA Ops:
  63.9 59.4 %all-to-all-start = ((s32[8,1,512]{2,1,0:T(1,128)}), s32[8,1,512]{2,1,0:T(1,128)S(1)}, u32[]{:S(2)}, u32[]{:S(2)}) async-start(s32[8,1,512]{2,1,0:T(1,128)} %bitcast.2), calls=%async_computation | async-start | bytes 32768 | tf_op jit(solution)/shard_map/all_to_all | solution.py:292
  123.3 10.8 all-to-all-start.3
  149.7 30.1 %all-to-all-start.4 = ((bf16[8,512,128]{2,1,0:T(8,128)(2,1)}), bf16[8,512,128]{2,1,0:T(8,128)(2,1)S(1)}, u32[]{:S(2)}, u32[]{:S(2)}) async-start(bf16[8,512,128]{2,1,0:T(8,128)(2,1)} %bitcast.36), calls=%async_computation.4 | async-start | bytes 2097152 | tf_op jit(solution)/shard_map/all_to_all | solution.py:294
  179.8 78.6 %all-to-all-start.1 = ((bf16[8,512,128]{2,1,0:T(8,128)(2,1)}), bf16[8,512,128]{2,1,0:T(8,128)(2,1)S(1)}, u32[]{:S(2)}, u32[]{:S(2)}) async-start(bf16[8,512,128]{2,1,0:T(8,128)(2,1)} %bitcast.2646), calls=%async_computation.1 | async-start | bytes 2097152 | tf_op jit(solution)/shard_map/all_to_all | solution.py:294
  183.4 205.0 %all-gather.6.cloned.1.call-start = ((), (), s32[]{:S(2)}) async-start(), calls=%async_computation.14 | async-start | bytes 2162688 | tf_op jit(solution)/shard_map/all_gather | solution.py:281
  258.4 60.0 %all-to-all-start.5 = ((bf16[4,1024,128]{1,2,0:T(8,128)(2,1)}), bf16[4,1024,128]{1,2,0:T(8,128)(2,1)S(1)}, u32[]{:S(2)}, u32[]{:S(2)}) async-start(bf16[4,1024,128]{1,2,0:T(8,128)(2,1)} %copy.191), calls=%async_computation.5 | async-start | bytes 2097152 | tf_op jit(solution)/shard_map/all_to_all | solution.py:296
  318.4 63.9 %all-to-all-start.2 = ((bf16[4,1024,128]{1,2,0:T(8,128)(2,1)}), bf16[4,1024,128]{1,2,0:T(8,128)(2,1)S(1)}, u32[]{:S(2)}, u32[]{:S(2)}) async-start(bf16[4,1024,128]{1,2,0:T(8,128)(2,1)} %copy.181), calls=%async_computation.2 | async-start | bytes 2097152 | tf_op jit(solution)/shard_map/all_to_all | solution.py:296
  321.9 1569.5 %reduce-scatter.13.cloned.1.call-start = ((), (), s32[]{:S(2)}) async-start(), calls=%async_computation.18 | async-start | bytes 270336
  941.0 363.7 %copy-start.7 = (f32[1024,512]{1,0:T(8,128)S(1)}, f32[1024,512]{1,0:T(8,128)}, u32[]{:S(2)}) copy-start(f32[1024,512]{1,0:T(8,128)} %copy-done.6) | copy-start | bytes 6291460
  941.0 363.7 %copy-start.67 = (f32[1024]{0:T(1024)S(1)}, f32[1024]{0:T(1024)}, u32[]{:S(2)}) copy-start(f32[1024]{0:T(1024)} %copy-done.66) | copy-start | bytes 12292
  1726.8 266.2 %reduce-scatter.11.cloned.1.call-start = ((), (), s32[]{:S(2)}) async-start(), calls=%async_computation.17 | async-start | bytes 1081344 | tf_op jit(solution)/shard_map/reduce_scatter | solution.py:320
  1730.5 395.8 %reduce-scatter.7.cloned.1.call-start = ((), (), s32[]{:S(2)}) async-start(), calls=%async_computation.15 | async-start | bytes 1081344 | tf_op jit(solution)/shard_map/reduce_scatter | solution.py:332
  1739.0 528.2 %reduce-scatter.9.cloned.1.call-start = ((), (), s32[]{:S(2)}) async-start(), calls=%async_computation.16 | async-start | bytes 4325376 | tf_op jit(solution)/shard_map/reduce_scatter | solution.py:317
  1771.0 18.8 all-to-all-start.6
  1789.8 24.4 %all-to-all-start.8 = ((bf16[4,2,65536]{2,1,0:T(2,128)(2,1)}), bf16[4,2,65536]{2,1,0:T(2,128)(2,1)S(1)}, u32[]{:S(2)}, u32[]{:S(2)}) async-start(bf16[4,2,65536]{2,1,0:T(2,128)(2,1)} %reshape.1765), calls=%async_computation.8 | async-start | bytes 2097152 | tf_op jit(solution)/shard_map/all_to_all | solution.py:304
  1814.2 69.7 %all-to-all-start.7 = ((bf16[8,512,128]{2,1,0:T(8,128)(2,1)}), bf16[8,512,128]{2,1,0:T(8,128)(2,1)}, u32[]{:S(2)}, u32[]{:S(2)}) async-start(bf16[8,512,128]{2,1,0:T(8,128)(2,1)} %bitcast.71), calls=%async_computation.7 | async-start | bytes 2097152 | tf_op jit(solution)/shard_map/all_to_all | solution.py:308
  1883.8 134.4 %all-to-all-start.9 = ((bf16[8,512,128]{2,1,0:T(8,128)(2,1)}), bf16[8,512,128]{2,1,0:T(8,128)(2,1)}, u32[]{:S(2)}, u32[]{:S(2)}) async-start(bf16[8,512,128]{2,1,0:T(8,128)(2,1)} %bitcast.90), calls=%async_computation.9 | async-start | bytes 2097152 | tf_op jit(solution)/shard_map/all_to_all | solution.py:308
  1890.1 424.0 %copy-start.37 = (f32[3200,128]{1,0:T(8,128)S(1)}, f32[3200,128]{1,0:T(8,128)}, u32[]{:S(2)}) copy-start(f32[3200,128]{1,0:T(8,128)} %param.31) | copy-start | bytes 4915204
  1890.7 420.8 %copy-start.113 = (f32[8,32]{1,0:T(8,128)S(1)}, f32[8,32]{1,0:T(8,128)}, u32[]{:S(2)}) copy-start(f32[8,32]{1,0:T(8,128)} %copy-done.112) | copy-start | bytes 3076
  1890.7 420.8 %copy-start.114 = (f32[8,32]{1,0:T(8,128)S(1)}, f32[8,32]{1,0:T(8,128)}, u32[]{:S(2)}) copy-start(f32[8,32]{1,0:T(8,128)} %param.44) | copy-start | bytes 3076
  1890.7 420.8 %copy-start.115 = (f32[8,32]{1,0:T(8,128)S(1)}, f32[8,32]{1,0:T(8,128)}, u32[]{:S(2)}) copy-start(f32[8,32]{1,0:T(8,128)} %param.45) | copy-start | bytes 3076
  1890.7 422.1 %copy-start.103 = (f32[3,16]{1,0:T(4,128)S(1)}, f32[3,16]{1,0:T(4,128)}, u32[]{:S(2)}) copy-start(f32[3,16]{1,0:T(4,128)} %param.40) | copy-start | bytes 580
  1890.8 422.1 %copy-start.116 = (f32[3,16]{1,0:T(4,128)S(1)}, f32[3,16]{1,0:T(4,128)}, u32[]{:S(2)}) copy-start(f32[3,16]{1,0:T(4,128)} %param.41) | copy-start | bytes 580
  1890.8 422.1 %copy-start.117 = (f32[3,16]{1,0:T(4,128)S(1)}, f32[3,16]{1,0:T(4,128)}, u32[]{:S(2)}) copy-start(f32[3,16]{1,0:T(4,128)} %param.42) | copy-start | bytes 580
  (133 other events, 2206.1 us)
Sparse Core Ops, SparseCore 0:
  187.8 60.8 all-gather.5
  1726.9 131.2 reduce-scatter.12
  1860.6 132.4 reduce-scatter.10
  1995.1 131.1 reduce-scatter.6
  2128.5 138.5 reduce-scatter.8
where the time goes:
time: 2350 us; the launch traced here: 2330 us
  matrix products  1220 us (52%)
  waiting for transfers between devices  343 us (15%)
  local copies, waits for them, and re-layouts  303 us (13%)
  blocking collectives  232 us (10%)
  other arithmetic  157 us (7%)
  starting transfers between devices  51.6 us (2%)
    dot_general x16, matrix products, head_scores(): jnp.einsum('id,jd->ij', head_query, head_keys, preferred_element_type=jnp...  501 us
    dot_general x16, matrix products, head_forward(): return jnp.dot(attend, head_value, preferred_element_type=jnp.float32)  443 us
    reduce_scatter x1, waiting for transfers between devices, local(): lax.psum_scatter(grad_big, ('col', 'row'), scatter_dimension=0, tiled=True)  137 us
    reduce_scatter x1, waiting for transfers between devices, local(): lax.psum_scatter(grad_small, ('col', 'row'), scatter_dimension=0, tiled=T...  99.5 us
    reduce_scatter x1, waiting for transfers between devices, local(): lax.psum_scatter(neg_layout, ('col', 'row'), scatter_dimension=0, tiled=T...  84.7 us
    psum x2, blocking collectives, local(): lax.psum((rab_grad, loss_total, count_total), ('col', 'row'))  84.7 us
    gather x2, local copies, waits for them, and re-layouts, local(): requests = group_ids[owner_order].reshape(row_count, -1)  81.1 us
    dot_general x16, matrix products, head_backward(): jnp.einsum('ij,id->jd', attend, grad_out, preferred_element_type=jnp.floa...  60.9 us
  transfers between devices with their start and end apart: 15, of which 6 were waited for; matrix products, arithmetic and copies ran while one was open for 11% of the time, Pallas kernels for 0%

commit v1 on v0

v1 whole, which is shorter than its diff:
```python
import jax
import jax.numpy as jnp
from jax import lax
from jax.experimental import pallas as pl
from jax.experimental.pallas import tpu as pltpu
from jax.sharding import PartitionSpec as P

NB = 32
STEP = 10
BETA_ONE = 0.9
BETA_TWO = 0.999
EPS_ADAM = 1e-08
EPS_NORM = 1e-06
WEIGHT_DECAY = 0.01
CLIP_NORM = 0.05
RATE_TABLE = 0.06
RATE_DENSE = 0.01
RATE_SMALL = 0.5
BOTH = ("col", "row")
TILE = 256
BF = jnp.bfloat16
F32 = jnp.float32


def dot_nn(left, right):
    return lax.dot_general(left, right, (((1,), (0,)), ((), ())), preferred_element_type=F32)


def dot_nt(left, right):
    return lax.dot_general(left, right, (((1,), (1,)), ((), ())), preferred_element_type=F32)


def dot_tn(left, right):
    return lax.dot_general(left, right, (((0,), (0,)), ((), ())), preferred_element_type=F32)


def row_scale(values):
    return lax.rsqrt(jnp.mean(values * values, axis=-1, keepdims=True) + EPS_NORM)


def row_back(values, scale, grad):
    cubed = scale * scale * scale
    return scale * grad - values * (cubed * jnp.mean(grad * values, axis=-1, keepdims=True))


def silu_slope(values):
    half = 0.5 * jnp.tanh(0.5 * values)
    sigmoid = 0.5 + half
    active = values * sigmoid
    return active, sigmoid + active * (0.5 - half)


def history_kernel(
    len_ref,
    recv_ref,
    order_ref,
    bucket_ref,
    dense_ref,
    negs_ref,
    gains_ref,
    bias_ref,
    ge_ref,
    big_ref,
    small_ref,
    gneg_ref,
    misc_ref,
    rab_ref,
    rows_s,
    event_s,
    normed_s,
    gatein_s,
    slope_s,
    value_s,
    valuem_s,
    query_s,
    keys_s,
    keyst_s,
    hot_s,
    hott_s,
    orderc_s,
    out_s,
    gout_s,
    ggate_s,
    gevent_s,
    dvalue_s,
    dkeys_s,
    dqueryt_s,
    gslots_s,
    carry_s,
    pairs_s,
):
    pieces, seq, piece = recv_ref.shape
    width = event_s.shape[1]
    groups = width // 128
    heads = 2 * groups
    length = len_ref[0]
    tiles = lax.div(length + (TILE - 1), TILE)
    gain_in = gains_ref[0:1, :]
    gain_mid = gains_ref[1:2, :]
    gain_out = gains_ref[2:3, :]
    lane = lax.broadcasted_iota(jnp.int32, (TILE, 128), 1)
    low_lanes = lane < 64

    def place(step):
        return pl.ds(pl.multiple_of(step * TILE, TILE), TILE)

    for one in range(pieces):
        rows_s[:, one * piece : (one + 1) * piece] = recv_ref[one]
    lane_square = lax.broadcasted_iota(jnp.int32, (128, 128), 1)
    for part in range(seq // 128):
        span = slice(part * 128, (part + 1) * 128)
        spread = jnp.broadcast_to(order_ref[0:1, span].astype(F32), (128, 128))
        orderc_s[span, :] = spread.T.astype(jnp.int32)
        spread = jnp.broadcast_to(bucket_ref[0:1, span].astype(F32), (128, 128))
        column = spread.T.astype(jnp.int32)
        hot_s[span, :] = jnp.where(
            column == jnp.bitwise_and(lane_square, 63), 1.0, 0.0
        ).astype(BF)
        hott_s[:, span] = jnp.where(
            bucket_ref[0:1, span] == 63 - lax.broadcasted_iota(jnp.int32, (64, 128), 0), 1.0, 0.0
        ).astype(BF)
    big_ref[...] = jnp.zeros_like(big_ref)
    small_ref[...] = jnp.zeros_like(small_ref)
    gneg_ref[...] = jnp.zeros_like(gneg_ref)
    misc_ref[...] = jnp.zeros_like(misc_ref)
    gslots_s[...] = jnp.zeros_like(gslots_s)
    carry_s[...] = jnp.zeros_like(carry_s)
    pairs_s[...] = jnp.zeros_like(pairs_s)

    def project(step, _):
        span = place(step)
        hot = jnp.where(
            order_ref[0:1, :] == lax.broadcasted_iota(jnp.int32, (TILE, seq), 0) + step * TILE,
            1.0,
            0.0,
        ).astype(BF)
        event = dot_nn(hot, rows_s[...])
        event_s[span, :] = event.astype(BF)
        normed = (event * row_scale(event) * gain_in).astype(BF)
        normed_s[span, :] = normed
        gatein_s[span, :] = dot_nn(normed, dense_ref[:, 0:width])
        bucket = hot_s[span, :]
        active, slope = silu_slope(dot_nn(normed, dense_ref[:, width : 2 * width]))
        slope_s[0, span, :] = slope.astype(BF)
        scaled = active.astype(BF) * BF(1.0 / seq)
        for group in range(groups):
            part = scaled[:, group * 128 : (group + 1) * 128]
            value_s[group, span, :] = part
            valuem_s[2 * group, span, :] = jnp.where(low_lanes, part, BF(0))
            valuem_s[2 * group + 1, span, :] = jnp.where(low_lanes, BF(0), part)
        active, slope = silu_slope(dot_nn(normed, dense_ref[:, 2 * width : 3 * width]))
        slope_s[1, span, :] = slope.astype(BF)
        scaled = active.astype(BF) * BF(0.25)
        bias = dot_nn(bucket, bias_ref[...]).astype(BF)
        for group in range(groups):
            part = scaled[:, group * 128 : (group + 1) * 128]
            query_s[2 * group, span, 0:128] = jnp.where(low_lanes, part, BF(0))
            query_s[2 * group + 1, span, 0:128] = jnp.where(low_lanes, BF(0), part)
            query_s[2 * group, span, 128:256] = bias[:, group * 256 : group * 256 + 128]
            query_s[2 * group + 1, span, 128:256] = bias[:, group * 256 + 128 : group * 256 + 256]
        active, slope = silu_slope(dot_nn(normed, dense_ref[:, 3 * width : 4 * width]))
        slope_s[2, span, :] = slope.astype(BF)
        scaled = active.astype(BF)
        for group in range(groups):
            part = scaled[:, group * 128 : (group + 1) * 128]
            keys_s[group, span, 0:128] = part
            keys_s[group, span, 128:256] = bucket
            turned = part.T
            keyst_s[2 * group, :, span] = turned[0:64, :]
            keyst_s[2 * group + 1, :, span] = turned[64:128, :]
        for group in range(groups):
            dvalue_s[group, span, :] = jnp.zeros((TILE, 128), F32)
        for head in range(heads):
            dkeys_s[head, span, :] = jnp.zeros((TILE, 256), F32)
            dqueryt_s[head, :, span] = jnp.zeros((64, TILE), F32)
        return 0

    lax.fori_loop(0, tiles, project, 0)

    square_row = lax.broadcasted_iota(jnp.int32, (TILE, TILE), 0)
    square_col = lax.broadcasted_iota(jnp.int32, (TILE, TILE), 1)

    def attend_group(group, _):
        def attend_tile(step, _):
            span = place(step)

            def attend(other, masked):
                near = place(other)
                total = None
                for half in range(2):
                    scores = dot_nt(query_s[2 * group + half, span, :], keys_s[group, near, :])
                    weight = scores + scores * jnp.tanh(scores)
                    if masked:
                        weight = jnp.where(square_col <= square_row, weight, 0.0)
                    part = dot_nn(weight.astype(BF), valuem_s[2 * group + half, near, :])
                    total = part if total is None else total + part
                return total

            out_s[group, span, :] = attend(step, True)

            def before(other, _):
                out_s[group, span, :] += attend(other, False)
                return 0

            lax.fori_loop(0, step, before, 0)
            return 0

        lax.fori_loop(0, tiles, attend_tile, 0)
        return 0

    lax.fori_loop(0, groups, attend_group, 0)

    def middle(step, _):
        span = place(step)
        event = event_s[span, :].astype(F32)
        merged = jnp.concatenate([out_s[group, span, :] for group in range(groups)], axis=1)
        scale_mid = row_scale(merged)
        normed_mid = merged * scale_mid
        gate, gate_slope = silu_slope(gatein_s[span, :])
        mixed = (normed_mid * gain_mid * gate).astype(BF)
        hidden = event + dot_nn(mixed, dense_ref[:, 4 * width : 5 * width])
        scale_out = row_scale(hidden)
        final = (hidden * scale_out * gain_out).astype(BF)
        final_f = final.astype(F32)
        following = event_s[pl.ds(pl.multiple_of((step + 1) * TILE, TILE), 16), :][0:1, :].astype(F32)
        following = jnp.where(step + 1 < tiles, following, 0.0)
        row_id = lax.broadcasted_iota(jnp.int32, (TILE, width), 0)
        target = jnp.where(
            row_id == TILE - 1, following, pltpu.roll(event, TILE - 1, 0)
        )
        positive = jnp.sum(final_f * target, axis=-1, keepdims=True)
        negative = dot_nt(final, negs_ref[...])
        highest = jnp.maximum(jnp.max(negative, axis=-1, keepdims=True), positive)
        neg_exp = jnp.exp(negative - highest)
        pos_exp = jnp.exp(positive - highest)
        totals = pos_exp + jnp.sum(neg_exp, axis=-1, keepdims=True)
        counted = (
            lax.broadcasted_iota(jnp.int32, (TILE, 1), 0) + step * TILE < length - 1
        )
        losses = jnp.where(counted, highest + jnp.log(totals) - positive, 0.0)
        misc_ref[3:4, :] += jnp.broadcast_to(jnp.sum(losses, axis=0, keepdims=True), (1, width))
        share = jnp.where(counted, 1.0 / totals, 0.0)
        grad_neg = (neg_exp * share).astype(BF)
        grad_pos = jnp.where(counted, pos_exp * share - 1.0, 0.0)
        grad_final = dot_nn(grad_neg, negs_ref[...]) + grad_pos * target
        gneg_ref[...] += dot_tn(grad_neg, final)
        pushed = grad_pos * final_f
        grad_event = jnp.where(row_id == 0, carry_s[0:1, :], pltpu.roll(pushed, 1, 0))
        carry_s[0:1, :] = pushed[TILE - 1 : TILE, :]
        misc_ref[2:3, :] += jnp.sum(grad_final * hidden * scale_out, axis=0, keepdims=True)
        grad_hidden = row_back(hidden, scale_out, grad_final * gain_out)
        gevent_s[span, :] = grad_event + grad_hidden
        branch = grad_hidden.astype(BF)
        small_ref[...] += dot_tn(mixed, branch)
        grad_mixed = dot_nt(branch, dense_ref[:, 4 * width : 5 * width])
        gated = grad_mixed * gate
        misc_ref[1:2, :] += jnp.sum(gated * normed_mid, axis=0, keepdims=True)
        ggate_s[span, :] = (grad_mixed * normed_mid * gain_mid * gate_slope).astype(BF)
        grad_out = row_back(merged, scale_mid, gated * gain_mid).astype(BF) * BF(0.5)
        for group in range(groups):
            part = grad_out[:, group * 128 : (group + 1) * 128]
            gout_s[2 * group, span, :] = jnp.where(low_lanes, part, BF(0))
            gout_s[2 * group + 1, span, :] = jnp.where(low_lanes, BF(0), part)
        return 0

    lax.fori_loop(0, tiles, middle, 0)

    def retreat_group(group, _):
        def retreat_tile(step, _):
            near = place(step)

            def retreat(other, masked):
                span = place(other)
                keys = keys_s[group, near, :]
                value = value_s[group, near, :]
                total = None
                for half in range(2):
                    head = 2 * group + half
                    gout = gout_s[head, span, :]
                    query = query_s[head, span, :]
                    scores = dot_nt(keys, query)
                    grads = dot_nt(value, gout)
                    bent = 1.0 + jnp.tanh(scores)
                    weight = scores * bent
                    slope = bent * ((1.0 + (scores + scores)) - weight)
                    grads = grads * slope
                    if masked:
                        visible = square_row <= square_col
                        weight = jnp.where(visible, weight, 0.0)
                        grads = jnp.where(visible, grads, 0.0)
                    grads = grads.astype(BF)
                    part = dot_nn(weight.astype(BF), gout)
                    total = part if total is None else total + part
                    dkeys_s[head, near, :] += dot_nn(
                        grads, jnp.concatenate([query[:, 0:128], hot_s[span, :]], axis=1)
                    )
                    dqueryt_s[head, :, span] += dot_nn(keyst_s[head, :, near], grads)
                dvalue_s[group, near, :] += total

            retreat(step, True)

            def after(other, _):
                retreat(other, False)
                return 0

            lax.fori_loop(step + 1, tiles, after, 0)
            return 0

        lax.fori_loop(0, tiles, retreat_tile, 0)
        return 0

    lax.fori_loop(0, groups, retreat_group, 0)

    def finish(step, _):
        span = place(step)
        normed = normed_s[span, :]
        parts = [ggate_s[span, :]]
        grad = jnp.concatenate([dvalue_s[group, span, :] for group in range(groups)], axis=1)
        parts.append((grad * (2.0 / seq) * slope_s[0, span, :].astype(F32)).astype(BF))
        grad = jnp.concatenate(
            [
                jnp.concatenate([dqueryt_s[2 * group, :, span], dqueryt_s[2 * group + 1, :, span]], axis=0).T
                for group in range(groups)
            ],
            axis=1,
        )
        parts.append((grad * 0.5 * slope_s[1, span, :].astype(F32)).astype(BF))
        grad = jnp.concatenate(
            [
                dkeys_s[2 * group, span, 0:128] + dkeys_s[2 * group + 1, span, 0:128]
                for group in range(groups)
            ],
            axis=1,
        )
        parts.append((grad * 2.0 * slope_s[2, span, :].astype(F32)).astype(BF))
        grad_normed = None
        for index in range(4):
            columns = slice(index * width, (index + 1) * width)
            big_ref[:, columns] += dot_tn(normed, parts[index])
            part = dot_nt(parts[index], dense_ref[:, columns])
            grad_normed = part if grad_normed is None else grad_normed + part
        hott = hott_s[:, span]
        for head in range(heads):
            wide = dkeys_s[head, span, 128:256]
            upper = wide.astype(BF)
            lower = (wide - upper.astype(F32)).astype(BF)
            pairs_s[head] += dot_nn(hott, upper) + dot_nn(hott, lower)
        event = event_s[span, :].astype(F32)
        scale = row_scale(event)
        misc_ref[0:1, :] += jnp.sum(grad_normed * event * scale, axis=0, keepdims=True)
        total = gevent_s[span, :] + row_back(event, scale, grad_normed * gain_in)
        column = orderc_s[...]
        hot = jnp.where(
            jnp.concatenate([column] * (TILE // 128), axis=1)
            == lax.broadcasted_iota(jnp.int32, (seq, TILE), 1) + step * TILE,
            1.0,
            0.0,
        ).astype(BF)
        gslots_s[...] += dot_nn(hot, total.astype(BF))
        return 0

    lax.fori_loop(0, tiles, finish, 0)

    for one in range(pieces):
        ge_ref[one] = gslots_s[:, one * piece : (one + 1) * piece].astype(BF)
    lane_row = lax.broadcasted_iota(jnp.int32, (64, 128), 1)
    for head in range(heads):
        kept = jnp.where(lane_row < 64, pairs_s[head], 0.0)
        turned = pltpu.roll(kept, 0, 1, stride=1, stride_axis=0)
        rab_ref[head : head + 1, :] = jnp.sum(turned, axis=0, keepdims=True)


def history_call(length, recv, order, bucket, dense, negs, gains, bias):
    pieces, seq, piece = recv.shape
    width = pieces * piece
    heads = width // 64
    groups = heads // 2
    vmem = pl.BlockSpec(memory_space=pltpu.VMEM)
    return pl.pallas_call(
        history_kernel,
        out_shape=(
            jax.ShapeDtypeStruct(recv.shape, BF),
            jax.ShapeDtypeStruct((width, 4 * width), F32),
            jax.ShapeDtypeStruct((width, width), F32),
            jax.ShapeDtypeStruct(negs.shape, F32),
            jax.ShapeDtypeStruct((8, width), F32),
            jax.ShapeDtypeStruct((heads, 128), F32),
        ),
        in_specs=[pl.BlockSpec(memory_space=pltpu.SMEM)] + [vmem] * 7,
        out_specs=(vmem,) * 6,
        scratch_shapes=[
            pltpu.VMEM((seq, width), BF),
            pltpu.VMEM((seq + TILE, width), BF),
            pltpu.VMEM((seq, width), BF),
            pltpu.VMEM((seq, width), F32),
            pltpu.VMEM((3, seq, width), BF),
            pltpu.VMEM((groups, seq, 128), BF),
            pltpu.VMEM((heads, seq, 128), BF),
            pltpu.VMEM((heads, seq, 256), BF),
            pltpu.VMEM((groups, seq, 256), BF),
            pltpu.VMEM((heads, 64, seq), BF),
            pltpu.VMEM((seq, 128), BF),
            pltpu.VMEM((64, seq), BF),
            pltpu.VMEM((seq, 128), jnp.int32),
            pltpu.VMEM((groups, seq, 128), F32),
            pltpu.VMEM((heads, seq, 128), BF),
            pltpu.VMEM((seq, width), BF),
            pltpu.VMEM((seq, width), F32),
            pltpu.VMEM((groups, seq, 128), F32),
            pltpu.VMEM((heads, seq, 256), F32),
            pltpu.VMEM((heads, 64, seq), F32),
            pltpu.VMEM((seq, width), F32),
            pltpu.VMEM((8, width), F32),
            pltpu.VMEM((heads, 64, 128), F32),
        ],
        compiler_params=pltpu.CompilerParams(vmem_limit_bytes=60 * 1024 * 1024),
        name="history",
    )(length, recv, order, bucket, dense, negs, gains, bias)


def lookup_kernel(hist_ref, ids_ref, table_ref, found_ref, stage_s):
    count = hist_ref.shape[0]
    per = stage_s.shape[0]

    def one(place, _):
        base = hist_ref[place] * per
        for index in range(per):
            stage_s[index : index + 1, :] = table_ref[pl.ds(ids_ref[base + index], 1), :]
        found_ref[pl.ds(pl.multiple_of(place * per, per), per), :] = stage_s[...].astype(BF)
        return 0

    lax.fori_loop(0, count, one, 0)


def lookup_call(hist, ids, table, per):
    count = hist.shape[0]
    smem = pl.BlockSpec(memory_space=pltpu.SMEM)
    vmem = pl.BlockSpec(memory_space=pltpu.VMEM)
    return pl.pallas_call(
        lookup_kernel,
        out_shape=jax.ShapeDtypeStruct((count * per, table.shape[1]), BF),
        in_specs=[smem, smem, vmem],
        out_specs=vmem,
        scratch_shapes=[pltpu.VMEM((per, table.shape[1]), F32)],
        compiler_params=pltpu.CompilerParams(vmem_limit_bytes=16 * 1024 * 1024),
        name="lookup",
    )(hist, ids, table)


def scatter_kernel(hist_ref, ids_ref, grads_ref, init_ref, total_ref, stage_s, *sums):
    count = hist_ref.shape[0]
    per = stage_s.shape[0]
    for one in sums:
        one[...] = jnp.zeros_like(one)

    def one(place, _):
        base = hist_ref[place] * per
        stage_s[...] = grads_ref[pl.ds(pl.multiple_of(place * per, per), per), :].astype(F32)
        for index in range(per):
            held = sums[index % len(sums)]
            spot = pl.ds(ids_ref[base + index], 1)
            held[spot, :] = held[spot, :] + stage_s[index : index + 1, :]
        return 0

    lax.fori_loop(0, count, one, 0)
    total = init_ref[...]
    for one in sums:
        total = total + one[...]
    total_ref[...] = total


def scatter_call(hist, ids, grads, init, per):
    smem = pl.BlockSpec(memory_space=pltpu.SMEM)
    vmem = pl.BlockSpec(memory_space=pltpu.VMEM)
    return pl.pallas_call(
        scatter_kernel,
        out_shape=jax.ShapeDtypeStruct(init.shape, F32),
        in_specs=[smem, smem, vmem, vmem],
        out_specs=vmem,
        scratch_shapes=[pltpu.VMEM((per, init.shape[1]), F32)] + [pltpu.VMEM(init.shape, F32)] * 4,
        compiler_params=pltpu.CompilerParams(vmem_limit_bytes=32 * 1024 * 1024),
        name="scatter",
    )(hist, ids, grads, init)


def negs_kernel(spots_ref, share_ref, grads_ref, total_ref, square_ref):
    total_ref[...] = grads_ref[...]
    for index in range(spots_ref.shape[0]):
        spot = pl.ds(spots_ref[index], 1)
        total_ref[spot, :] = total_ref[spot, :] + share_ref[index : index + 1, :]
    total = total_ref[...]
    square_ref[...] = jnp.sum(total * total, axis=0, keepdims=True)


def negs_call(spots, share, grads):
    smem = pl.BlockSpec(memory_space=pltpu.SMEM)
    vmem = pl.BlockSpec(memory_space=pltpu.VMEM)
    return pl.pallas_call(
        negs_kernel,
        out_shape=(
            jax.ShapeDtypeStruct(grads.shape, F32),
            jax.ShapeDtypeStruct((1, grads.shape[1]), F32),
        ),
        in_specs=[smem, vmem, vmem],
        out_specs=(vmem, vmem),
        compiler_params=pltpu.CompilerParams(vmem_limit_bytes=32 * 1024 * 1024),
        name="negatives",
    )(spots, share, grads)


def bias_table(rab):
    place = jnp.arange(64)
    both = 0.5 * rab[:, jnp.clip(place[:, None] - place[None, :], 0, NB - 1)]
    upper = lax.reduce_precision(both, 8, 7)
    parts = jnp.concatenate([upper, both - upper], axis=2).astype(BF)
    parts = parts.transpose(1, 0, 2).reshape(64, -1)
    return jnp.concatenate([parts, jnp.zeros_like(parts)], axis=0)


def fold_bias(spread):
    return jnp.concatenate(
        [
            jnp.sum(spread[:, :64], axis=1, keepdims=True),
            spread[:, 64 : 62 + NB],
            jnp.sum(spread[:, 62 + NB :], axis=1, keepdims=True),
        ],
        axis=1,
    )


def adamw_update(weight, first, second, grad, rate):
    first = BETA_ONE * first + (1.0 - BETA_ONE) * grad
    second = BETA_TWO * second + (1.0 - BETA_TWO) * grad * grad
    fixed_first = first / (1.0 - BETA_ONE**STEP)
    fixed_second = second / (1.0 - BETA_TWO**STEP)
    weight = weight - rate * (
        fixed_first / (jnp.sqrt(fixed_second) + EPS_ADAM) + WEIGHT_DECAY * weight
    )
    return (weight, first, second)


def exchange(values, axes, groups=None):
    return lax.all_to_all(
        values, axes, split_axis=0, concat_axis=0, tiled=True, axis_index_groups=groups
    )


def spread_sum(values, devices):
    copies = jnp.broadcast_to(values[None], (devices,) + values.shape)
    return jnp.sum(exchange(copies, BOTH), axis=0)


def fold_dense(grads, col_count, row_count):
    rows, columns = grads.shape
    half = row_count // 2
    pairs = [[2 * index, 2 * index + 1] for index in range(half)]
    alike = [list(range(first, row_count, 2)) for first in range(2)]
    own = rows // (col_count * row_count)
    low = grads.astype(BF).reshape(col_count * half, 2, own, columns).transpose(1, 0, 2, 3)
    got = exchange(low.reshape(2, rows // 2, columns), "row", pairs)
    low = jnp.sum(got.astype(F32), axis=0).astype(BF)
    got = exchange(low.reshape(col_count, half * own, columns), "col")
    low = jnp.sum(got.astype(F32), axis=0).astype(BF)
    got = exchange(low.reshape(half, own, columns), "row", alike)
    return jnp.sum(got.astype(F32), axis=0)


def local(
    lengths,
    items,
    negatives,
    time_buckets,
    table,
    table_m,
    table_v,
    w_in,
    w_in_m,
    w_in_v,
    w_out,
    w_out_m,
    w_out_v,
    gains,
    gains_m,
    gains_v,
    rab,
    rab_m,
    rab_v,
):
    col_count = lax.axis_size("col")
    row_count = lax.axis_size("row")
    devices = col_count * row_count
    row_place = lax.axis_index("row")
    me = lax.axis_index("col") * row_count + row_place
    rows_dev, piece = table.shape
    own, width = w_out.shape
    slots, _, seq = items.shape
    per = seq // row_count
    neg_total = negatives.shape[0]
    neg_own = neg_total // row_count
    own_negs = (
        lax.dynamic_slice_in_dim(negatives, row_place * neg_own, neg_own) - row_place * rows_dev
    )
    dense = lax.all_gather(
        jnp.concatenate(
            [
                w_in.astype(BF),
                w_out.astype(BF),
                table[own_negs].astype(BF).reshape(own, -1),
                jnp.pad(gains.T, ((0, 0), (0, 128 - gains.shape[0]))).astype(BF),
            ],
            axis=1,
        ),
        BOTH,
        axis=0,
        tiled=True,
    )
    neg_rows = (
        dense[:, 5 * width : 6 * width]
        .reshape(col_count, row_count, neg_own, piece)
        .transpose(1, 2, 0, 3)
        .reshape(neg_total, width)
    )
    gain_all = dense[:, 6 * width : 6 * width + gains.shape[0]].T.astype(F32)
    bias = bias_table(rab)
    mine = items[:, 0]
    key, sorted_items = lax.sort(
        (mine // rows_dev * seq + jnp.arange(seq)[None, :], mine), dimension=1, num_keys=1
    )
    block = key // seq
    order = key - block * seq
    numbers = (sorted_items - block * rows_dev).reshape(slots, row_count, per).transpose(1, 0, 2)
    told = jnp.concatenate(
        [
            numbers.reshape(row_count, slots * per),
            jnp.broadcast_to(jnp.pad(lengths[:, 0], (0, 128 - slots))[None], (row_count, 128)),
        ],
        axis=1,
    )
    told = jnp.broadcast_to(told[None], (col_count,) + told.shape).reshape(devices, -1)
    heard = exchange(told, BOTH)
    ids = heard[:, : slots * per].reshape(-1)
    every_length = heard[:, slots * per : slots * per + slots].reshape(-1)
    total = devices * slots
    number = jnp.arange(total)
    ahead = (every_length[None, :] > every_length[:, None]) | (
        (every_length[None, :] == every_length[:, None]) & (number[None, :] < number[:, None])
    )
    rank = jnp.sum(ahead.astype(jnp.int32), axis=1)
    wanted = jnp.stack(
        [
            slot * devices + (jnp.arange(devices) if slot % 2 == 0 else devices - 1 - jnp.arange(devices))
            for slot in range(slots)
        ]
    )
    hist = jnp.sum(
        jnp.where(rank[None, None, :] == wanted[:, :, None], number[None, None, :], 0), axis=2
    )
    my_hist = lax.dynamic_slice_in_dim(hist, me, 1, axis=1)[:, 0]
    about = jnp.stack([order, time_buckets[:, 0]], axis=1)
    about = lax.all_gather(about, "row", axis=0, tiled=True)
    about = lax.all_gather(about, "col", axis=0, tiled=True)
    sent = []
    for slot in range(slots):
        found = lookup_call(hist[slot], ids, table, per)
        sent.append(exchange(found.reshape(devices, per, piece), BOTH))
    back = []
    dense_grads = None
    for slot in range(slots):
        own_about = lax.dynamic_slice_in_dim(about, my_hist[slot], 1, axis=0)[0]
        results = history_call(
            lax.dynamic_slice_in_dim(every_length, my_hist[slot], 1),
            sent[slot].reshape(col_count, seq, piece),
            own_about[0:1],
            own_about[1:2],
            dense,
            neg_rows,
            gain_all,
            bias,
        )
        back.append(exchange(results[0].reshape(devices, per, piece), BOTH))
        grads = results[1:]
        if dense_grads is None:
            dense_grads = grads
        else:
            dense_grads = tuple(first + second for first, second in zip(dense_grads, grads))
    grad_big, grad_small, grad_negs, grad_misc, grad_spread = dense_grads
    loss_count = jnp.sum(jnp.maximum(every_length - 1, 0)).astype(F32)
    packed = jnp.concatenate(
        [
            grad_big,
            grad_small,
            grad_negs.reshape(row_count, neg_own, col_count, piece)
            .transpose(2, 0, 1, 3)
            .reshape(width, -1),
            jnp.pad(grad_misc[:3].T, ((0, 0), (0, 125))),
        ],
        axis=1,
    )
    shard = fold_dense(packed, col_count, row_count)
    shared = jnp.concatenate(
        [fold_bias(grad_spread).reshape(-1), jnp.broadcast_to(grad_misc[3, 0], (128,))]
    )
    shared = spread_sum(shared, devices)
    rab_sum = shared[: rab.size].reshape(rab.shape)
    loss_sum = shared[rab.size]
    table_sum = jnp.zeros((rows_dev, piece), F32)
    for slot in range(slots):
        table_sum = scatter_call(
            hist[slot], ids, back[slot].reshape(devices * per, piece), table_sum, per
        )
    table_sum, squares = negs_call(
        own_negs, shard[:, 5 * width : 6 * width].reshape(neg_own, piece), table_sum
    )
    shard_big = shard[:, : 4 * width]
    shard_small = shard[:, 4 * width : 5 * width]
    shard_gain = shard[:, 6 * width : 6 * width + 3].T
    local_squares = (
        jnp.sum(squares)
        + jnp.sum(shard_big * shard_big)
        + jnp.sum(shard_small * shard_small)
        + jnp.sum(shard_gain * shard_gain)
    )
    all_squares = spread_sum(jnp.broadcast_to(local_squares, (128,)), devices)[0]
    grad_norm = jnp.sqrt(all_squares + jnp.sum(rab_sum * rab_sum)) / loss_count
    factor = jnp.minimum(1.0, CLIP_NORM / grad_norm) / loss_count
    table_new, table_m_new, table_v_new = adamw_update(
        table, table_m, table_v, table_sum * factor, RATE_TABLE
    )
    w_in_new, w_in_m_new, w_in_v_new = adamw_update(
        w_in, w_in_m, w_in_v, shard_big * factor, RATE_DENSE
    )
    w_out_new, w_out_m_new, w_out_v_new = adamw_update(
        w_out, w_out_m, w_out_v, shard_small * factor, RATE_DENSE
    )
    gains_new, gains_m_new, gains_v_new = adamw_update(
        gains, gains_m, gains_v, shard_gain * factor, RATE_SMALL
    )
    rab_new, rab_m_new, rab_v_new = adamw_update(rab, rab_m, rab_v, rab_sum * factor, RATE_SMALL)
    return (
        loss_sum,
        loss_count,
        grad_norm,
        table_new,
        table_m_new,
        table_v_new,
        table_new.astype(BF),
        w_in_new,
        w_in_m_new,
        w_in_v_new,
        w_in_new.astype(BF),
        w_out_new,
        w_out_m_new,
        w_out_v_new,
        w_out_new.astype(BF),
        gains_new,
        gains_m_new,
        gains_v_new,
        rab_new,
        rab_m_new,
        rab_v_new,
    )


def solution(mesh):
    placed = (
        P(None, ("col", "row")),
        P(None, ("col", "row"), None),
        P(),
        P(None, ("col", "row"), None),
        P("row", "col"),
        P("row", "col"),
        P("row", "col"),
        P(("col", "row"), None),
        P(("col", "row"), None),
        P(("col", "row"), None),
        P(("col", "row"), None),
        P(("col", "row"), None),
        P(("col", "row"), None),
        P(None, ("col", "row")),
        P(None, ("col", "row")),
        P(None, ("col", "row")),
        P(),
        P(),
        P(),
    )
    return jax.shard_map(
        local,
        mesh=mesh,
        in_specs=placed,
        out_specs=(
            P(),
            P(),
            P(),
            P("row", "col"),
            P("row", "col"),
            P("row", "col"),
            P("row", "col"),
            P(("col", "row"), None),
            P(("col", "row"), None),
            P(("col", "row"), None),
            P(("col", "row"), None),
            P(("col", "row"), None),
            P(("col", "row"), None),
            P(("col", "row"), None),
            P(("col", "row"), None),
            P(None, ("col", "row")),
            P(None, ("col", "row")),
            P(None, ("col", "row")),
            P(),
            P(),
            P(),
        ),
        check_vma=False,
    )
```

time: 2350 us -> 432 us (0.18)
  matrix products: 1220 us -> 0 us
  waiting for transfers between devices: 343 us -> 72.4 us
  local copies, waits for them, and re-layouts: 303 us -> 37.5 us
  blocking collectives: 232 us -> 90.9 us
  Pallas kernels: 0 us -> 121 us
  other arithmetic: 157 us -> 40.5 us
    dot_general x148 -> x0, matrix products: 1220 us -> none  [the longest x16 501 us: head_scores(): jnp.einsum('id,jd->ij', head_query, head_keys, preferred_element_type=jnp...]
    reduce_scatter x3 -> x0, waiting for transfers between devices: 322 us -> none  [the longest x1 137 us: local(): lax.psum_scatter(grad_big, ('col', 'row'), scatter_dimension=0, tiled=True)]
    gather x73 -> x2, local copies, waits for them, and re-layouts: 212 us -> 16.2 us  [the longest x1 14.2 us: bias_table(): both = 0.5 * rab[:, jnp.clip(place[:, None] - place[None, :], 0, NB - 1)]]
    pallas_call x0 -> x7, Pallas kernels: none -> 121 us  [the longest x2 93.2 us: history_call(): pl.pallas_call(history_kernel, out_shape=(jax.ShapeDtypeStruct(recv.shape...]
    all_gather x5 -> x2, blocking collectives: 148 us -> 36.6 us  [the longest x1 26.1 us: local(): about = lax.all_gather(about, 'row', axis=0, tiled=True)]
    psum x2 -> x0, blocking collectives: 84.7 us -> none  [local(): lax.psum((rab_grad, loss_total, count_total), ('col', 'row'))]
    all_to_all x0 -> x3, blocking collectives: none -> 54.3 us  [exchange(): lax.all_to_all(values, axes, split_axis=0, concat_axis=0, tiled=True, axi...]
    all_to_all x10 -> x7, waiting for transfers between devices: 21.1 us -> 72.4 us  [exchange(): lax.all_to_all(values, axes, split_axis=0, concat_axis=0, tiled=True, axi...]
  transfers between devices with their start and end apart: 15 -> 8, of which waited for: 6 -> 6; matrix products, arithmetic and copies ran while one was open for 11% -> 9% of each run, Pallas kernels for 0% -> 9%
where the time goes in v1:
time: 432 us; the launch traced here: 430 us
  Pallas kernels  121 us (28%)
  blocking collectives  90.9 us (21%)
  waiting for transfers between devices  72.4 us (17%)
  starting transfers between devices  41.2 us (10%)
  other arithmetic  40.5 us (9%)
  local copies, waits for them, and re-layouts  37.5 us (9%)
  between operations  26.2 us (6%)
    pallas_call x2, Pallas kernels, history_call(): pl.pallas_call(history_kernel, out_shape=(jax.ShapeDtypeStruct(recv.shape...  93.2 us
    all_to_all x7, waiting for transfers between devices, exchange(): lax.all_to_all(values, axes, split_axis=0, concat_axis=0, tiled=True, axi...  72.4 us
    all_to_all x3, blocking collectives, exchange(): lax.all_to_all(values, axes, split_axis=0, concat_axis=0, tiled=True, axi...  54.3 us
    all_to_all x7, starting transfers between devices, exchange(): lax.all_to_all(values, axes, split_axis=0, concat_axis=0, tiled=True, axi...  41.1 us
    all_gather x1, blocking collectives, local(): about = lax.all_gather(about, 'row', axis=0, tiled=True)  26.1 us
    pallas_call x2, Pallas kernels, scatter_call(): pl.pallas_call(scatter_kernel, out_shape=jax.ShapeDtypeStruct(init.shape,...  14.8 us
    gather x1, local copies, waits for them, and re-layouts, bias_table(): both = 0.5 * rab[:, jnp.clip(place[:, None] - place[None, :], 0, NB - 1)]  14.2 us
    pallas_call x2, Pallas kernels, lookup_call(): pl.pallas_call(lookup_kernel, out_shape=jax.ShapeDtypeStruct((count * per...  11.8 us
  transfers between devices with their start and end apart: 8, of which 6 were waited for; matrix products, arithmetic and copies ran while one was open for 9% of the time, Pallas kernels for 9%

profile of v1, /device:TPU:0, one launch (start us, length us, event | category | flops | bytes accessed | tf_op | source)
XLA Modules:
  0.0 429.7 jit_solution(7835785787881863055)
XLA Ops:
  19.8 7.3 %all-to-all-start = ((s32[32,1,384]{2,1,0:T(1,128)}), s32[32,1,384]{2,1,0:T(1,128)S(1)}, u32[]{:S(2)}, u32[]{:S(2)}) async-start(s32[32,1,384]{2,1,0:T(1,128)} %all_to_all.37), calls=%async_computation | async-start | bytes 98304 | tf_op jit(solution)/shard_map/all_to_all | solution.py:543
  27.2 7.3 %all-to-all-done = s32[32,1,384]{2,1,0:T(1,128)S(1)} async-done(((s32[32,1,384]{2,1,0:T(1,128)}), s32[32,1,384]{2,1,0:T(1,128)S(1)}, u32[]{:S(2)}, u32[]{:S(2)}) %all-to-all-start) | async-done | bytes 49184 | tf_op jit(solution)/shard_map/all_to_all | solution.py:543
  37.1 5.9 %lookup.3 = bf16[4096,128]{1,0:T(8,128)(2,1)} custom-call(s32[32]{0:T(128)S(1)} %get-tuple-element.190.hist_ref, s32[8192]{0:T(1024)S(1)} %bitcast.94, f32[3200,128]{1,0:T(8,128)S(1)} %copy-done), custom_call_target="tpu_custom_call" | custom-call | tf_op jit(solution)/shard_map/lookup/pallas_call | solution.py:439
  46.0 14.2 %gather_fusion.1 = f32[4096,8]{1,0:T(8,128)} fusion(f32[8,32]{0,1:T(8,128)S(1)} %copy.193, s32[4096]{0:T(1024)S(1)} %broadcast_clamp_fusion), kind=kCustom, calls=%fused_computation.1 | custom fusion | bytes 278528 | tf_op jit(solution)/shard_map/gather | solution.py:513
  60.2 5.9 %lookup.2 = bf16[4096,128]{1,0:T(8,128)(2,1)} custom-call(s32[32]{0:T(128)S(1)} %get-tuple-element.191.hist_ref, s32[8192]{0:T(1024)S(1)} %bitcast.95, f32[3200,128]{1,0:T(8,128)S(1)} %copy-done.1), custom_call_target="tpu_custom_call" | custom-call | tf_op jit(solution)/shard_map/lookup/pallas_call | solution.py:439
  66.1 19.4 %all-to-all-done.2 = bf16[32,128,128]{2,1,0:T(8,128)(2,1)S(1)} async-done(((bf16[32,128,128]{2,1,0:T(8,128)(2,1)}), bf16[32,128,128]{2,1,0:T(8,128)(2,1)S(1)}, u32[]{:S(2)}, u32[]{:S(2)}) %all-to-all-start.2) | async-done | bytes 1048608 | tf_op jit(solution)/shard_map/all_to_all | solution.py:543
  95.1 26.1 %all_gather.9 = s32[16,2,1024]{2,1,0:T(2,128)S(1)} all-gather(s32[2,2,1024]{2,1,0:T(2,128)S(1)} %pad_add_fusion), channel_id=1, replica_groups=mesh['col'=4,'row'=8] {'row'}, dimensions={0}, use_global_device_ids=true | all-gather | bytes 147456 | tf_op jit(solution)/shard_map/all_gather | solution.py:660
  121.2 10.5 %all_gather.10 = s32[64,2,1024]{2,1,0:T(2,128)S(1)} all-gather(s32[16,2,1024]{2,1,0:T(2,128)S(1)} %all_gather.9), channel_id=1, replica_groups=mesh['col'=4,'row'=8] {'col'}, dimensions={0}, use_global_device_ids=true | all-gather | bytes 655360 | tf_op jit(solution)/shard_map/all_gather | solution.py:661
  141.7 17.8 %history.3 = (bf16[4,1024,128]{2,1,0:T(8,128)(2,1)}, f32[512,2048]{1,0:T(8,128)}, f32[512,512]{1,0:T(8,128)}, f32[512,512]{1,0:T(8,128)}, f32[8,512]{1,0:T(8,128)}, /*index=5*/f32[8,128]{1,0:T(8,128)}) custom-call(s32[1]{0:T(128)} %get-tuple-element.194.len_ref, bf16[4,1024,128]{2,1,0:T(8,128)(2,1)} %bitcast.104, s32[1,1024]{1,0:T(1,128)} %get-tuple-element.181.order_ref, ...), custom_call_target="tpu_custom_call" | custom-call | tf_op jit(solution)/shard_map/history/pallas_call | solution.py:379
  159.6 75.3 %history.2 = (bf16[4,1024,128]{2,1,0:T(8,128)(2,1)}, f32[512,2048]{1,0:T(8,128)}, f32[512,512]{1,0:T(8,128)}, f32[512,512]{1,0:T(8,128)}, f32[8,512]{1,0:T(8,128)}, /*index=5*/f32[8,128]{1,0:T(8,128)}) custom-call(s32[1]{0:T(128)} %get-tuple-element.195.len_ref, bf16[4,1024,128]{2,1,0:T(8,128)(2,1)} %bitcast.6.recv_ref, ...), custom_call_target="tpu_custom_call" | custom-call | tf_op jit(solution)/shard_map/history/pallas_call | solution.py:379
  240.2 4.1 add_convert_fusion
  244.8 7.3 %all_to_all.59 = bf16[2,256,3200]{2,1,0:T(8,128)(2,1)} all-to-all(bf16[2,256,3200]{2,1,0:T(8,128)(2,1)S(1)} %bitcast.98), channel_id=1, replica_groups={{0,1},{2,3},{4,5},{6,7},{8,9},{10,11},{12,13},{14,15},{16,17},{18,19},{..., dimensions={0} | all-to-all | bytes 6553600 | tf_op jit(solution)/shard_map/all_to_all | solution.py:543
  252.1 4.1 reduce_sum.147
  256.2 17.6 %all-to-all-start.5 = ((bf16[4,64,3200]{2,1,0:T(8,128)(2,1)}), bf16[4,64,3200]{2,1,0:T(8,128)(2,1)S(1)}, u32[]{:S(2)}, u32[]{:S(2)}) async-start(bf16[4,64,3200]{2,1,0:T(8,128)(2,1)} %bitcast.101), calls=%async_computation.5 | async-start | bytes 3276800 | tf_op jit(solution)/shard_map/all_to_all | solution.py:543
  275.7 19.2 %all-to-all-done.5 = bf16[4,64,3200]{2,1,0:T(8,128)(2,1)S(1)} async-done(((bf16[4,64,3200]{2,1,0:T(8,128)(2,1)}), bf16[4,64,3200]{2,1,0:T(8,128)(2,1)S(1)}, u32[]{:S(2)}, u32[]{:S(2)}) %all-to-all-start.5) | async-done | bytes 1638432 | tf_op jit(solution)/shard_map/all_to_all | solution.py:543
  295.5 4.1 all-to-all-start.3
  300.7 6.2 %all-to-all-done.3 = f32[32,1,384]{2,1,0:T(1,128)S(1)} async-done(((f32[32,1,384]{2,1,0:T(1,128)}), f32[32,1,384]{2,1,0:T(1,128)S(1)}, u32[]{:S(2)}, u32[]{:S(2)}) %all-to-all-start.3) | async-done | bytes 49184 | tf_op jit(solution)/shard_map/all_to_all | solution.py:543
  307.0 16.0 %all_to_all.60 = bf16[4,16,3200]{2,1,0:T(8,128)(2,1)S(1)} all-to-all(bf16[4,16,3200]{2,1,0:T(8,128)(2,1)} %bitcast.109), channel_id=1, replica_groups={{0,2,4,6},{1,3,5,7},{8,10,12,14},{9,11,13,15},{16,18,20,22},{17,19,21,2..., dimensions={0} | all-to-all | bytes 819200 | tf_op jit(solution)/shard_map/all_to_all | solution.py:543
  323.0 31.0 %all_to_all.61 = bf16[32,128,128]{2,1,0:T(8,128)(2,1)} all-to-all(bf16[32,128,128]{2,1,0:T(8,128)(2,1)} %bitcast.110), channel_id=1, replica_groups=mesh['col'=4,'row'=8] {'col','row'}, dimensions={0} | all-to-all | bytes 2097152 | tf_op jit(solution)/shard_map/all_to_all | solution.py:543
  362.0 7.3 %scatter.2.init_ref = f32[3200,128]{1,0:T(8,128)S(1)} custom-call(s32[32]{0:T(128)S(1)} %get-tuple-element.191.hist_ref, s32[8192]{0:T(1024)S(1)} %bitcast.96, bf16[4096,128]{1,0:T(8,128)(2,1)S(1)} %bitcast.93, f32[3200,128]{1,0:T(8,128)S(1)} %broadcast_in_dim.34.init_ref), custom_call_target="tpu_custom_call" | custom-call | tf_op jit(solution)/shard_map/scatter/pallas_call | solution.py:475
  369.2 15.6 %all-to-all-done.7 = bf16[32,128,128]{2,1,0:T(8,128)(2,1)} async-done(((bf16[32,128,128]{2,1,0:T(8,128)(2,1)}), bf16[32,128,128]{2,1,0:T(8,128)(2,1)}, u32[]{:S(2)}, u32[]{:S(2)}) %all-to-all-start.7) | async-done | bytes 1048608 | tf_op jit(solution)/shard_map/all_to_all | solution.py:543
  384.9 7.5 %scatter.3.grads_ref = f32[3200,128]{1,0:T(8,128)S(1)} custom-call(s32[32]{0:T(128)S(1)} %get-tuple-element.190.hist_ref, s32[8192]{0:T(1024)S(1)} %bitcast.97, bf16[4096,128]{1,0:T(8,128)(2,1)} %bitcast.35.grads_ref, f32[3200,128]{1,0:T(8,128)S(1)} %scatter.2.init_ref), custom_call_target="tpu_custom_call" | custom-call | tf_op jit(solution)/shard_map/scatter/pallas_call | solution.py:475
  402.5 4.6 %all-to-all-done.9 = f32[32,1,128]{2,1,0:T(1,128)S(1)} async-done(((f32[32,1,128]{2,1,0:T(1,128)}), f32[32,1,128]{2,1,0:T(1,128)S(1)}, u32[]{:S(2)}, u32[]{:S(2)}) %all-to-all-start.9) | async-done | bytes 16416 | tf_op jit(solution)/shard_map/all_to_all | solution.py:543
  414.7 5.3 %fusion.19 = (bf16[3200,128]{1,0:T(8,128)(2,1)}, f32[3200,128]{1,0:T(8,128)}, f32[3200,128]{1,0:T(8,128)}, f32[3200,128]{1,0:T(8,128)}) fusion(f32[3200,128]{1,0:T(8,128)S(1)} %copy-done.1, f32[3200,128]{1,0:T(8,128)S(1)} %get-tuple-element.52, f32[]{:T(128)S(6)} %div.107, f32[3200,128]{1,0:T(8,128)} %param.24, f32[3200,128]{1,0:T(8,128)} %param.25), kind=kLoop, calls=%fused_computation.89 | loop fusion | flops 6963200 | bytes 12288004 | tf_op jit(solution)/shard_map/convert_element_type | solution.py:746
  (137 shorter events, 63.8 us)
Async XLA Ops:
  8.0 9.7 %sort.17.cloned.1.call-start = ((), (), s32[]{:S(2)}) async-start(), calls=%async_computation.11 | async-start | bytes 49184 | tf_op jit(solution)/shard_map/sort | solution.py:626
  10.7 126.7 %all-gather.2.cloned.1.call-start = ((), (), s32[]{:S(2)}) async-start(), calls=%async_computation.10 | async-start | bytes 3379200 | tf_op jit(solution)/shard_map/all_gather | solution.py:603
  19.8 14.7 %all-to-all-start = ((s32[32,1,384]{2,1,0:T(1,128)}), s32[32,1,384]{2,1,0:T(1,128)S(1)}, u32[]{:S(2)}, u32[]{:S(2)}) async-start(s32[32,1,384]{2,1,0:T(1,128)} %all_to_all.37), calls=%async_computation | async-start | bytes 98304 | tf_op jit(solution)/shard_map/all_to_all | solution.py:543
  35.7 1.4 copy-start
  43.0 2.9 copy-start.11
  43.0 42.5 %all-to-all-start.2 = ((bf16[32,128,128]{2,1,0:T(8,128)(2,1)}), bf16[32,128,128]{2,1,0:T(8,128)(2,1)S(1)}, u32[]{:S(2)}, u32[]{:S(2)}) async-start(bf16[32,128,128]{2,1,0:T(8,128)(2,1)} %bitcast.17), calls=%async_computation.2 | async-start | bytes 2097152 | tf_op jit(solution)/shard_map/all_to_all | solution.py:543
  45.8 14.4 %copy-start.1 = (f32[3200,128]{1,0:T(8,128)S(1)}, f32[3200,128]{1,0:T(8,128)}, u32[]{:S(2)}) copy-start(f32[3200,128]{1,0:T(8,128)} %table_ref.3) | copy-start | bytes 4915204
  85.5 6.5 %copy-start.3 = (bf16[32,128,128]{2,1,0:T(8,128)(2,1)}, bf16[32,128,128]{2,1,0:T(8,128)(2,1)S(1)}, u32[]{:S(2)}) copy-start(bf16[32,128,128]{2,1,0:T(8,128)(2,1)S(1)} %all-to-all-done.2) | copy-start | bytes 3145732
  85.5 74.1 %all-to-all-start.1 = ((bf16[32,128,128]{2,1,0:T(8,128)(2,1)}), bf16[32,128,128]{2,1,0:T(8,128)(2,1)}, u32[]{:S(2)}, u32[]{:S(2)}) async-start(bf16[32,128,128]{2,1,0:T(8,128)(2,1)} %bitcast.5), calls=%async_computation.1 | async-start | bytes 2097152 | tf_op jit(solution)/shard_map/all_to_all | solution.py:543
  92.0 3.1 copy-start.13
  237.5 2.4 copy-start.9
  237.5 2.4 copy-start.10
  256.2 18.1 %copy-start.14 = (f32[8,128]{1,0:T(8,128)S(1)}, f32[8,128]{1,0:T(8,128)}, u32[]{:S(2)}) copy-start(f32[8,128]{1,0:T(8,128)} %get-tuple-element.40) | copy-start | bytes 12292
  256.2 18.1 %copy-start.15 = (f32[8,128]{1,0:T(8,128)S(1)}, f32[8,128]{1,0:T(8,128)}, u32[]{:S(2)}) copy-start(f32[8,128]{1,0:T(8,128)} %get-tuple-element.39) | copy-start | bytes 12292
  256.2 38.7 %all-to-all-start.5 = ((bf16[4,64,3200]{2,1,0:T(8,128)(2,1)}), bf16[4,64,3200]{2,1,0:T(8,128)(2,1)S(1)}, u32[]{:S(2)}, u32[]{:S(2)}) async-start(bf16[4,64,3200]{2,1,0:T(8,128)(2,1)} %bitcast.101), calls=%async_computation.5 | async-start | bytes 3276800 | tf_op jit(solution)/shard_map/all_to_all | solution.py:543
  295.5 11.4 %all-to-all-start.3 = ((f32[32,1,384]{2,1,0:T(1,128)}), f32[32,1,384]{2,1,0:T(1,128)S(1)}, u32[]{:S(2)}, u32[]{:S(2)}) async-start(f32[32,1,384]{2,1,0:T(1,128)} %broadcast_in_dim.33), calls=%async_computation.3 | async-start | bytes 98304 | tf_op jit(solution)/shard_map/all_to_all | solution.py:543
  353.9 31.0 %all-to-all-start.7 = ((bf16[32,128,128]{2,1,0:T(8,128)(2,1)}), bf16[32,128,128]{2,1,0:T(8,128)(2,1)}, u32[]{:S(2)}, u32[]{:S(2)}) async-start(bf16[32,128,128]{2,1,0:T(8,128)(2,1)} %bitcast.34), calls=%async_computation.7 | async-start | bytes 2097152 | tf_op jit(solution)/shard_map/all_to_all | solution.py:543
  358.7 2.0 copy-start.4
  392.4 17.7 %copy-start.6 = (f32[16,512]{1,0:T(8,128)S(1)}, f32[16,512]{1,0:T(8,128)}, u32[]{:S(2)}) copy-start(f32[16,512]{1,0:T(8,128)} %param.29) | copy-start | bytes 98308
  392.4 17.7 %copy-start.7 = (f32[16,512]{1,0:T(8,128)S(1)}, f32[16,512]{1,0:T(8,128)}, u32[]{:S(2)}) copy-start(f32[16,512]{1,0:T(8,128)} %param.30) | copy-start | bytes 98308
  392.4 17.7 %copy-start.8 = (f32[16,512]{1,0:T(8,128)S(1)}, f32[16,512]{1,0:T(8,128)}, u32[]{:S(2)}) copy-start(f32[16,512]{1,0:T(8,128)} %param.31) | copy-start | bytes 98308
  392.4 19.1 %copy-start.5 = (f32[16,2048]{1,0:T(8,128)S(1)}, f32[16,2048]{1,0:T(8,128)}, u32[]{:S(2)}) copy-start(f32[16,2048]{1,0:T(8,128)} %param.26) | copy-start | bytes 393220
  392.4 20.9 %copy-start.12 = (f32[8,32]{1,0:T(8,128)S(1)}, f32[8,32]{1,0:T(8,128)}, u32[]{:S(2)}) copy-start(f32[8,32]{1,0:T(8,128)} %param.35) | copy-start | bytes 3076
  397.5 9.6 %all-to-all-start.9 = ((f32[32,1,128]{2,1,0:T(1,128)}), f32[32,1,128]{2,1,0:T(1,128)S(1)}, u32[]{:S(2)}, u32[]{:S(2)}) async-start(f32[32,1,128]{2,1,0:T(1,128)} %broadcast_in_dim_broadcast_in_dim_broadcast_in_dim.3), calls=%async_computation.9 | async-start | bytes 32768 | tf_op jit(solution)/shard_map/all_to_all | solution.py:543
  (1 other events, 1.2 us)
Sparse Core Ops, SparseCore 0:
  11.9 5.5 sort.19.cloned.1.call-done
  (1 shorter events, 0.0 us)
Sparse Core Ops, SparseCore 1:
  16.8 68.6 all-gather.1

commit v2 on v1

v2 whole, which is shorter than its diff:
```python
import functools
import jax
import jax.numpy as jnp
from jax import lax
from jax.experimental import pallas as pl
from jax.experimental.pallas import tpu as pltpu
from jax.sharding import PartitionSpec as P

NB = 32
STEP = 10
BETA_ONE = 0.9
BETA_TWO = 0.999
EPS_ADAM = 1e-08
EPS_NORM = 1e-06
WEIGHT_DECAY = 0.01
CLIP_NORM = 0.05
RATE_TABLE = 0.06
RATE_DENSE = 0.01
RATE_SMALL = 0.5
BOTH = ("col", "row")
TILE = 256
BF = jnp.bfloat16
F32 = jnp.float32


def dot_nn(left, right):
    return lax.dot_general(left, right, (((1,), (0,)), ((), ())), preferred_element_type=F32)


def dot_nt(left, right):
    return lax.dot_general(left, right, (((1,), (1,)), ((), ())), preferred_element_type=F32)


def dot_tn(left, right):
    return lax.dot_general(left, right, (((0,), (0,)), ((), ())), preferred_element_type=F32)


def row_scale(values):
    return lax.rsqrt(jnp.mean(values * values, axis=-1, keepdims=True) + EPS_NORM)


def row_back(values, scale, grad):
    cubed = scale * scale * scale
    return scale * grad - values * (cubed * jnp.mean(grad * values, axis=-1, keepdims=True))


def silu_slope(values):
    half = 0.5 * jnp.tanh(0.5 * values)
    sigmoid = 0.5 + half
    active = values * sigmoid
    return active, sigmoid + active * (0.5 - half)


def history_kernel(last, blocked, *refs):
    if last:
        (len_ref, core_ref, recv_ref, dense_ref, bias_ref, misc0_ref, big0_ref, small0_ref, gneg0_ref) = refs[:9]
        (ge_ref, misc_ref, keep_ref, send_ref) = refs[9:13]
        (big_ref, small_ref, gneg_ref, load_sem) = refs[13:17]
        scratch = refs[17:]
    else:
        (len_ref, recv_ref, dense_ref, bias_ref) = refs[:4]
        (ge_ref, misc_ref, big_ref, small_ref, gneg_ref) = refs[4:9]
        scratch = refs[9:]
    (
        rows_s,
        event_s,
        normed_s,
        gatein_s,
        slope_s,
        valuem_s,
        query_s,
        keys_s,
        keyst_s,
        hot_s,
        hott_s,
        orderc_s,
        order_s,
        out_s,
        gout_s,
        ggate_s,
        dkeys_s,
        dqueryt_s,
        gslots_s,
        carry_s,
        pairs_s,
        gains_s,
        negs_s,
        bias_s,
    ) = scratch
    pieces, blocks, tall, piece = recv_ref.shape
    per = tall - 16
    seq, width = normed_s.shape
    groups = width // 128
    heads = 2 * groups
    devices = pieces * blocks
    own = width // devices
    length = len_ref[0]
    tiles = lax.div(length + (TILE - 1), TILE)
    lane = lax.broadcasted_iota(jnp.int32, (TILE, 128), 1)
    low_lanes = lane < 64
    if last:
        loads = [
            pltpu.make_async_copy(big0_ref, big_ref, load_sem.at[0]),
            pltpu.make_async_copy(small0_ref, small_ref, load_sem.at[1]),
            pltpu.make_async_copy(gneg0_ref, gneg_ref, load_sem.at[2]),
        ]
        for one in loads:
            one.start()
    else:
        big_ref[...] = jnp.zeros_like(big_ref)
        small_ref[...] = jnp.zeros_like(small_ref)
        gneg_ref[...] = jnp.zeros_like(gneg_ref)

    def place(step):
        return pl.ds(pl.multiple_of(step * TILE, TILE), TILE)

    for block in range(blocks):
        span = slice(block * per, (block + 1) * per)
        for one in range(pieces):
            rows_s[span, one * piece : (one + 1) * piece] = recv_ref[one, block, 0:per, :]
        about = recv_ref[0, block, per : per + 16, :].astype(F32)
        spot = about[0:1, 0:per] * 32.0 + about[1:2, 0:per]
        order_s[0:1, span] = spot.astype(jnp.int32)
        orderc_s[span, :] = jnp.broadcast_to(about[0:1, :] * 32.0 + about[1:2, :], (128, 128)).T[0:per, :].astype(jnp.int32)
        rows_s[span, width : width + 128] = jnp.broadcast_to(about[2:3, :], (128, 128)).T[0:per, :].astype(BF)
    if blocked:
        for one in range(pieces):
            for block in range(blocks):
                source = slice((one * blocks + block) * own, (one * blocks + block + 1) * own)
                for index in range(width // piece):
                    start = (block * (width // piece) + index) * own
                    negs_s[start : start + own, one * piece : (one + 1) * piece] = dense_ref[
                        source, 5 * width + index * piece : 5 * width + (index + 1) * piece
                    ]
    else:
        negs_s[...] = dense_ref[:, 5 * width : 6 * width]
    gains_s[...] = dense_ref[:, 6 * width : 6 * width + 128].astype(F32).T[0:8, :]
    lane_half = lax.broadcasted_iota(jnp.int32, (64, 128), 1) < 64
    for head in range(heads):
        line = jnp.broadcast_to(bias_ref[head : head + 1, :], (64, 128))
        wide = pltpu.roll(line, 0, 1, stride=1, stride_axis=0)
        again = pltpu.roll(wide, 64, 1)
        whole = jnp.where(lane_half, wide, again)
        upper = whole.astype(BF)
        lower = (whole - upper.astype(F32)).astype(BF)
        bias_s[0:64, head * 128 : (head + 1) * 128] = jnp.where(lane_half, upper, lower)
    bias_s[64:128, :] = jnp.zeros((64, heads * 128), BF)
    misc_ref[...] = misc0_ref[...] if last else jnp.zeros_like(misc_ref)
    gslots_s[...] = jnp.zeros_like(gslots_s)
    carry_s[...] = jnp.zeros_like(carry_s)
    pairs_s[...] = jnp.zeros_like(pairs_s)
    gain_in = gains_s[0:1, :]
    gain_mid = gains_s[1:2, :]
    gain_out = gains_s[2:3, :]

    def project(step, _):
        span = place(step)
        hot = jnp.where(
            order_s[0:1, :] == lax.broadcasted_iota(jnp.int32, (TILE, seq), 0) + step * TILE,
            1.0,
            0.0,
        ).astype(BF)
        wide = dot_nn(hot, rows_s[...])
        event = wide[:, 0:width]
        times = wide[:, width : width + 128].astype(jnp.int32)
        bucket = jnp.where(times == jnp.bitwise_and(lane, 63), 1.0, 0.0).astype(BF)
        hot_s[span, :] = bucket
        hott_s[:, span] = jnp.where(times == 63 - lane, 1.0, 0.0).T[0:64, :].astype(BF)
        event_s[span, :] = event.astype(BF)
        normed = (event * row_scale(event) * gain_in).astype(BF)
        normed_s[span, :] = normed
        gatein_s[span, :] = dot_nn(normed, dense_ref[:, 0:width])
        active, slope = silu_slope(dot_nn(normed, dense_ref[:, width : 2 * width]))
        slope_s[0, span, :] = slope.astype(BF)
        scaled = active.astype(BF) * BF(1.0 / seq)
        for group in range(groups):
            part = scaled[:, group * 128 : (group + 1) * 128]
            valuem_s[2 * group, span, :] = jnp.where(low_lanes, part, BF(0))
            valuem_s[2 * group + 1, span, :] = jnp.where(low_lanes, BF(0), part)
        active, slope = silu_slope(dot_nn(normed, dense_ref[:, 2 * width : 3 * width]))
        slope_s[1, span, :] = slope.astype(BF)
        scaled = active.astype(BF) * BF(0.25)
        bias = dot_nn(bucket, bias_s[...]).astype(BF)
        for group in range(groups):
            part = scaled[:, group * 128 : (group + 1) * 128]
            query_s[2 * group, span, 0:128] = jnp.where(low_lanes, part, BF(0))
            query_s[2 * group + 1, span, 0:128] = jnp.where(low_lanes, BF(0), part)
            query_s[2 * group, span, 128:256] = bias[:, group * 256 : group * 256 + 128]
            query_s[2 * group + 1, span, 128:256] = bias[:, group * 256 + 128 : group * 256 + 256]
        active, slope = silu_slope(dot_nn(normed, dense_ref[:, 3 * width : 4 * width]))
        slope_s[2, span, :] = slope.astype(BF)
        scaled = active.astype(BF)
        for group in range(groups):
            part = scaled[:, group * 128 : (group + 1) * 128]
            keys_s[group, span, 0:128] = part
            keys_s[group, span, 128:256] = bucket
            turned = part.T
            keyst_s[2 * group, :, span] = turned[0:64, :]
            keyst_s[2 * group + 1, :, span] = turned[64:128, :]
        for head in range(heads):
            dkeys_s[head, span, :] = jnp.zeros((TILE, 256), F32)
            dqueryt_s[head, :, span] = jnp.zeros((64, TILE), F32)
        return 0

    lax.fori_loop(0, tiles, project, 0)

    square_row = lax.broadcasted_iota(jnp.int32, (TILE, TILE), 0)
    square_col = lax.broadcasted_iota(jnp.int32, (TILE, TILE), 1)

    def attend_group(group, _):
        def attend_tile(step, _):
            span = place(step)

            def attend(other, masked):
                near = place(other)
                total = None
                for half in range(2):
                    scores = dot_nt(query_s[2 * group + half, span, :], keys_s[group, near, :])
                    weight = scores + scores * jnp.tanh(scores)
                    if masked:
                        weight = jnp.where(square_col <= square_row, weight, 0.0)
                    part = dot_nn(weight.astype(BF), valuem_s[2 * group + half, near, :])
                    total = part if total is None else total + part
                return total

            out_s[group, span, :] = attend(step, True)

            def before(other, _):
                out_s[group, span, :] += attend(other, False)
                return 0

            lax.fori_loop(0, step, before, 0)
            return 0

        lax.fori_loop(0, tiles, attend_tile, 0)
        return 0

    lax.fori_loop(0, groups, attend_group, 0)

    if last:
        for one in loads:
            one.wait()

    def middle(step, _):
        span = place(step)
        event = event_s[span, :].astype(F32)
        merged = jnp.concatenate([out_s[group, span, :] for group in range(groups)], axis=1)
        for group in range(groups):
            out_s[group, span, :] = jnp.zeros((TILE, 128), F32)
        scale_mid = row_scale(merged)
        normed_mid = merged * scale_mid
        gate, gate_slope = silu_slope(gatein_s[span, :])
        mixed = (normed_mid * gain_mid * gate).astype(BF)
        hidden = event + dot_nn(mixed, dense_ref[:, 4 * width : 5 * width])
        scale_out = row_scale(hidden)
        final = (hidden * scale_out * gain_out).astype(BF)
        final_f = final.astype(F32)
        following = event_s[pl.ds(pl.multiple_of((step + 1) * TILE, TILE), 16), :][0:1, :].astype(F32)
        following = jnp.where(step + 1 < tiles, following, 0.0)
        row_id = lax.broadcasted_iota(jnp.int32, (TILE, width), 0)
        target = jnp.where(
            row_id == TILE - 1, following, pltpu.roll(event, TILE - 1, 0)
        )
        positive = jnp.sum(final_f * target, axis=-1, keepdims=True)
        negative = dot_nt(final, negs_s[...])
        highest = jnp.maximum(jnp.max(negative, axis=-1, keepdims=True), positive)
        neg_exp = jnp.exp(negative - highest)
        pos_exp = jnp.exp(positive - highest)
        totals = pos_exp + jnp.sum(neg_exp, axis=-1, keepdims=True)
        counted = (
            lax.broadcasted_iota(jnp.int32, (TILE, 1), 0) + step * TILE < length - 1
        )
        losses = jnp.where(counted, highest + jnp.log(totals) - positive, 0.0)
        misc_ref[3:4, :] += jnp.broadcast_to(jnp.sum(losses, axis=0, keepdims=True), (1, width))
        share = jnp.where(counted, 1.0 / totals, 0.0)
        grad_neg = (neg_exp * share).astype(BF)
        grad_pos = jnp.where(counted, pos_exp * share - 1.0, 0.0)
        grad_final = dot_nn(grad_neg, negs_s[...]) + grad_pos * target
        gneg_ref[...] += dot_tn(grad_neg, final)
        pushed = grad_pos * final_f
        grad_event = jnp.where(row_id == 0, carry_s[0:1, :], pltpu.roll(pushed, 1, 0))
        carry_s[0:1, :] = pushed[TILE - 1 : TILE, :]
        misc_ref[2:3, :] += jnp.sum(grad_final * hidden * scale_out, axis=0, keepdims=True)
        grad_hidden = row_back(hidden, scale_out, grad_final * gain_out)
        gatein_s[span, :] = grad_event + grad_hidden
        branch = grad_hidden.astype(BF)
        small_ref[...] += dot_tn(mixed, branch)
        grad_mixed = dot_nt(branch, dense_ref[:, 4 * width : 5 * width])
        gated = grad_mixed * gate
        misc_ref[1:2, :] += jnp.sum(gated * normed_mid, axis=0, keepdims=True)
        ggate_s[span, :] = (grad_mixed * normed_mid * gain_mid * gate_slope).astype(BF)
        grad_out = row_back(merged, scale_mid, gated * gain_mid).astype(BF) * BF(0.5)
        for group in range(groups):
            part = grad_out[:, group * 128 : (group + 1) * 128]
            gout_s[2 * group, span, :] = jnp.where(low_lanes, part, BF(0))
            gout_s[2 * group + 1, span, :] = jnp.where(low_lanes, BF(0), part)
        return 0

    lax.fori_loop(0, tiles, middle, 0)

    def retreat_group(group, _):
        def retreat_tile(step, _):
            near = place(step)

            def retreat(other, masked):
                span = place(other)
                keys = keys_s[group, near, :]
                total = None
                for half in range(2):
                    head = 2 * group + half
                    gout = gout_s[head, span, :]
                    query = query_s[head, span, :]
                    scores = dot_nt(keys, query)
                    grads = dot_nt(valuem_s[head, near, :], gout)
                    bent = 1.0 + jnp.tanh(scores)
                    weight = scores * bent
                    slope = bent * ((1.0 + (scores + scores)) - weight)
                    grads = grads * slope
                    if masked:
                        visible = square_row <= square_col
                        weight = jnp.where(visible, weight, 0.0)
                        grads = jnp.where(visible, grads, 0.0)
                    grads = grads.astype(BF)
                    part = dot_nn(weight.astype(BF), gout)
                    total = part if total is None else total + part
                    dkeys_s[head, near, :] += dot_nn(
                        grads, jnp.concatenate([query[:, 0:128], hot_s[span, :]], axis=1)
                    )
                    dqueryt_s[head, :, span] += dot_nn(keyst_s[head, :, near], grads)
                out_s[group, near, :] += total

            retreat(step, True)

            def after(other, _):
                retreat(other, False)
                return 0

            lax.fori_loop(step + 1, tiles, after, 0)
            return 0

        lax.fori_loop(0, tiles, retreat_tile, 0)
        return 0

    lax.fori_loop(0, groups, retreat_group, 0)

    def finish(step, _):
        span = place(step)
        normed = normed_s[span, :]
        parts = [ggate_s[span, :]]
        grad = jnp.concatenate([out_s[group, span, :] for group in range(groups)], axis=1)
        parts.append((grad * (2.0 / seq) * slope_s[0, span, :].astype(F32)).astype(BF))
        grad = jnp.concatenate(
            [
                jnp.concatenate([dqueryt_s[2 * group, :, span], dqueryt_s[2 * group + 1, :, span]], axis=0).T
                for group in range(groups)
            ],
            axis=1,
        )
        parts.append((grad * 0.5 * slope_s[1, span, :].astype(F32)).astype(BF))
        grad = jnp.concatenate(
            [
                dkeys_s[2 * group, span, 0:128] + dkeys_s[2 * group + 1, span, 0:128]
                for group in range(groups)
            ],
            axis=1,
        )
        parts.append((grad * 2.0 * slope_s[2, span, :].astype(F32)).astype(BF))
        grad_normed = None
        for index in range(4):
            columns = slice(index * width, (index + 1) * width)
            big_ref[:, columns] += dot_tn(normed, parts[index])
            part = dot_nt(parts[index], dense_ref[:, columns])
            grad_normed = part if grad_normed is None else grad_normed + part
        hott = hott_s[:, span]
        for head in range(heads):
            wide = dkeys_s[head, span, 128:256]
            upper = wide.astype(BF)
            lower = (wide - upper.astype(F32)).astype(BF)
            pairs_s[head] += dot_nn(hott, upper) + dot_nn(hott, lower)
        event = event_s[span, :].astype(F32)
        scale = row_scale(event)
        misc_ref[0:1, :] += jnp.sum(grad_normed * event * scale, axis=0, keepdims=True)
        total = gatein_s[span, :] + row_back(event, scale, grad_normed * gain_in)
        column = orderc_s[...]
        hot = jnp.where(
            jnp.concatenate([column] * (TILE // 128), axis=1)
            == lax.broadcasted_iota(jnp.int32, (seq, TILE), 1) + step * TILE,
            1.0,
            0.0,
        ).astype(BF)
        gslots_s[...] += dot_nn(hot, total.astype(BF))
        return 0

    lax.fori_loop(0, tiles, finish, 0)

    for block in range(blocks):
        span = slice(block * per, (block + 1) * per)
        for one in range(pieces):
            ge_ref[one, block] = gslots_s[span, one * piece : (one + 1) * piece].astype(BF)
    lane_row = lax.broadcasted_iota(jnp.int32, (64, 128), 1)
    for head in range(heads):
        kept = jnp.where(lane_row < 64, pairs_s[head], 0.0)
        turned = pltpu.roll(kept, 0, 1, stride=1, stride_axis=0)
        misc_ref[8 + head : 9 + head, 0:128] += jnp.sum(turned, axis=0, keepdims=True)
    if last:
        kept = jnp.where(lax.broadcasted_iota(jnp.int32, (8, width), 0) < 3, misc_ref[0:8, :], 0.0)
        gain_rows = jnp.concatenate([kept, jnp.zeros((120, width), F32)], axis=0)
        gain_rows = gain_rows.T.astype(BF)

        def pack(out_ref, target, source, one, block):
            out_ref[target, 0 : 4 * width] = big_ref[source, :].astype(BF)
            out_ref[target, 4 * width : 5 * width] = small_ref[source, :].astype(BF)
            if blocked:
                for index in range(width // piece):
                    start = (block * (width // piece) + index) * own
                    out_ref[target, 5 * width + index * piece : 5 * width + (index + 1) * piece] = gneg_ref[
                        start : start + own, one * piece : (one + 1) * piece
                    ].astype(BF)
            else:
                out_ref[target, 5 * width : 6 * width] = gneg_ref[source, :].astype(BF)
            out_ref[target, 6 * width : 6 * width + 128] = gain_rows[source, :]

        if blocked:
            for core in range(2):

                @pl.when(core_ref[0] == core)
                def _(core=core):
                    for device in range(devices):
                        one, block = device // blocks, device % blocks
                        source = slice(device * own, (device + 1) * own)
                        target = slice(device // 2 * own, (device // 2 + 1) * own)
                        pack(keep_ref if device % 2 == core else send_ref, target, source, one, block)

        else:
            half = width // 2
            pack(keep_ref, slice(0, half), slice(0, half), 0, 0)
            pack(send_ref, slice(0, half), slice(half, width), 0, 0)


def history_call(length, recv, dense, bias, core, before, blocked):
    last = before is not None
    pieces, blocks, tall, piece = recv.shape
    per = tall - 16
    seq = blocks * per
    width = pieces * piece
    heads = width // 64
    groups = heads // 2
    neg_total = width
    vmem = pl.BlockSpec(memory_space=pltpu.VMEM)
    smem = pl.BlockSpec(memory_space=pltpu.SMEM)
    anywhere = pl.BlockSpec(memory_space=pl.ANY)
    shapes = [
        jax.ShapeDtypeStruct((pieces, blocks, per, piece), BF),
        jax.ShapeDtypeStruct((16, width), F32),
    ]
    sums = [(width, 4 * width), (width, width), (neg_total, width)]
    if last:
        operands = (length, core, recv, dense, bias, *before)
        specs = [smem, smem, vmem, vmem, vmem, vmem, anywhere, anywhere, anywhere]
        shapes += [jax.ShapeDtypeStruct((width // 2, 6 * width + 128), BF)] * 2
        extra = [pltpu.VMEM(one, F32) for one in sums] + [pltpu.SemaphoreType.DMA((3,))]
    else:
        operands = (length, recv, dense, bias)
        specs = [smem, vmem, vmem, vmem]
        shapes += [jax.ShapeDtypeStruct(one, F32) for one in sums]
        extra = []
    return pl.pallas_call(
        functools.partial(history_kernel, last, blocked),
        out_shape=tuple(shapes),
        in_specs=specs,
        out_specs=(vmem,) * len(shapes),
        scratch_shapes=extra
        + [
            pltpu.VMEM((seq, width + 128), BF),
            pltpu.VMEM((seq + TILE, width), BF),
            pltpu.VMEM((seq, width), BF),
            pltpu.VMEM((seq, width), F32),
            pltpu.VMEM((3, seq, width), BF),
            pltpu.VMEM((heads, seq, 128), BF),
            pltpu.VMEM((heads, seq, 256), BF),
            pltpu.VMEM((groups, seq, 256), BF),
            pltpu.VMEM((heads, 64, seq), BF),
            pltpu.VMEM((seq, 128), BF),
            pltpu.VMEM((64, seq), BF),
            pltpu.VMEM((seq, 128), jnp.int32),
            pltpu.VMEM((8, seq), jnp.int32),
            pltpu.VMEM((groups, seq, 128), F32),
            pltpu.VMEM((heads, seq, 128), BF),
            pltpu.VMEM((seq, width), BF),
            pltpu.VMEM((heads, seq, 256), F32),
            pltpu.VMEM((heads, 64, seq), F32),
            pltpu.VMEM((seq, width), F32),
            pltpu.VMEM((8, width), F32),
            pltpu.VMEM((heads, 64, 128), F32),
            pltpu.VMEM((8, width), F32),
            pltpu.VMEM((neg_total, width), BF),
            pltpu.VMEM((128, heads * 128), BF),
        ],
        compiler_params=pltpu.CompilerParams(vmem_limit_bytes=60 * 1024 * 1024),
        cost_estimate=pl.CostEstimate(
            flops=40_000_000_000, bytes_accessed=20_000_000, transcendentals=10_000_000
        ),
        name="history_last" if last else "history_first",
    )(*operands)


def lookup_kernel(hist_ref, ids_ref, about_ref, table_ref, found_ref, stage_s):
    count, tall, piece = found_ref.shape
    per = tall - 16

    def one(place, _):
        number = hist_ref[place]
        for index in range(per):
            stage_s[index : index + 1, :] = table_ref[pl.ds(ids_ref[number, index], 1), :]
        found_ref[place, 0:per, :] = stage_s[...].astype(BF)
        spot = about_ref[number, 1:2, :]
        upper = lax.shift_right_logical(spot, 5)
        rows = [upper, spot - upper * 32, about_ref[number, 2:3, :], jnp.zeros((13, piece), jnp.int32)]
        found_ref[place, per:tall, :] = jnp.concatenate(rows, axis=0).astype(F32).astype(BF)
        return 0

    lax.fori_loop(0, count, one, 0)


def lookup_call(hist, ids, about, table, per):
    count = hist.shape[0]
    smem = pl.BlockSpec(memory_space=pltpu.SMEM)
    vmem = pl.BlockSpec(memory_space=pltpu.VMEM)
    return pl.pallas_call(
        lookup_kernel,
        out_shape=jax.ShapeDtypeStruct((count, per + 16, table.shape[1]), BF),
        in_specs=[smem, smem, vmem, vmem],
        out_specs=vmem,
        scratch_shapes=[pltpu.VMEM((per, table.shape[1]), F32)],
        compiler_params=pltpu.CompilerParams(vmem_limit_bytes=60 * 1024 * 1024),
        cost_estimate=pl.CostEstimate(
            flops=5_000_000_000, bytes_accessed=4_000_000, transcendentals=0
        ),
        name="lookup",
    )(hist, ids, about, table)


def add_rows(hist_ref, ids_ref, grads_ref, stage_s, sums):
    count = hist_ref.shape[0]
    per = stage_s.shape[0]
    for held in sums:
        held[...] = jnp.zeros_like(held)

    def one(place, _):
        number = hist_ref[place]
        stage_s[...] = grads_ref[pl.ds(pl.multiple_of(place * per, per), per), :].astype(F32)
        for index in range(per):
            held = sums[index % len(sums)]
            spot = pl.ds(ids_ref[number, index], 1)
            held[spot, :] = held[spot, :] + stage_s[index : index + 1, :]
        return 0

    lax.fori_loop(0, count, one, 0)


def scatter_kernel(hist_ref, ids_ref, grads_ref, *refs):
    total_ref, stage_s = refs[-6:-4]
    add_rows(hist_ref, ids_ref, grads_ref, stage_s, refs[-4:])
    total = refs[-4][...]
    for held in refs[-3:]:
        total = total + held[...]
    for init_ref in refs[:-6]:
        total = total + init_ref[...]
    total_ref[...] = total


def scatter_call(hist, ids, grads, rows, per, *init):
    smem = pl.BlockSpec(memory_space=pltpu.SMEM)
    vmem = pl.BlockSpec(memory_space=pltpu.VMEM)
    piece = grads.shape[1]
    return pl.pallas_call(
        scatter_kernel,
        out_shape=jax.ShapeDtypeStruct((rows, piece), F32),
        in_specs=[smem, smem, vmem] + [vmem] * len(init),
        out_specs=vmem,
        scratch_shapes=[pltpu.VMEM((per, piece), F32)] + [pltpu.VMEM((rows, piece), F32)] * 4,
        compiler_params=pltpu.CompilerParams(vmem_limit_bytes=60 * 1024 * 1024),
        cost_estimate=pl.CostEstimate(
            flops=6_000_000_000, bytes_accessed=4_000_000, transcendentals=0
        ),
        name="scatter",
    )(hist, ids, grads, *init)


def gather_up_kernel(width, spots_ref, table_ref, misc_ref, base_ref, *refs):
    total_ref, shard_ref, gain_ref, told_ref = refs[-4:]
    shard = base_ref[...]
    for got in refs[:-4]:
        shard = shard + got[...].astype(F32)
    shard_ref[...] = shard
    own = shard.shape[0]
    total_ref[...] = table_ref[...]
    for index in range(spots_ref.shape[0]):
        spot = pl.ds(spots_ref[index], 1)
        row = index % own
        start = 5 * width + index // own * 128
        total_ref[spot, :] = total_ref[spot, :] + shard_ref[row : row + 1, start : start + 128]
    total = total_ref[...]
    squares = jnp.sum(total * total, axis=0, keepdims=True)
    for index in range(5 * width // 128):
        part = shard_ref[:, index * 128 : (index + 1) * 128]
        squares = squares + jnp.sum(part * part, axis=0, keepdims=True)
    part = shard_ref[:, 6 * width : 6 * width + 128]
    squares = squares + jnp.sum(part * part, axis=0, keepdims=True)
    turned = jnp.concatenate([part, jnp.zeros((128 - own, 128), F32)], axis=0).T
    gain_ref[...] = turned[0:8, :]
    spread = misc_ref[8:16, 0:128]
    lane = lax.broadcasted_iota(jnp.int32, (8, 128), 1)
    low = jnp.sum(jnp.where(lane < 63, spread, 0.0), axis=1, keepdims=True)
    high = jnp.sum(jnp.where(lane >= 62 + NB, spread, 0.0), axis=1, keepdims=True)
    folded = jnp.where(lane < NB - 1, pltpu.roll(spread, 65, 1), 0.0)
    folded = folded + jnp.where(lane == 0, low, 0.0) + jnp.where(lane == NB - 1, high, 0.0)
    rows = []
    for half in range(2):
        row = folded[4 * half : 4 * half + 1, :]
        for index in range(1, 4):
            row = row + pltpu.roll(folded[4 * half + index : 4 * half + index + 1, :], NB * index, 1)
        rows.append(row)
    rows += [misc_ref[3:4, 0:128], squares]
    told_ref[...] = jnp.broadcast_to(jnp.concatenate(rows, axis=0)[None], told_ref.shape)


def gather_up_call(spots, table_sum, misc, base, gots, devices):
    vmem = pl.BlockSpec(memory_space=pltpu.VMEM)
    return pl.pallas_call(
        functools.partial(gather_up_kernel, misc.shape[1]),
        out_shape=(
            jax.ShapeDtypeStruct(table_sum.shape, F32),
            jax.ShapeDtypeStruct(base.shape, F32),
            jax.ShapeDtypeStruct((8, 128), F32),
            jax.ShapeDtypeStruct((devices, 4, 128), F32),
        ),
        in_specs=[pl.BlockSpec(memory_space=pltpu.SMEM)] + [vmem] * (3 + len(gots)),
        out_specs=(vmem,) * 4,
        compiler_params=pltpu.CompilerParams(vmem_limit_bytes=60 * 1024 * 1024),
        name="gather_up",
    )(spots, table_sum, misc, base, *gots)


def fold_kernel(parts, place_ref, base_ref, *refs):
    gots = refs[: len(refs) - parts]
    own_ref = refs[len(refs) - parts]
    sends = refs[len(refs) - parts + 1 :]
    tall = own_ref.shape[0]
    for offset in range(parts):
        span = pl.ds(pl.multiple_of(lax.bitwise_xor(place_ref[0], offset) * tall, tall), tall)
        total = base_ref[span, :].astype(F32)
        for got in gots:
            total = total + got[span, :].astype(F32)
        if offset == 0:
            own_ref[...] = total
        else:
            sends[offset - 1][...] = total.astype(BF)


def fold_call(place, base, gots, parts):
    tall = base.shape[0] // parts
    vmem = pl.BlockSpec(memory_space=pltpu.VMEM)
    shapes = [jax.ShapeDtypeStruct((tall, base.shape[1]), F32)]
    shapes += [jax.ShapeDtypeStruct((tall, base.shape[1]), BF)] * (parts - 1)
    return pl.pallas_call(
        functools.partial(fold_kernel, parts),
        out_shape=tuple(shapes),
        in_specs=[pl.BlockSpec(memory_space=pltpu.SMEM)] + [vmem] * (1 + len(gots)),
        out_specs=(vmem,) * parts,
        compiler_params=pltpu.CompilerParams(vmem_limit_bytes=60 * 1024 * 1024),
        name="fold",
    )(place, base, *gots)


def update_kernel(
    width,
    count_ref,
    heard_ref,
    shard_ref,
    sum_ref,
    table_ref,
    table_m_ref,
    table_v_ref,
    w_in_ref,
    w_in_m_ref,
    w_in_v_ref,
    w_out_ref,
    w_out_m_ref,
    w_out_v_ref,
    gain_grad_ref,
    gains_ref,
    gains_m_ref,
    gains_v_ref,
    rab_ref,
    rab_m_ref,
    rab_v_ref,
    scalars_ref,
    table_new_ref,
    table_m_new_ref,
    table_v_new_ref,
    table_low_ref,
    w_in_new_ref,
    w_in_m_new_ref,
    w_in_v_new_ref,
    w_in_low_ref,
    w_out_new_ref,
    w_out_m_new_ref,
    w_out_v_new_ref,
    w_out_low_ref,
    gains_new_ref,
    gains_m_new_ref,
    gains_v_new_ref,
    rab_new_ref,
    rab_m_new_ref,
    rab_v_new_ref,
    factor_s,
    rab_s,
):
    def update(weight_ref, first_ref, second_ref, grad, rate, outs):
        weight, first, second = adamw_update(
            weight_ref[...], first_ref[...], second_ref[...], grad, rate
        )
        outs[0][...] = weight
        outs[1][...] = first
        outs[2][...] = second
        if len(outs) > 3:
            outs[3][...] = weight.astype(BF)

    @pl.when(pl.program_id(0) == 0)
    def _():
        heard = jnp.sum(heard_ref[...], axis=0)
        for head in range(rab_s.shape[0]):
            rab_s[head : head + 1, :] = heard[
                head // 4 : head // 4 + 1, head % 4 * NB : (head % 4 + 1) * NB
            ]
        count = jnp.full((1, 1), count_ref[0].astype(F32))
        squares = jnp.sum(heard[3:4, :], axis=1, keepdims=True)
        squares = squares + jnp.sum(jnp.sum(heard[0:2, :] * heard[0:2, :], axis=1, keepdims=True), axis=0, keepdims=True)
        norm = jnp.sqrt(squares) / count
        factor = jnp.minimum(1.0, CLIP_NORM / norm) / count
        factor_s[...] = jnp.broadcast_to(factor, factor_s.shape)
        scalars_ref[...] = jnp.concatenate([jnp.broadcast_to(one, (1, 128)) for one in (heard[2:3, 0:1], count, norm)] + [jnp.zeros((5, 128), F32)], axis=0)
        update(
            w_in_ref,
            w_in_m_ref,
            w_in_v_ref,
            shard_ref[:, 0 : 4 * width] * factor,
            RATE_DENSE,
            (w_in_new_ref, w_in_m_new_ref, w_in_v_new_ref, w_in_low_ref),
        )
        update(
            w_out_ref,
            w_out_m_ref,
            w_out_v_ref,
            shard_ref[:, 4 * width : 5 * width] * factor,
            RATE_DENSE,
            (w_out_new_ref, w_out_m_new_ref, w_out_v_new_ref, w_out_low_ref),
        )
        update(
            gains_ref,
            gains_m_ref,
            gains_v_ref,
            gain_grad_ref[0:3, 0 : gains_ref.shape[1]] * factor,
            RATE_SMALL,
            (gains_new_ref, gains_m_new_ref, gains_v_new_ref),
        )
        update(
            rab_ref,
            rab_m_ref,
            rab_v_ref,
            rab_s[...] * factor,
            RATE_SMALL,
            (rab_new_ref, rab_m_new_ref, rab_v_new_ref),
        )

    update(
        table_ref,
        table_m_ref,
        table_v_ref,
        sum_ref[...] * factor_s[0:1, :],
        RATE_TABLE,
        (table_new_ref, table_m_new_ref, table_v_new_ref, table_low_ref),
    )


def update_call(count, heard, shard, table_sum, tables, w_ins, w_outs, gain_grad, gains, rabs):
    steps = 5
    rows, piece = table_sum.shape

    def whole(array):
        zeros = (0,) * len(array.shape)
        return pl.BlockSpec(array.shape, lambda step: zeros)

    def block(array):
        return pl.BlockSpec((rows // steps, piece), lambda step: (step, 0))

    operands = [heard, shard, table_sum, *tables, *w_ins, *w_outs, gain_grad, *gains, *rabs]
    specs = [pl.BlockSpec(memory_space=pltpu.SMEM)]
    specs += [block(one) if one.shape == (rows, piece) else whole(one) for one in operands]

    def like(array, kind=F32):
        return jax.ShapeDtypeStruct(array.shape, kind)

    shapes = [jax.ShapeDtypeStruct((8, 128), F32)]
    for group in (tables, w_ins, w_outs, gains, rabs):
        shapes += [like(group[0])] * 3
        if group is tables or group is w_ins or group is w_outs:
            shapes.append(like(group[0], BF))
    return pl.pallas_call(
        functools.partial(update_kernel, shard.shape[1] // 6 // 128 * 128),
        out_shape=tuple(shapes),
        grid=(steps,),
        in_specs=specs,
        out_specs=tuple(block(one) if one.shape == (rows, piece) else whole(one) for one in shapes),
        scratch_shapes=[pltpu.VMEM((8, 128), F32), pltpu.VMEM(rabs[0].shape, F32)],
        compiler_params=pltpu.CompilerParams(vmem_limit_bytes=60 * 1024 * 1024),
        name="update",
    )(count, *operands)


def bias_line(rab):
    first = jnp.broadcast_to(rab[:, :1], (rab.shape[0], 64))
    final = jnp.broadcast_to(rab[:, NB - 1 :], (rab.shape[0], 65 - NB))
    return 0.5 * jnp.concatenate([first, final, rab[:, NB - 1 : 0 : -1]], axis=1)


def adamw_update(weight, first, second, grad, rate):
    first = BETA_ONE * first + (1.0 - BETA_ONE) * grad
    second = BETA_TWO * second + (1.0 - BETA_TWO) * grad * grad
    fixed_first = first / (1.0 - BETA_ONE**STEP)
    fixed_second = second / (1.0 - BETA_TWO**STEP)
    weight = weight - rate * (
        fixed_first / (jnp.sqrt(fixed_second) + EPS_ADAM) + WEIGHT_DECAY * weight
    )
    return (weight, first, second)


def exchange(values, axes, groups=None):
    return lax.all_to_all(
        values, axes, split_axis=0, concat_axis=0, tiled=True, axis_index_groups=groups
    )


def swap_sum(values, axis, count, stride, parts):
    mine = (lax.axis_index(axis) // stride) % parts

    def part(index):
        return lax.dynamic_index_in_dim(values, index, axis=0, keepdims=False)

    total = part(mine).astype(F32)
    for offset in range(1, parts):
        pairs = []
        for place in range(count):
            spot = (place // stride) % parts
            pairs.append((place, place + ((spot ^ offset) - spot) * stride))
        got = lax.ppermute(part(mine ^ offset).astype(BF), axis, pairs)
        total = total + got.astype(F32)
    return total


def swap_parts(sends, axis, count, stride):
    gots = []
    for offset, send in enumerate(sends, 1):
        pairs = []
        for place in range(count):
            spot = place // stride
            pairs.append((place, place + ((spot ^ offset) - spot) * stride))
        gots.append(lax.ppermute(send, axis, pairs))
    return gots


def fold_dense(keep, send, col_count, row_count, blocked, between):
    columns = keep.shape[1]
    half = row_count // 2
    own = keep.shape[0] // (col_count * half)
    got = lax.ppermute(send, "row", [(place, place ^ 1) for place in range(row_count)])
    if blocked:
        total, *sends = fold_call(lax.axis_index("col").reshape(1), keep, [got], col_count)
        gots = swap_parts(sends, "col", col_count, 1)
        gots[0] = between(gots[0])
        total, *sends = fold_call((lax.axis_index("row") // 2).reshape(1), total, gots, half)
        return total, swap_parts(sends, "row", row_count, 2)
    total = (keep.astype(F32) + got.astype(F32)).reshape(col_count, half * own, columns)
    total = swap_sum(total, "col", col_count, 1, col_count)
    return swap_sum(total.reshape(half, own, columns), "row", row_count, 2, half), []


def local(
    lengths,
    items,
    negatives,
    time_buckets,
    table,
    table_m,
    table_v,
    w_in,
    w_in_m,
    w_in_v,
    w_out,
    w_out_m,
    w_out_v,
    gains,
    gains_m,
    gains_v,
    rab,
    rab_m,
    rab_v,
):
    col_count = lax.axis_size("col")
    row_count = lax.axis_size("row")
    devices = col_count * row_count
    row_place = lax.axis_index("row")
    me = lax.axis_index("col") * row_count + row_place
    rows_dev, piece = table.shape
    own, width = w_out.shape
    slots, _, seq = items.shape
    per = seq // row_count
    neg_total = negatives.shape[0]
    neg_own = neg_total // row_count
    blocked = own % 16 == 0
    own_negs = (
        lax.dynamic_slice_in_dim(negatives, row_place * neg_own, neg_own) - row_place * rows_dev
    )
    neg_rows = table[own_negs].astype(BF)
    neg_rows = neg_rows.reshape(neg_own // own, own, piece).transpose(1, 0, 2)
    dense = lax.all_gather(
        jnp.concatenate(
            [
                w_in.astype(BF),
                w_out.astype(BF),
                neg_rows.reshape(own, -1),
                jnp.pad(gains.T, ((0, 0), (0, 128 - gains.shape[0]))).astype(BF),
            ],
            axis=1,
        ),
        BOTH,
        axis=0,
        tiled=True,
    )
    if not blocked:
        neg_rows = (
            dense[:, 5 * width : 6 * width]
            .reshape(col_count, row_count, own, neg_own // own, piece)
            .transpose(1, 3, 2, 0, 4)
            .reshape(neg_total, width)
        )
        dense = jnp.concatenate([dense[:, : 5 * width], neg_rows, dense[:, 6 * width :]], axis=1)
    bias = bias_line(rab)
    mine = items[:, 0]
    key, sorted_items, sorted_times = lax.sort(
        (mine // rows_dev * seq + jnp.arange(seq)[None, :], mine, time_buckets[:, 0]),
        dimension=1,
        num_keys=1,
    )
    block = key // seq
    about = jnp.stack([sorted_items - block * rows_dev, key - block * seq, sorted_times], axis=1)
    about = about.reshape(slots, 3, row_count, per).transpose(2, 0, 1, 3)
    about = jnp.pad(about, ((0, 0), (0, 0), (0, 0), (0, 128 - per))).reshape(row_count, -1, 128)
    told = jnp.concatenate(
        [
            about,
            jnp.broadcast_to(
                jnp.pad(lengths[:, 0], (0, 128 - slots))[None, None], (row_count, 1, 128)
            ),
        ],
        axis=1,
    )
    told = jnp.broadcast_to(told[None], (col_count,) + told.shape).reshape(devices, -1, 128)
    heard = exchange(told, BOTH)
    about = heard[:, : 3 * slots].reshape(devices * slots, 3, 128)
    ids = about[:, 0]
    every_length = heard[:, 3 * slots, :slots].reshape(-1)
    total = devices * slots
    number = jnp.arange(total)
    ahead = (every_length[None, :] > every_length[:, None]) | (
        (every_length[None, :] == every_length[:, None]) & (number[None, :] < number[:, None])
    )
    rank = jnp.sum(ahead.astype(jnp.int32), axis=1)
    wanted = jnp.stack(
        [
            slot * devices + (jnp.arange(devices) if slot % 2 == 0 else devices - 1 - jnp.arange(devices))
            for slot in range(slots)
        ]
    )
    hist = jnp.sum(
        jnp.where(rank[None, None, :] == wanted[:, :, None], number[None, None, :], 0), axis=2
    )
    my_length = jnp.sum(
        jnp.where(
            rank[None, :] == lax.dynamic_slice_in_dim(wanted, me, 1, axis=1),
            every_length[None, :],
            0,
        ),
        axis=1,
    )
    sent = []
    for slot in range(slots):
        found = lookup_call(hist[slot], ids, about, table, per)
        sent.append(exchange(found, BOTH).reshape(col_count, row_count, per + 16, piece))
    core = (row_place % 2).reshape(1)
    first = history_call(my_length[0:1], sent[0], dense, bias, core, None, blocked)
    back = [exchange(first[0].reshape(devices, per, piece), BOTH)]
    final = history_call(my_length[1:2], sent[1], dense, bias, core, first[1:], blocked)
    final_rows, back[0] = lax.optimization_barrier((final[0], back[0]))
    back.append(exchange(final_rows.reshape(devices, per, piece), BOTH))
    grad_misc, keep, send = final[1:]
    if not blocked:
        packed = jnp.concatenate([keep, send], axis=0)
        neg_part = (
            packed[:, 5 * width : 6 * width]
            .reshape(row_count, neg_own // own, own, col_count, piece)
            .transpose(3, 0, 2, 1, 4)
            .reshape(width, width)
        )
        packed = jnp.concatenate(
            [packed[:, : 5 * width], neg_part, packed[:, 6 * width :]], axis=1
        ).reshape(devices // 2, 2, own, -1)
        keep = lax.dynamic_index_in_dim(packed, core[0], axis=1, keepdims=False)
        send = lax.dynamic_index_in_dim(packed, 1 - core[0], axis=1, keepdims=False)
        keep = keep.reshape(width // 2, -1)
        send = send.reshape(width // 2, -1)
    loss_count = jnp.sum(jnp.maximum(every_length - 1, 0)).reshape(1)
    table_part = scatter_call(hist[0], ids, back[0].reshape(devices * per, piece), rows_dev, per)
    base, gots = fold_dense(
        keep,
        send,
        col_count,
        row_count,
        blocked,
        lambda value: lax.optimization_barrier((value, table_part))[0],
    )
    table_sum = scatter_call(
        hist[1], ids, back[1].reshape(devices * per, piece), rows_dev, per, table_part
    )
    table_sum, shard, gain_grad, told = gather_up_call(
        own_negs, table_sum, grad_misc, base, gots, devices
    )
    heard = exchange(told, BOTH)
    scalars, *updated = update_call(
        loss_count,
        heard,
        shard,
        table_sum,
        (table, table_m, table_v),
        (w_in, w_in_m, w_in_v),
        (w_out, w_out_m, w_out_v),
        gain_grad,
        (gains, gains_m, gains_v),
        (rab, rab_m, rab_v),
    )
    return (scalars[0, 0], scalars[1, 0], scalars[2, 0], *updated)


def solution(mesh):
    placed = (
        P(None, ("col", "row")),
        P(None, ("col", "row"), None),
        P(),
        P(None, ("col", "row"), None),
        P("row", "col"),
        P("row", "col"),
        P("row", "col"),
        P(("col", "row"), None),
        P(("col", "row"), None),
        P(("col", "row"), None),
        P(("col", "row"), None),
        P(("col", "row"), None),
        P(("col", "row"), None),
        P(None, ("col", "row")),
        P(None, ("col", "row")),
        P(None, ("col", "row")),
        P(),
        P(),
        P(),
    )
    return jax.shard_map(
        local,
        mesh=mesh,
        in_specs=placed,
        out_specs=(
            P(),
            P(),
            P(),
            P("row", "col"),
            P("row", "col"),
            P("row", "col"),
            P("row", "col"),
            P(("col", "row"), None),
            P(("col", "row"), None),
            P(("col", "row"), None),
            P(("col", "row"), None),
            P(("col", "row"), None),
            P(("col", "row"), None),
            P(("col", "row"), None),
            P(("col", "row"), None),
            P(None, ("col", "row")),
            P(None, ("col", "row")),
            P(None, ("col", "row")),
            P(),
            P(),
            P(),
        ),
        check_vma=False,
    )
```

time: 432 us -> 317 us (0.73)
  blocking collectives: 90.9 us -> 10.8 us
  other arithmetic: 40.5 us -> 8.98 us
  local copies, waits for them, and re-layouts: 37.5 us -> 15.2 us
  Pallas kernels: 121 us -> 141 us
  starting transfers between devices: 41.2 us -> 55.7 us
  between operations: 26.2 us -> 15.8 us
    all_to_all x3 -> x1, blocking collectives: 54.3 us -> 10.8 us  [exchange(): lax.all_to_all(values, axes, split_axis=0, concat_axis=0, tiled=True, axi...]
    all_gather x2 -> x0, blocking collectives: 36.6 us -> none  [the longest x1 26.1 us: local(): about = lax.all_gather(about, 'row', axis=0, tiled=True)]
    all_to_all x7 -> x5, waiting for transfers between devices: 72.4 us -> 51.6 us  [exchange(): lax.all_to_all(values, axes, split_axis=0, concat_axis=0, tiled=True, axi...]
    pallas_call x7 -> x10, Pallas kernels: 121 us -> 141 us  [the longest x2 92.8 us: history_call(): pl.pallas_call(functools.partial(history_kernel, last, blocked), out_shap...]
    ppermute x0 -> x7, waiting for transfers between devices: none -> 16.5 us  [the longest x6 16.5 us: swap_parts(): gots.append(lax.ppermute(send, axis, pairs))]
    gather x2 -> x1, local copies, waits for them, and re-layouts: 16.2 us -> 2.03 us  [local(): neg_rows = table[own_negs].astype(BF)]
    reduce_sum x13 -> x1, other arithmetic: 10.6 us -> 0.18 us  [local(): jnp.sum(jnp.where(rank[None, :] == lax.dynamic_slice_in_dim(wanted, me, 1...]
    convert_element_type x4 -> x0, other arithmetic: 9.47 us -> none  [the longest x1 5.28 us: local(): table_new.astype(BF)]
  transfers between devices with their start and end apart: 8 -> 13, of which waited for: 6 -> 6; matrix products, arithmetic and copies ran while one was open for 9% -> 3% of each run, Pallas kernels for 9% -> 41%
where the time goes in v2:
time: 317 us; the launch traced here: 316 us
  Pallas kernels  141 us (44%)
  waiting for transfers between devices  68.2 us (22%)
  starting transfers between devices  55.7 us (18%)
  between operations  15.8 us (5%)
  local copies, waits for them, and re-layouts  15.2 us (5%)
  blocking collectives  10.8 us (3%)
  other arithmetic  8.98 us (3%)
    pallas_call x2, Pallas kernels, history_call(): pl.pallas_call(functools.partial(history_kernel, last, blocked), out_shap...  92.8 us
    all_to_all x5, waiting for transfers between devices, exchange(): lax.all_to_all(values, axes, split_axis=0, concat_axis=0, tiled=True, axi...  51.6 us
    all_to_all x5, starting transfers between devices, exchange(): lax.all_to_all(values, axes, split_axis=0, concat_axis=0, tiled=True, axi...  47.5 us
    pallas_call x2, Pallas kernels, scatter_call(): pl.pallas_call(scatter_kernel, out_shape=jax.ShapeDtypeStruct((rows, piec...  17.7 us
    ppermute x6, waiting for transfers between devices, swap_parts(): gots.append(lax.ppermute(send, axis, pairs))  16.5 us
    pallas_call x2, Pallas kernels, lookup_call(): pl.pallas_call(lookup_kernel, out_shape=jax.ShapeDtypeStruct((count, per...  12.9 us
    all_to_all x1, blocking collectives, exchange(): lax.all_to_all(values, axes, split_axis=0, concat_axis=0, tiled=True, axi...  10.8 us
    pallas_call x1, Pallas kernels, update_call(): pl.pallas_call(functools.partial(update_kernel, shard.shape[1] // 6 // 12...  8.69 us
  transfers between devices with their start and end apart: 13, of which 6 were waited for; matrix products, arithmetic and copies ran while one was open for 3% of the time, Pallas kernels for 41%

profile of v2, /device:TPU:0, one launch (start us, length us, event | category | flops | bytes accessed | tf_op | source)
XLA Modules:
  0.0 315.5 jit_solution(8822671162717077873)
XLA Ops:
  12.9 2.0 gather_fusion
  22.0 7.3 %all-to-all-start = ((s32[32,7,128]{2,1,0:T(8,128)}), s32[32,7,128]{2,1,0:T(8,128)S(1)}, u32[]{:S(2)}, u32[]{:S(2)}) async-start(s32[32,7,128]{2,1,0:T(8,128)} %bitcast.3), calls=%async_computation | async-start | bytes 262144 | tf_op jit(solution)/shard_map/all_to_all | solution.py:840
  29.3 8.4 %all-to-all-done = s32[32,7,128]{2,1,0:T(8,128)S(1)} async-done(((s32[32,7,128]{2,1,0:T(8,128)}), s32[32,7,128]{2,1,0:T(8,128)S(1)}, u32[]{:S(2)}, u32[]{:S(2)}) %all-to-all-start) | async-done | bytes 114720 | tf_op jit(solution)/shard_map/all_to_all | solution.py:840
  40.2 6.4 %lookup.3 = bf16[32,144,128]{2,1,0:T(8,128)(2,1)} custom-call(s32[32]{0:T(128)} %get-tuple-element.124.hist_ref, s32[64,128]{1,0:T(8,128)} %bitcast.67, s32[64,3,128]{2,1,0:T(4,128)} %copy-done.8, f32[3200,128]{1,0:T(8,128)} %table_ref.5), custom_call_target="tpu_custom_call" | custom-call | flops 5000000000 | bytes 4000000 | tf_op jit(solution)/shard_map/lookup/pallas_call | solution.py:529
  46.6 2.8 all-to-all-start.2
  51.5 6.4 %lookup.2 = bf16[32,144,128]{2,1,0:T(8,128)(2,1)} custom-call(s32[32]{0:T(128)} %get-tuple-element.125.hist_ref, s32[64,128]{1,0:T(8,128)} %bitcast.68, s32[64,3,128]{2,1,0:T(4,128)} %copy-done.8, f32[3200,128]{1,0:T(8,128)} %table_ref.5), custom_call_target="tpu_custom_call" | custom-call | flops 5000000000 | bytes 4000000 | tf_op jit(solution)/shard_map/lookup/pallas_call | solution.py:529
  57.9 33.1 %all-to-all-done.2 = bf16[32,144,128]{2,1,0:T(8,128)(2,1)S(1)} async-done(((bf16[32,144,128]{2,1,0:T(8,128)(2,1)}), bf16[32,144,128]{2,1,0:T(8,128)(2,1)S(1)}, u32[]{:S(2)}, u32[]{:S(2)}) %all-to-all-start.2) | async-done | bytes 1179680 | tf_op jit(solution)/shard_map/all_to_all | solution.py:840
  91.0 2.7 all-to-all-start.1
  93.7 75.6 %history_first.1 = (bf16[4,8,128,128]{3,2,1,0:T(8,128)(2,1)}, f32[16,512]{1,0:T(8,128)}, f32[512,2048]{1,0:T(8,128)}, f32[512,512]{1,0:T(8,128)}, f32[512,512]{1,0:T(8,128)}) custom-call(s32[1]{0:T(128)} %get-tuple-element.126.refs_0_, bf16[4,8,144,128]{3,2,1,0:T(8,128)(2,1)} %bitcast.56, bf16[512,3200]{1,0:T(8,128)(2,1)} %all-gather.2.cloned.1.call-done.refs_2_.refs_3_, ...), custom_call_target="tpu_custom_call" | custom-call | flops 40000000000 | bytes 20000000 | tf_op jit(solution)/shard_map/history_first/pallas_call | solution.py:467
  169.3 4.9 %all-to-all-start.3 = ((bf16[32,128,128]{2,1,0:T(8,128)(2,1)}), bf16[32,128,128]{2,1,0:T(8,128)(2,1)S(1)}, u32[]{:S(2)}, u32[]{:S(2)}) async-start(bf16[32,128,128]{2,1,0:T(8,128)(2,1)} %bitcast.61), calls=%async_computation.3 | async-start | bytes 2097152 | tf_op jit(solution)/shard_map/all_to_all | solution.py:840
  174.2 17.2 %history_last.1 = (bf16[4,8,128,128]{3,2,1,0:T(8,128)(2,1)}, f32[16,512]{1,0:T(8,128)}, bf16[256,3200]{1,0:T(8,128)(2,1)}, bf16[256,3200]{1,0:T(8,128)(2,1)}) custom-call(s32[1]{0:T(128)} %get-tuple-element.127.refs_0_, s32[1]{0:T(128)} %bitcast.7.refs_1_, bf16[4,8,144,128]{3,2,1,0:T(8,128)(2,1)} %bitcast.57, ...), custom_call_target="tpu_custom_call" | custom-call | flops 40000000000 | bytes 20000000 | tf_op jit(solution)/shard_map/history_last/pallas_call | solution.py:467
  191.7 10.1 %all-to-all-done.3 = bf16[32,128,128]{2,1,0:T(8,128)(2,1)S(1)} async-done(((bf16[32,128,128]{2,1,0:T(8,128)(2,1)}), bf16[32,128,128]{2,1,0:T(8,128)(2,1)S(1)}, u32[]{:S(2)}, u32[]{:S(2)}) %all-to-all-start.3) | async-done | bytes 1048608 | tf_op jit(solution)/shard_map/all_to_all | solution.py:840
  202.8 29.8 %all-to-all-start.4 = ((bf16[32,128,128]{2,1,0:T(8,128)(2,1)}), bf16[32,128,128]{2,1,0:T(8,128)(2,1)S(1)}, u32[]{:S(2)}, u32[]{:S(2)}) async-start(bf16[32,128,128]{2,1,0:T(8,128)(2,1)} %bitcast.58), calls=%async_computation.4 | async-start | bytes 2097152 | tf_op jit(solution)/shard_map/all_to_all | solution.py:840
  233.8 3.3 %fold.2 = (f32[64,3200]{1,0:T(8,128)}, bf16[64,3200]{1,0:T(8,128)(2,1)}, bf16[64,3200]{1,0:T(8,128)(2,1)}, bf16[64,3200]{1,0:T(8,128)(2,1)}) custom-call(s32[1]{0:T(128)} %bitcast.19.place_ref, bf16[256,3200]{1,0:T(8,128)(2,1)} %get-tuple-element.79.base_ref, bf16[256,3200]{1,0:T(8,128)(2,1)} %copy-done), custom_call_target="tpu_custom_call" | custom-call | tf_op jit(solution)/shard_map/fold/pallas_call | solution.py:666
  237.2 1.6 collective-permute-start.1
  240.7 8.6 %scatter.2.refs_0_ = f32[3200,128]{1,0:T(8,128)} custom-call(s32[32]{0:T(128)} %get-tuple-element.124.hist_ref, s32[64,128]{1,0:T(8,128)} %bitcast.69, bf16[4096,128]{1,0:T(8,128)(2,1)} %bitcast.60), custom_call_target="tpu_custom_call" | custom-call | flops 6000000000 | bytes 4000000 | tf_op jit(solution)/shard_map/scatter/pallas_call | solution.py:576
  249.2 5.1 %collective-permute-done.1.refs_0_ = bf16[64,3200]{1,0:T(8,128)(2,1)S(1)} collective-permute-done((bf16[64,3200]{1,0:T(8,128)(2,1)}, bf16[64,3200]{1,0:T(8,128)(2,1)S(1)}, u32[]{:S(2)}, u32[]{:S(2)}) %collective-permute-start.1) | collective-permute-done | bytes 409632 | tf_op jit(solution)/shard_map/ppermute | solution.py:869
  255.4 10.4 %collective-permute-done.3.refs_2_ = bf16[64,3200]{1,0:T(8,128)(2,1)S(1)} collective-permute-done((bf16[64,3200]{1,0:T(8,128)(2,1)}, bf16[64,3200]{1,0:T(8,128)(2,1)S(1)}, u32[]{:S(2)}, u32[]{:S(2)}) %collective-permute-start.3) | collective-permute-done | bytes 409632 | tf_op jit(solution)/shard_map/ppermute | solution.py:869
  266.5 2.3 fold.3
  269.7 2.6 collective-permute-start.5
  274.2 9.2 %scatter.3.table_ref = f32[3200,128]{1,0:T(8,128)} custom-call(s32[32]{0:T(128)} %get-tuple-element.125.hist_ref, s32[64,128]{1,0:T(8,128)} %bitcast.70, bf16[4096,128]{1,0:T(8,128)(2,1)} %bitcast.59, f32[3200,128]{1,0:T(8,128)} %scatter.2.refs_0_), custom_call_target="tpu_custom_call" | custom-call | flops 6000000000 | bytes 4000000 | tf_op jit(solution)/shard_map/scatter/pallas_call | solution.py:576
  284.1 3.2 %gather_up.1 = (f32[3200,128]{1,0:T(8,128)}, f32[16,3200]{1,0:T(8,128)}, f32[8,128]{1,0:T(8,128)}, f32[32,4,128]{2,1,0:T(4,128)}) custom-call(s32[64]{0:T(128)} %get-tuple-element.118.spots_ref, f32[3200,128]{1,0:T(8,128)} %scatter.3.table_ref, f32[16,512]{1,0:T(8,128)} %get-tuple-element.78.misc_ref, f32[16,3200]{1,0:T(8,128)} %get-tuple-element.86.base_ref, ...), custom_call_target="tpu_custom_call" | custom-call | tf_op jit(solution)/shard_map/gather_up/pallas_call | solution.py:630
  287.2 10.8 %all_to_all.30.heard_ref = f32[32,4,128]{2,1,0:T(4,128)} all-to-all(f32[32,4,128]{2,1,0:T(4,128)} %get-tuple-element.90), channel_id=1, replica_groups=mesh['col'=4,'row'=8] {'col','row'}, dimensions={0} | all-to-all | bytes 131072 | tf_op jit(solution)/shard_map/all_to_all | solution.py:840
  298.1 8.7 %update.1 = (f32[8,128]{1,0:T(8,128)}, f32[3200,128]{1,0:T(8,128)}, f32[3200,128]{1,0:T(8,128)}, f32[3200,128]{1,0:T(8,128)}, bf16[3200,128]{1,0:T(8,128)(2,1)},...) custom-call(s32[1]{0:T(128)} %bitcast.4.count_ref, ...), custom_call_target="tpu_custom_call" | custom-call | tf_op jit(solution)/shard_map/update/pallas_call | solution.py:810
  (86 shorter events, 27.3 us)
Async XLA Ops:
  8.0 11.1 %sort.23.cloned.1.call-start = ((), (), s32[]{:S(2)}) async-start(), calls=%async_computation.7 | async-start | bytes 73760 | tf_op jit(solution)/shard_map/sort | solution.py:951
  10.7 83.0 %all-gather.2.cloned.1.call-start = ((), (), s32[]{:S(2)}) async-start(), calls=%async_computation.6 | async-start | bytes 3379200 | tf_op jit(solution)/shard_map/all_gather | solution.py:927
  22.0 15.8 %all-to-all-start = ((s32[32,7,128]{2,1,0:T(8,128)}), s32[32,7,128]{2,1,0:T(8,128)S(1)}, u32[]{:S(2)}, u32[]{:S(2)}) async-start(s32[32,7,128]{2,1,0:T(8,128)} %bitcast.3), calls=%async_computation | async-start | bytes 262144 | tf_op jit(solution)/shard_map/all_to_all | solution.py:840
  38.6 1.6 copy-start.8
  46.6 3.0 copy-start.12
  46.6 44.4 %all-to-all-start.2 = ((bf16[32,144,128]{2,1,0:T(8,128)(2,1)}), bf16[32,144,128]{2,1,0:T(8,128)(2,1)S(1)}, u32[]{:S(2)}, u32[]{:S(2)}) async-start(bf16[32,144,128]{2,1,0:T(8,128)(2,1)} %lookup.3), calls=%async_computation.2 | async-start | bytes 2359296 | tf_op jit(solution)/shard_map/all_to_all | solution.py:840
  91.0 2.7 copy-start.1
  91.0 78.3 %all-to-all-start.1 = ((bf16[32,144,128]{2,1,0:T(8,128)(2,1)}), bf16[32,144,128]{2,1,0:T(8,128)(2,1)S(1)}, u32[]{:S(2)}, u32[]{:S(2)}) async-start(bf16[32,144,128]{2,1,0:T(8,128)(2,1)} %lookup.2), calls=%async_computation.1 | async-start | bytes 2359296 | tf_op jit(solution)/shard_map/all_to_all | solution.py:840
  169.3 4.9 %copy-start.2 = (bf16[32,144,128]{2,1,0:T(8,128)(2,1)}, bf16[32,144,128]{2,1,0:T(8,128)(2,1)S(1)}, u32[]{:S(2)}) copy-start(bf16[32,144,128]{2,1,0:T(8,128)(2,1)S(1)} %all-to-all-done.1) | copy-start | bytes 3538948
  169.3 32.5 %all-to-all-start.3 = ((bf16[32,128,128]{2,1,0:T(8,128)(2,1)}), bf16[32,128,128]{2,1,0:T(8,128)(2,1)S(1)}, u32[]{:S(2)}, u32[]{:S(2)}) async-start(bf16[32,128,128]{2,1,0:T(8,128)(2,1)} %bitcast.61), calls=%async_computation.3 | async-start | bytes 2097152 | tf_op jit(solution)/shard_map/all_to_all | solution.py:840
  191.4 41.2 %collective-permute-start = (bf16[256,3200]{1,0:T(8,128)(2,1)}, bf16[256,3200]{1,0:T(8,128)(2,1)S(1)}, u32[]{:S(2)}, u32[]{:S(2)}) collective-permute-start(bf16[256,3200]{1,0:T(8,128)(2,1)} %get-tuple-element.80), channel_id=1, source_target_pairs={{0,1},{1,0},{2,3},{3,2},{4,5},{5,4},{6,7},{7,6},{8,9},{9,8},{10,11... | collective-permute-start | bytes 4915208 | tf_op jit(solution)/shard_map/ppermute | solution.py:877
  201.8 1.0 copy-start.4
  202.8 70.5 %all-to-all-start.4 = ((bf16[32,128,128]{2,1,0:T(8,128)(2,1)}), bf16[32,128,128]{2,1,0:T(8,128)(2,1)S(1)}, u32[]{:S(2)}, u32[]{:S(2)}) async-start(bf16[32,128,128]{2,1,0:T(8,128)(2,1)} %bitcast.58), calls=%async_computation.4 | async-start | bytes 2097152 | tf_op jit(solution)/shard_map/all_to_all | solution.py:840
  232.7 1.2 copy-start
  237.2 17.1 %collective-permute-start.1 = (bf16[64,3200]{1,0:T(8,128)(2,1)}, bf16[64,3200]{1,0:T(8,128)(2,1)S(1)}, u32[]{:S(2)}, u32[]{:S(2)}) collective-permute-start(bf16[64,3200]{1,0:T(8,128)(2,1)} %get-tuple-element.82), channel_id=1, source_target_pairs={{0,8},{8,0},{16,24},{24,16},{1,9},{9,1},{17,25},{25,17},{2,10},{10... | collective-permute-start | bytes 1228808 | tf_op jit(solution)/shard_map/ppermute | solution.py:869
  238.7 16.6 %collective-permute-start.2 = (bf16[64,3200]{1,0:T(8,128)(2,1)}, bf16[64,3200]{1,0:T(8,128)(2,1)S(1)}, u32[]{:S(2)}, u32[]{:S(2)}) collective-permute-start(bf16[64,3200]{1,0:T(8,128)(2,1)} %get-tuple-element.84), channel_id=1, source_target_pairs={{0,16},{8,24},{16,0},{24,8},{1,17},{9,25},{17,1},{25,9},{2,18},{10... | collective-permute-start | bytes 1228808 | tf_op jit(solution)/shard_map/ppermute | solution.py:869
  240.2 25.6 %collective-permute-start.3 = (bf16[64,3200]{1,0:T(8,128)(2,1)}, bf16[64,3200]{1,0:T(8,128)(2,1)S(1)}, u32[]{:S(2)}, u32[]{:S(2)}) collective-permute-start(bf16[64,3200]{1,0:T(8,128)(2,1)} %get-tuple-element.85), channel_id=1, source_target_pairs={{0,24},{8,16},{16,8},{24,0},{1,25},{9,17},{17,9},{25,1},{2,26},{10... | collective-permute-start | bytes 1228808 | tf_op jit(solution)/shard_map/ppermute | solution.py:869
  254.3 11.4 %copy-start.5 = (bf16[64,3200]{1,0:T(8,128)(2,1)}, bf16[64,3200]{1,0:T(8,128)(2,1)S(1)}, u32[]{:S(2)}) copy-start(bf16[64,3200]{1,0:T(8,128)(2,1)S(1)} %collective-permute-done.1.refs_0_) | copy-start | bytes 1228804
  255.4 10.4 %copy-start.6 = (bf16[64,3200]{1,0:T(8,128)(2,1)}, bf16[64,3200]{1,0:T(8,128)(2,1)S(1)}, u32[]{:S(2)}) copy-start(bf16[64,3200]{1,0:T(8,128)(2,1)S(1)} %collective-permute-done.2.refs_1_) | copy-start | bytes 1228804
  265.7 0.8 copy-start.7
  268.9 14.5 %collective-permute-start.4 = (bf16[16,3200]{1,0:T(8,128)(2,1)}, bf16[16,3200]{1,0:T(8,128)(2,1)S(1)}, u32[]{:S(2)}, u32[]{:S(2)}) collective-permute-start(bf16[16,3200]{1,0:T(8,128)(2,1)} %get-tuple-element.87), channel_id=1, source_target_pairs={{0,2},{1,3},{2,0},{3,1},{4,6},{5,7},{6,4},{7,5},{8,10},{9,11},{10,... | collective-permute-start | bytes 307208 | tf_op jit(solution)/shard_map/ppermute | solution.py:869
  269.7 13.7 %collective-permute-start.5 = (bf16[16,3200]{1,0:T(8,128)(2,1)}, bf16[16,3200]{1,0:T(8,128)(2,1)S(1)}, u32[]{:S(2)}, u32[]{:S(2)}) collective-permute-start(bf16[16,3200]{1,0:T(8,128)(2,1)} %get-tuple-element.88), channel_id=1, source_target_pairs={{0,4},{1,5},{2,6},{3,7},{4,0},{5,1},{6,2},{7,3},{8,12},{9,13},{10,... | collective-permute-start | bytes 307208 | tf_op jit(solution)/shard_map/ppermute | solution.py:869
  272.3 11.1 %collective-permute-start.6 = (bf16[16,3200]{1,0:T(8,128)(2,1)}, bf16[16,3200]{1,0:T(8,128)(2,1)S(1)}, u32[]{:S(2)}, u32[]{:S(2)}) collective-permute-start(bf16[16,3200]{1,0:T(8,128)(2,1)} %get-tuple-element.89), channel_id=1, source_target_pairs={{0,6},{1,7},{2,4},{3,5},{4,2},{5,3},{6,0},{7,1},{8,14},{9,15},{10,... | collective-permute-start | bytes 307208 | tf_op jit(solution)/shard_map/ppermute | solution.py:869
  273.2 1.0 copy-start.3
  (3 other events, 2.0 us)
Sparse Core Ops, SparseCore 0:
  12.0 6.9 sort.25.cloned.1.call-done
  (1 shorter events, 0.0 us)
Sparse Core Ops, SparseCore 1:
  17.3 71.1 all-gather.1

commit v3 on v2

--- a/solution.py
+++ b/solution.py
@@ -19,6 +19,7 @@
 RATE_SMALL = 0.5
 BOTH = ("col", "row")
 TILE = 256
+WIDE = 4
 BF = jnp.bfloat16
 F32 = jnp.float32
 
@@ -53,14 +54,15 @@
 
 def history_kernel(last, blocked, *refs):
     if last:
-        (len_ref, core_ref, recv_ref, dense_ref, bias_ref, misc0_ref, big0_ref, small0_ref, gneg0_ref) = refs[:9]
-        (ge_ref, misc_ref, keep_ref, send_ref) = refs[9:13]
-        (big_ref, small_ref, gneg_ref, load_sem) = refs[13:17]
-        scratch = refs[17:]
+        (len_ref, spot_ref, recv_ref, same_ref, other_ref, bias_ref) = refs[:6]
+        (misc0_ref, big0_ref, small0_ref, gneg0_ref) = refs[6:10]
+        (ge_ref, misc_ref, keep_ref, send_ref) = refs[10:14]
+        (big_ref, small_ref, gneg_ref, load_sem) = refs[14:18]
+        scratch = refs[18:]
     else:
-        (len_ref, recv_ref, dense_ref, bias_ref) = refs[:4]
-        (ge_ref, misc_ref, big_ref, small_ref, gneg_ref) = refs[4:9]
-        scratch = refs[9:]
+        (len_ref, spot_ref, recv_ref, same_ref, other_ref, bias_ref) = refs[:6]
+        (ge_ref, misc_ref, big_ref, small_ref, gneg_ref) = refs[6:11]
+        scratch = refs[11:]
     (
         rows_s,
         event_s,
@@ -86,6 +88,8 @@
         gains_s,
         negs_s,
         bias_s,
+        dense_ref,
+        dense_sem,
     ) = scratch
     pieces, blocks, tall, piece = recv_ref.shape
     per = tall - 16
@@ -98,6 +102,24 @@
     tiles = lax.div(length + (TILE - 1), TILE)
     lane = lax.broadcasted_iota(jnp.int32, (TILE, 128), 1)
     low_lanes = lane < 64
+    pulls = []
+    if blocked:
+        for index in range(devices // 2):
+            far_col, far_z = index // (blocks // 2), index % (blocks // 2)
+            base = lax.bitwise_xor(spot_ref[0], far_col) * blocks
+            base = base + lax.bitwise_xor(spot_ref[1], far_z) * 2
+            for which, source in enumerate((same_ref, other_ref)):
+                core = spot_ref[2] if which == 0 else 1 - spot_ref[2]
+                target = pl.ds(pl.multiple_of((base + core) * own, own), own)
+                pulls.append(
+                    pltpu.make_async_copy(
+                        source.at[index], dense_ref.at[target, :], dense_sem.at[2 * index + which]
+                    )
+                )
+    else:
+        pulls.append(pltpu.make_async_copy(same_ref, dense_ref, dense_sem.at[0]))
+    for one in pulls:
+        one.start()
     if last:
         loads = [
             pltpu.make_async_copy(big0_ref, big_ref, load_sem.at[0]),
@@ -123,6 +145,8 @@
         order_s[0:1, span] = spot.astype(jnp.int32)
         orderc_s[span, :] = jnp.broadcast_to(about[0:1, :] * 32.0 + about[1:2, :], (128, 128)).T[0:per, :].astype(jnp.int32)
         rows_s[span, width : width + 128] = jnp.broadcast_to(about[2:3, :], (128, 128)).T[0:per, :].astype(BF)
+    for one in pulls:
+        one.wait()
     if blocked:
         for one in range(pieces):
             for block in range(blocks):
@@ -207,35 +231,42 @@
     square_row = lax.broadcasted_iota(jnp.int32, (TILE, TILE), 0)
     square_col = lax.broadcasted_iota(jnp.int32, (TILE, TILE), 1)
 
-    def attend_group(group, _):
-        def attend_tile(step, _):
-            span = place(step)
-
-            def attend(other, masked):
-                near = place(other)
-                total = None
-                for half in range(2):
-                    scores = dot_nt(query_s[2 * group + half, span, :], keys_s[group, near, :])
-                    weight = scores + scores * jnp.tanh(scores)
+    def attend_tile(step, _):
+        span = place(step)
+
+        def attend(other, masked):
+            near = place(other)
+
+            def attend_heads(base, _):
+                for extra in range(WIDE):
+                    group = base * WIDE + extra
+                    total = None
+                    for half in range(2):
+                        head = 2 * group + half
+                        scores = dot_nt(query_s[head, span, :], keys_s[group, near, :])
+                        weight = scores + scores * jnp.tanh(scores)
+                        if masked:
+                            weight = jnp.where(square_col <= square_row, weight, 0.0)
+                        part = dot_nn(weight.astype(BF), valuem_s[head, near, :])
+                        total = part if total is None else total + part
                     if masked:
-                        weight = jnp.where(square_col <= square_row, weight, 0.0)
-                    part = dot_nn(weight.astype(BF), valuem_s[2 * group + half, near, :])
-                    total = part if total is None else total + part
-                return total
-
-            out_s[group, span, :] = attend(step, True)
-
-            def before(other, _):
-                out_s[group, span, :] += attend(other, False)
+                        out_s[group, span, :] = total
+                    else:
+                        out_s[group, span, :] += total
                 return 0
 
-            lax.fori_loop(0, step, before, 0)
+            lax.fori_loop(0, groups // WIDE, attend_heads, 0)
+
+        attend(step, True)
+
+        def before(other, _):
+            attend(other, False)
             return 0
 
-        lax.fori_loop(0, tiles, attend_tile, 0)
+        lax.fori_loop(0, step, before, 0)
         return 0
 
-    lax.fori_loop(0, groups, attend_group, 0)
+    lax.fori_loop(0, tiles, attend_tile, 0)
 
     if last:
         for one in loads:
@@ -298,50 +329,53 @@
 
     lax.fori_loop(0, tiles, middle, 0)
 
-    def retreat_group(group, _):
-        def retreat_tile(step, _):
-            near = place(step)
-
-            def retreat(other, masked):
-                span = place(other)
-                keys = keys_s[group, near, :]
-                total = None
-                for half in range(2):
-                    head = 2 * group + half
-                    gout = gout_s[head, span, :]
-                    query = query_s[head, span, :]
-                    scores = dot_nt(keys, query)
-                    grads = dot_nt(valuem_s[head, near, :], gout)
-                    bent = 1.0 + jnp.tanh(scores)
-                    weight = scores * bent
-                    slope = bent * ((1.0 + (scores + scores)) - weight)
-                    grads = grads * slope
-                    if masked:
-                        visible = square_row <= square_col
-                        weight = jnp.where(visible, weight, 0.0)
-                        grads = jnp.where(visible, grads, 0.0)
-                    grads = grads.astype(BF)
-                    part = dot_nn(weight.astype(BF), gout)
-                    total = part if total is None else total + part
-                    dkeys_s[head, near, :] += dot_nn(
-                        grads, jnp.concatenate([query[:, 0:128], hot_s[span, :]], axis=1)
-                    )
-                    dqueryt_s[head, :, span] += dot_nn(keyst_s[head, :, near], grads)
-                out_s[group, near, :] += total
-
-            retreat(step, True)
-
-            def after(other, _):
-                retreat(other, False)
+    def retreat_tile(step, _):
+        near = place(step)
+
+        def retreat(other, masked):
+            span = place(other)
+
+            def retreat_heads(base, _):
+                for extra in range(WIDE):
+                    group = base * WIDE + extra
+                    keys = keys_s[group, near, :]
+                    total = None
+                    for half in range(2):
+                        head = 2 * group + half
+                        gout = gout_s[head, span, :]
+                        query = query_s[head, span, :]
+                        scores = dot_nt(keys, query)
+                        grads = dot_nt(valuem_s[head, near, :], gout)
+                        bent = 1.0 + jnp.tanh(scores)
+                        weight = scores * bent
+                        slope = bent * ((1.0 + (scores + scores)) - weight)
+                        grads = grads * slope
+                        if masked:
+                            visible = square_row <= square_col
+                            weight = jnp.where(visible, weight, 0.0)
+                            grads = jnp.where(visible, grads, 0.0)
+                        grads = grads.astype(BF)
+                        part = dot_nn(weight.astype(BF), gout)
+                        total = part if total is None else total + part
+                        dkeys_s[head, near, :] += dot_nn(
+                            grads, jnp.concatenate([query[:, 0:128], hot_s[span, :]], axis=1)
+                        )
+                        dqueryt_s[head, :, span] += dot_nn(keyst_s[head, :, near], grads)
+                    out_s[group, near, :] += total
                 return 0
 
-            lax.fori_loop(step + 1, tiles, after, 0)
+            lax.fori_loop(0, groups // WIDE, retreat_heads, 0)
+
+        retreat(step, True)
+
+        def after(other, _):
+            retreat(other, False)
             return 0
 
-        lax.fori_loop(0, tiles, retreat_tile, 0)
+        lax.fori_loop(step + 1, tiles, after, 0)
         return 0
 
-    lax.fori_loop(0, groups, retreat_group, 0)
+    lax.fori_loop(0, tiles, retreat_tile, 0)
 
     def finish(step, _):
         span = place(step)
@@ -423,7 +457,7 @@
         if blocked:
             for core in range(2):
 
-                @pl.when(core_ref[0] == core)
+                @pl.when(spot_ref[2] == core)
                 def _(core=core):
                     for device in range(devices):
                         one, block = device // blocks, device % blocks
@@ -437,7 +471,7 @@
             pack(send_ref, slice(0, half), slice(half, width), 0, 0)
 
 
-def history_call(length, recv, dense, bias, core, before, blocked):
+def history_call(length, spot, recv, same, other, bias, before, blocked):
     last = before is not None
     pieces, blocks, tall, piece = recv.shape
     per = tall - 16
@@ -454,14 +488,14 @@
         jax.ShapeDtypeStruct((16, width), F32),
     ]
     sums = [(width, 4 * width), (width, width), (neg_total, width)]
+    operands = (length, spot, recv, same, other, bias)
+    specs = [smem, smem, vmem, anywhere, anywhere, vmem]
     if last:
-        operands = (length, core, recv, dense, bias, *before)
-        specs = [smem, smem, vmem, vmem, vmem, vmem, anywhere, anywhere, anywhere]
+        operands += tuple(before)
+        specs += [vmem, anywhere, anywhere, anywhere]
         shapes += [jax.ShapeDtypeStruct((width // 2, 6 * width + 128), BF)] * 2
         extra = [pltpu.VMEM(one, F32) for one in sums] + [pltpu.SemaphoreType.DMA((3,))]
     else:
-        operands = (length, recv, dense, bias)
-        specs = [smem, vmem, vmem, vmem]
         shapes += [jax.ShapeDtypeStruct(one, F32) for one in sums]
         extra = []
     return pl.pallas_call(
@@ -495,6 +529,8 @@
             pltpu.VMEM((8, width), F32),
             pltpu.VMEM((neg_total, width), BF),
             pltpu.VMEM((128, heads * 128), BF),
+            pltpu.VMEM((width, same.shape[-1]), BF),
+            pltpu.SemaphoreType.DMA((pieces * blocks,)),
         ],
         compiler_params=pltpu.CompilerParams(vmem_limit_bytes=60 * 1024 * 1024),
         cost_estimate=pl.CostEstimate(
@@ -502,6 +538,105 @@
         ),
         name="history_last" if last else "history_first",
     )(*operands)
+
+
+def prepare_kernel(
+    rows_dev,
+    col_count,
+    len_ref,
+    spots_ref,
+    items_ref,
+    times_ref,
+    table_ref,
+    w_in_ref,
+    w_out_ref,
+    gains_ref,
+    told_ref,
+    payload_ref,
+    stage_s,
+):
+    slots, seq = items_ref.shape
+    own, width = w_out_ref.shape
+    blocks = told_ref.shape[0] // col_count
+    per = seq // blocks
+    payload_ref[:, 0 : 4 * width] = w_in_ref[...].astype(BF)
+    payload_ref[:, 4 * width : 5 * width] = w_out_ref[...].astype(BF)
+    for index in range(spots_ref.shape[0]):
+        stage_s[index : index + 1, :] = table_ref[pl.ds(spots_ref[index], 1), :]
+    for index in range(spots_ref.shape[0] // own):
+        payload_ref[:, 5 * width + index * 128 : 5 * width + (index + 1) * 128] = stage_s[
+            index * own : (index + 1) * own, :
+        ].astype(BF)
+    square = jnp.zeros((128, 128), F32)
+    stage_s[...] = jnp.zeros_like(stage_s)
+    stage_s[0 : gains_ref.shape[0], 0:own] = gains_ref[...]
+    square = stage_s[0:128, :].T
+    payload_ref[:, 6 * width : 6 * width + 128] = square[0:own, :].astype(BF)
+    before = jnp.where(
+        lax.broadcasted_iota(jnp.int32, (128, 128), 0) < lax.broadcasted_iota(jnp.int32, (128, 128), 1),
+        1.0,
+        0.0,
+    ).astype(BF)
+    block_row = lax.broadcasted_iota(jnp.int32, (blocks, seq), 0)
+    time = lax.broadcasted_iota(jnp.int32, (1, seq), 1)
+    lane = lax.broadcasted_iota(jnp.int32, (1, 128), 1)
+    lengths = jnp.zeros((1, 128), jnp.int32)
+    for slot in range(slots):
+        lengths = jnp.where(lane == slot, len_ref[slot], lengths)
+        item = items_ref[slot : slot + 1, :]
+        block = jnp.zeros((1, seq), jnp.int32)
+        for index in range(1, blocks):
+            block = block + jnp.where(item >= index * rows_dev, 1, 0)
+        place = item - block * rows_dev
+        member = jnp.where(block_row == block, 1.0, 0.0)
+        counts = []
+        running = jnp.zeros((blocks, 1), F32)
+        for part in range(seq // 128):
+            piece = member[:, part * 128 : (part + 1) * 128]
+            counts.append(dot_nn(piece.astype(BF), before) + running)
+            running = running + jnp.sum(piece, axis=1, keepdims=True)
+        rank = jnp.sum(member * jnp.concatenate(counts, axis=1), axis=0, keepdims=True)
+        target = block * per + rank.astype(jnp.int32)
+        upper = lax.shift_right_logical(place, 6)
+        late = lax.shift_right_logical(time, 5)
+        values = [upper, place - upper * 64, late, time - late * 32, times_ref[slot : slot + 1, :]]
+        values = jnp.concatenate(values + [jnp.zeros((11, seq), jnp.int32)], axis=0)
+        values = values.astype(F32).astype(BF)
+        for index in range(seq // 256):
+            span = slice(index * 256, (index + 1) * 256)
+            hot = jnp.where(
+                lax.broadcasted_iota(jnp.int32, (256, seq), 0) + index * 256 == target, 1.0, 0.0
+            ).astype(BF)
+            moved = dot_nt(values, hot).astype(jnp.int32)
+            rows = [moved[0:1] * 64 + moved[1:2], moved[2:3] * 32 + moved[3:4], moved[4:5]]
+            for inner in range(256 // per):
+                cut = slice(inner * per, (inner + 1) * per)
+                row = jnp.concatenate([one[:, cut] for one in rows], axis=0)
+                if per < 128:
+                    row = jnp.concatenate([row, jnp.zeros((3, 128 - per), jnp.int32)], axis=1)
+                for one in range(col_count):
+                    told_ref[one * blocks + index * (256 // per) + inner, 3 * slot : 3 * slot + 3, :] = row
+    for index in range(told_ref.shape[0]):
+        told_ref[index, 3 * slots : 3 * slots + 1, :] = lengths
+
+
+def prepare_call(lengths, spots, items, times, table, w_in, w_out, gains, devices, col_count):
+    slots = items.shape[0]
+    own, width = w_out.shape
+    smem = pl.BlockSpec(memory_space=pltpu.SMEM)
+    vmem = pl.BlockSpec(memory_space=pltpu.VMEM)
+    return pl.pallas_call(
+        functools.partial(prepare_kernel, table.shape[0], col_count),
+        out_shape=(
+            jax.ShapeDtypeStruct((devices, 3 * slots + 1, 128), jnp.int32),
+            jax.ShapeDtypeStruct((own, 6 * width + 128), BF),
+        ),
+        in_specs=[smem, smem] + [vmem] * 6,
+        out_specs=(vmem, vmem),
+        scratch_shapes=[pltpu.VMEM((128, 128), F32)],
+        compiler_params=pltpu.CompilerParams(vmem_limit_bytes=60 * 1024 * 1024),
+        name="prepare",
+    )(lengths, spots, items, times, table, w_in, w_out, gains)
 
 
 def lookup_kernel(hist_ref, ids_ref, about_ref, table_ref, found_ref, stage_s):
@@ -922,52 +1057,36 @@
     own_negs = (
         lax.dynamic_slice_in_dim(negatives, row_place * neg_own, neg_own) - row_place * rows_dev
     )
-    neg_rows = table[own_negs].astype(BF)
-    neg_rows = neg_rows.reshape(neg_own // own, own, piece).transpose(1, 0, 2)
-    dense = lax.all_gather(
-        jnp.concatenate(
-            [
-                w_in.astype(BF),
-                w_out.astype(BF),
-                neg_rows.reshape(own, -1),
-                jnp.pad(gains.T, ((0, 0), (0, 128 - gains.shape[0]))).astype(BF),
-            ],
-            axis=1,
-        ),
-        BOTH,
-        axis=0,
-        tiled=True,
-    )
-    if not blocked:
+    told, payload = prepare_call(
+        lengths[:, 0],
+        own_negs,
+        items[:, 0],
+        time_buckets[:, 0],
+        table,
+        w_in,
+        w_out,
+        gains,
+        devices,
+        col_count,
+    )
+    bias = bias_line(rab)
+    heard = exchange(told, BOTH)
+    if blocked:
+        half = row_count // 2
+        same = jnp.stack([payload] + swap_parts([payload] * (half - 1), "row", row_count, 2))
+        same = jnp.stack([same] + swap_parts([same] * (col_count - 1), "col", col_count, 1))
+        same = same.reshape(devices // 2, own, -1)
+        other = lax.ppermute(same, "row", [(place, place ^ 1) for place in range(row_count)])
+    else:
+        dense = lax.all_gather(payload, BOTH, axis=0, tiled=True)
         neg_rows = (
             dense[:, 5 * width : 6 * width]
             .reshape(col_count, row_count, own, neg_own // own, piece)
             .transpose(1, 3, 2, 0, 4)
             .reshape(neg_total, width)
         )
-        dense = jnp.concatenate([dense[:, : 5 * width], neg_rows, dense[:, 6 * width :]], axis=1)
-    bias = bias_line(rab)
-    mine = items[:, 0]
-    key, sorted_items, sorted_times = lax.sort(
-        (mine // rows_dev * seq + jnp.arange(seq)[None, :], mine, time_buckets[:, 0]),
-        dimension=1,
-        num_keys=1,
-    )
-    block = key // seq
-    about = jnp.stack([sorted_items - block * rows_dev, key - block * seq, sorted_times], axis=1)
-    about = about.reshape(slots, 3, row_count, per).transpose(2, 0, 1, 3)
-    about = jnp.pad(about, ((0, 0), (0, 0), (0, 0), (0, 128 - per))).reshape(row_count, -1, 128)
-    told = jnp.concatenate(
-        [
-            about,
-            jnp.broadcast_to(
-                jnp.pad(lengths[:, 0], (0, 128 - slots))[None, None], (row_count, 1, 128)
-            ),
-        ],
-        axis=1,
-    )
-    told = jnp.broadcast_to(told[None], (col_count,) + told.shape).reshape(devices, -1, 128)
-    heard = exchange(told, BOTH)
+        same = jnp.concatenate([dense[:, : 5 * width], neg_rows, dense[:, 6 * width :]], axis=1)
+        other = same
     about = heard[:, : 3 * slots].reshape(devices * slots, 3, 128)
     ids = about[:, 0]
     every_length = heard[:, 3 * slots, :slots].reshape(-1)
@@ -999,9 +1118,10 @@
         found = lookup_call(hist[slot], ids, about, table, per)
         sent.append(exchange(found, BOTH).reshape(col_count, row_count, per + 16, piece))
     core = (row_place % 2).reshape(1)
-    first = history_call(my_length[0:1], sent[0], dense, bias, core, None, blocked)
+    spot = jnp.stack([lax.axis_index("col"), row_place // 2, row_place % 2])
+    first = history_call(my_length[0:1], spot, sent[0], same, other, bias, None, blocked)
     back = [exchange(first[0].reshape(devices, per, piece), BOTH)]
-    final = history_call(my_length[1:2], sent[1], dense, bias, core, first[1:], blocked)
+    final = history_call(my_length[1:2], spot, sent[1], same, other, bias, first[1:], blocked)
     final_rows, back[0] = lax.optimization_barrier((final[0], back[0]))
     back.append(exchange(final_rows.reshape(devices, per, piece), BOTH))
     grad_misc, keep, send = final[1:]

time: 317 us -> 273 us (0.86)
  waiting for transfers between devices: 68.2 us -> 47.9 us
  between operations: 15.8 us -> 0.96 us
  Pallas kernels: 141 us -> 135 us
  local copies, waits for them, and re-layouts: 15.2 us -> 10.5 us
  starting transfers between devices: 55.7 us -> 60.3 us
    all_to_all x5, waiting for transfers between devices: 51.6 us -> 22.4 us  [exchange(): lax.all_to_all(values, axes, split_axis=0, concat_axis=0, tiled=True, axi...]
    pallas_call x2, Pallas kernels: 92.8 us -> 83.4 us  [history_call(): pl.pallas_call(functools.partial(history_kernel, last, blocked), out_shap...]
    ppermute x6 -> x12, starting transfers between devices: 7.87 us -> 17.1 us  [swap_parts(): gots.append(lax.ppermute(send, axis, pairs))]
    ppermute x6 -> x12, waiting for transfers between devices: 16.5 us -> 25.5 us  [swap_parts(): gots.append(lax.ppermute(send, axis, pairs))]
    all_to_all x5, starting transfers between devices: 47.5 us -> 42.8 us  [exchange(): lax.all_to_all(values, axes, split_axis=0, concat_axis=0, tiled=True, axi...]
    pallas_call x0 -> x1, Pallas kernels: none -> 3.84 us  [prepare_call(): pl.pallas_call(functools.partial(prepare_kernel, table.shape[0], col_coun...]
    unnamed x32 -> x33, local copies, waits for them, and re-layouts: 6.6 us -> 6.66 us
  transfers between devices with their start and end apart: 13 -> 19, of which waited for: 6 -> 8; matrix products, arithmetic and copies ran while one was open for 3% -> 3% of each run, Pallas kernels for 41% -> 44%
where the time goes in v3:
time: 273 us; the launch traced here: 272 us
  Pallas kernels  135 us (49%)
  starting transfers between devices  60.3 us (22%)
  waiting for transfers between devices  47.9 us (18%)
  blocking collectives  10.8 us (4%)
  local copies, waits for them, and re-layouts  10.5 us (4%)
  other arithmetic  6.25 us (2%)
    pallas_call x2, Pallas kernels, history_call(): pl.pallas_call(functools.partial(history_kernel, last, blocked), out_shap...  83.4 us
    all_to_all x5, starting transfers between devices, exchange(): lax.all_to_all(values, axes, split_axis=0, concat_axis=0, tiled=True, axi...  42.8 us
    ppermute x12, waiting for transfers between devices, swap_parts(): gots.append(lax.ppermute(send, axis, pairs))  25.5 us
    all_to_all x5, waiting for transfers between devices, exchange(): lax.all_to_all(values, axes, split_axis=0, concat_axis=0, tiled=True, axi...  22.4 us
    pallas_call x2, Pallas kernels, scatter_call(): pl.pallas_call(scatter_kernel, out_shape=jax.ShapeDtypeStruct((rows, piec...  17.7 us
    ppermute x12, starting transfers between devices, swap_parts(): gots.append(lax.ppermute(send, axis, pairs))  17.1 us
    pallas_call x2, Pallas kernels, lookup_call(): pl.pallas_call(lookup_kernel, out_shape=jax.ShapeDtypeStruct((count, per...  12.9 us
    all_to_all x1, blocking collectives, exchange(): lax.all_to_all(values, axes, split_axis=0, concat_axis=0, tiled=True, axi...  10.8 us
  transfers between devices with their start and end apart: 19, of which 8 were waited for; matrix products, arithmetic and copies ran while one was open for 3% of the time, Pallas kernels for 44%

profile of v3, /device:TPU:0, one launch (start us, length us, event | category | flops | bytes accessed | tf_op | source)
XLA Modules:
  0.0 272.1 jit_solution(6303536983638178140)
XLA Ops:
  3.3 3.8 %prepare.1 = (s32[32,7,128]{2,1,0:T(8,128)}, bf16[16,3200]{1,0:T(8,128)(2,1)}) custom-call(s32[2]{0:T(128)} %bitcast.56, s32[64]{0:T(128)} %dynamic-slice_subtract_fusion.spots_ref, s32[2,1024]{1,0:T(2,128)} %get-tuple-element.125.items_ref, s32[2,1024]{1,0:T(2,128)} %get-tuple-element.124.times_ref, f32[3200,128]{1,0:T(8,128)} %table_ref.7, ...), custom_call_target="tpu_custom_call" | custom-call | tf_op jit(solution)/shard_map/prepare/pallas_call | solution.py:628
  7.1 5.0 %collective-permute-start.2 = (bf16[16,3200]{1,0:T(8,128)(2,1)}, bf16[16,3200]{1,0:T(8,128)(2,1)S(1)}, u32[]{:S(2)}, u32[]{:S(2)}) collective-permute-start(bf16[16,3200]{1,0:T(8,128)(2,1)} %get-tuple-element.67), channel_id=1, source_target_pairs={{0,6},{1,7},{2,4},{3,5},{4,2},{5,3},{6,0},{7,1},{8,14},{9,15},{10,... | collective-permute-start | bytes 307208 | tf_op jit(solution)/shard_map/ppermute | solution.py:1004
  12.8 6.0 %all-to-all-start = ((s32[32,7,128]{2,1,0:T(8,128)}), s32[32,7,128]{2,1,0:T(8,128)S(1)}, u32[]{:S(2)}, u32[]{:S(2)}) async-start(s32[32,7,128]{2,1,0:T(8,128)} %get-tuple-element.66), calls=%async_computation | async-start | bytes 262144 | tf_op jit(solution)/shard_map/all_to_all | solution.py:975
  29.3 6.4 %lookup.3 = bf16[32,144,128]{2,1,0:T(8,128)(2,1)} custom-call(s32[32]{0:T(128)} %get-tuple-element.120.hist_ref, s32[64,128]{1,0:T(8,128)} %bitcast.52, s32[64,3,128]{2,1,0:T(4,128)} %copy-done.11, f32[3200,128]{1,0:T(8,128)} %table_ref.7), custom_call_target="tpu_custom_call" | custom-call | flops 5000000000 | bytes 4000000 | tf_op jit(solution)/shard_map/lookup/pallas_call | solution.py:664
  35.8 3.3 %all-to-all-start.2 = ((bf16[32,144,128]{2,1,0:T(8,128)(2,1)}), bf16[32,144,128]{2,1,0:T(8,128)(2,1)S(1)}, u32[]{:S(2)}, u32[]{:S(2)}) async-start(bf16[32,144,128]{2,1,0:T(8,128)(2,1)} %lookup.3), calls=%async_computation.2 | async-start | bytes 2359296 | tf_op jit(solution)/shard_map/all_to_all | solution.py:975
  39.1 6.6 %collective-permute-done.5 = bf16[4,16,3200]{2,1,0:T(8,128)(2,1)S(1)} collective-permute-done((bf16[4,16,3200]{2,1,0:T(8,128)(2,1)S(1)}, bf16[4,16,3200]{2,1,0:T(8,128)(2,1)S(1)}, u32[]{:S(2)}, u32[]{:S(2)}) %collective-permute-start.5) | collective-permute-done | bytes 409632 | tf_op jit(solution)/shard_map/ppermute | solution.py:1004
  50.8 6.4 %lookup.2 = bf16[32,144,128]{2,1,0:T(8,128)(2,1)} custom-call(s32[32]{0:T(128)} %get-tuple-element.121.hist_ref, s32[64,128]{1,0:T(8,128)} %bitcast.53, s32[64,3,128]{2,1,0:T(4,128)} %copy-done.11, f32[3200,128]{1,0:T(8,128)} %table_ref.7), custom_call_target="tpu_custom_call" | custom-call | flops 5000000000 | bytes 4000000 | tf_op jit(solution)/shard_map/lookup/pallas_call | solution.py:664
  57.2 12.2 %all-to-all-done.2 = bf16[32,144,128]{2,1,0:T(8,128)(2,1)S(1)} async-done(((bf16[32,144,128]{2,1,0:T(8,128)(2,1)}), bf16[32,144,128]{2,1,0:T(8,128)(2,1)S(1)}, u32[]{:S(2)}, u32[]{:S(2)}) %all-to-all-start.2) | async-done | bytes 1179680 | tf_op jit(solution)/shard_map/all_to_all | solution.py:975
  69.4 3.4 %all-to-all-start.1 = ((bf16[32,144,128]{2,1,0:T(8,128)(2,1)}), bf16[32,144,128]{2,1,0:T(8,128)(2,1)}, u32[]{:S(2)}, u32[]{:S(2)}) async-start(bf16[32,144,128]{2,1,0:T(8,128)(2,1)} %lookup.2), calls=%async_computation.1 | async-start | bytes 2359296 | tf_op jit(solution)/shard_map/all_to_all | solution.py:975
  72.8 64.8 %history_first.1 = (bf16[4,8,128,128]{3,2,1,0:T(8,128)(2,1)}, f32[16,512]{1,0:T(8,128)}, f32[512,2048]{1,0:T(8,128)}, f32[512,512]{1,0:T(8,128)}, f32[512,512]{1,0:T(8,128)}) custom-call(s32[1]{0:T(128)} %get-tuple-element.122.refs_0_, s32[3]{0:T(128)} %pad_add_fusion.1.refs_1_, bf16[4,8,144,128]{3,2,1,0:T(8,128)(2,1)} %bitcast.39, ...), custom_call_target="tpu_custom_call" | custom-call | flops 40000000000 | bytes 20000000 | tf_op jit(solution)/shard_map/history_first/pallas_call | solution.py:501
  137.7 4.9 %all-to-all-start.3 = ((bf16[32,128,128]{2,1,0:T(8,128)(2,1)}), bf16[32,128,128]{2,1,0:T(8,128)(2,1)S(1)}, u32[]{:S(2)}, u32[]{:S(2)}) async-start(bf16[32,128,128]{2,1,0:T(8,128)(2,1)} %bitcast.43), calls=%async_computation.3 | async-start | bytes 2097152 | tf_op jit(solution)/shard_map/all_to_all | solution.py:975
  142.5 18.5 %history_last.1 = (bf16[4,8,128,128]{3,2,1,0:T(8,128)(2,1)}, f32[16,512]{1,0:T(8,128)}, bf16[256,3200]{1,0:T(8,128)(2,1)}, bf16[256,3200]{1,0:T(8,128)(2,1)}) custom-call(s32[1]{0:T(128)} %get-tuple-element.123.refs_0_, s32[3]{0:T(128)} %pad_add_fusion.1.refs_1_, bf16[4,8,144,128]{3,2,1,0:T(8,128)(2,1)} %bitcast.7.refs_2_, bf16[16,16,3200]{2,1,0:T(8,128)(2,1)} %bitcast.38, ...), custom_call_target="tpu_custom_call" | custom-call | flops 40000000000 | bytes 20000000 | tf_op jit(solution)/shard_map/history_last/pallas_call | solution.py:501
  161.4 8.7 %all-to-all-done.3 = bf16[32,128,128]{2,1,0:T(8,128)(2,1)S(1)} async-done(((bf16[32,128,128]{2,1,0:T(8,128)(2,1)}), bf16[32,128,128]{2,1,0:T(8,128)(2,1)S(1)}, u32[]{:S(2)}, u32[]{:S(2)}) %all-to-all-start.3) | async-done | bytes 1048608 | tf_op jit(solution)/shard_map/all_to_all | solution.py:975
  171.1 25.3 %all-to-all-start.4 = ((bf16[32,128,128]{2,1,0:T(8,128)(2,1)}), bf16[32,128,128]{2,1,0:T(8,128)(2,1)S(1)}, u32[]{:S(2)}, u32[]{:S(2)}) async-start(bf16[32,128,128]{2,1,0:T(8,128)(2,1)} %bitcast.40), calls=%async_computation.4 | async-start | bytes 2097152 | tf_op jit(solution)/shard_map/all_to_all | solution.py:975
  197.6 3.4 %fold.2 = (f32[64,3200]{1,0:T(8,128)}, bf16[64,3200]{1,0:T(8,128)(2,1)}, bf16[64,3200]{1,0:T(8,128)(2,1)}, bf16[64,3200]{1,0:T(8,128)(2,1)}) custom-call(s32[1]{0:T(128)} %bitcast.4.place_ref, bf16[256,3200]{1,0:T(8,128)(2,1)} %get-tuple-element.77.base_ref, bf16[256,3200]{1,0:T(8,128)(2,1)} %copy-done.1), custom_call_target="tpu_custom_call" | custom-call | tf_op jit(solution)/shard_map/fold/pallas_call | solution.py:801
  204.5 8.6 %scatter.2.refs_0_ = f32[3200,128]{1,0:T(8,128)} custom-call(s32[32]{0:T(128)} %get-tuple-element.120.hist_ref, s32[64,128]{1,0:T(8,128)} %bitcast.54, bf16[4096,128]{1,0:T(8,128)(2,1)} %bitcast.42), custom_call_target="tpu_custom_call" | custom-call | flops 6000000000 | bytes 4000000 | tf_op jit(solution)/shard_map/scatter/pallas_call | solution.py:711
  213.0 5.3 %collective-permute-done.8.refs_0_ = bf16[64,3200]{1,0:T(8,128)(2,1)S(1)} collective-permute-done((bf16[64,3200]{1,0:T(8,128)(2,1)}, bf16[64,3200]{1,0:T(8,128)(2,1)S(1)}, u32[]{:S(2)}, u32[]{:S(2)}) %collective-permute-start.8) | collective-permute-done | bytes 409632 | tf_op jit(solution)/shard_map/ppermute | solution.py:1004
  219.4 10.4 %collective-permute-done.10.refs_2_ = bf16[64,3200]{1,0:T(8,128)(2,1)S(1)} collective-permute-done((bf16[64,3200]{1,0:T(8,128)(2,1)}, bf16[64,3200]{1,0:T(8,128)(2,1)S(1)}, u32[]{:S(2)}, u32[]{:S(2)}) %collective-permute-start.10) | collective-permute-done | bytes 409632 | tf_op jit(solution)/shard_map/ppermute | solution.py:1004
  230.5 2.3 fold.3
  233.7 2.6 collective-permute-start.12
  238.2 9.2 %scatter.3.table_ref = f32[3200,128]{1,0:T(8,128)} custom-call(s32[32]{0:T(128)} %get-tuple-element.121.hist_ref, s32[64,128]{1,0:T(8,128)} %bitcast.55, bf16[4096,128]{1,0:T(8,128)(2,1)} %bitcast.41, f32[3200,128]{1,0:T(8,128)} %scatter.2.refs_0_), custom_call_target="tpu_custom_call" | custom-call | flops 6000000000 | bytes 4000000 | tf_op jit(solution)/shard_map/scatter/pallas_call | solution.py:711
  248.1 3.2 %gather_up.1 = (f32[3200,128]{1,0:T(8,128)}, f32[16,3200]{1,0:T(8,128)}, f32[8,128]{1,0:T(8,128)}, f32[32,4,128]{2,1,0:T(4,128)}) custom-call(s32[64]{0:T(128)} %dynamic-slice_subtract_fusion.spots_ref, f32[3200,128]{1,0:T(8,128)} %scatter.3.table_ref, f32[16,512]{1,0:T(8,128)} %get-tuple-element.76.misc_ref, f32[16,3200]{1,0:T(8,128)} %get-tuple-element.84.base_ref, ...), custom_call_target="tpu_custom_call" | custom-call | tf_op jit(solution)/shard_map/gather_up/pallas_call | solution.py:765
  251.3 10.8 %all_to_all.30.heard_ref = f32[32,4,128]{2,1,0:T(4,128)} all-to-all(f32[32,4,128]{2,1,0:T(4,128)} %get-tuple-element.88), channel_id=1, replica_groups=mesh['col'=4,'row'=8] {'col','row'}, dimensions={0} | all-to-all | bytes 131072 | tf_op jit(solution)/shard_map/all_to_all | solution.py:975
  262.1 8.7 %update.1 = (f32[8,128]{1,0:T(8,128)}, f32[3200,128]{1,0:T(8,128)}, f32[3200,128]{1,0:T(8,128)}, f32[3200,128]{1,0:T(8,128)}, bf16[3200,128]{1,0:T(8,128)(2,1)},...) custom-call(s32[1]{0:T(128)} %bitcast.1.count_ref, ...), custom_call_target="tpu_custom_call" | custom-call | tf_op jit(solution)/shard_map/update/pallas_call | solution.py:945
  (83 shorter events, 31.3 us)
Async XLA Ops:
  7.1 11.7 %collective-permute-start.2 = (bf16[16,3200]{1,0:T(8,128)(2,1)}, bf16[16,3200]{1,0:T(8,128)(2,1)S(1)}, u32[]{:S(2)}, u32[]{:S(2)}) collective-permute-start(bf16[16,3200]{1,0:T(8,128)(2,1)} %get-tuple-element.67), channel_id=1, source_target_pairs={{0,6},{1,7},{2,4},{3,5},{4,2},{5,3},{6,0},{7,1},{8,14},{9,15},{10,... | collective-permute-start | bytes 307208 | tf_op jit(solution)/shard_map/ppermute | solution.py:1004
  12.1 8.8 %collective-permute-start.1 = (bf16[16,3200]{1,0:T(8,128)(2,1)}, bf16[16,3200]{1,0:T(8,128)(2,1)S(1)}, u32[]{:S(2)}, u32[]{:S(2)}) collective-permute-start(bf16[16,3200]{1,0:T(8,128)(2,1)} %get-tuple-element.67), channel_id=1, source_target_pairs={{0,4},{1,5},{2,6},{3,7},{4,0},{5,1},{6,2},{7,3},{8,12},{9,13},{10,... | collective-permute-start | bytes 307208 | tf_op jit(solution)/shard_map/ppermute | solution.py:1004
  12.1 8.8 %collective-permute-start = (bf16[16,3200]{1,0:T(8,128)(2,1)}, bf16[16,3200]{1,0:T(8,128)(2,1)S(1)}, u32[]{:S(2)}, u32[]{:S(2)}) collective-permute-start(bf16[16,3200]{1,0:T(8,128)(2,1)} %get-tuple-element.67), channel_id=1, source_target_pairs={{0,2},{1,3},{2,0},{3,1},{4,6},{5,7},{6,4},{7,5},{8,10},{9,11},{10,... | collective-permute-start | bytes 307208 | tf_op jit(solution)/shard_map/ppermute | solution.py:1004
  12.8 14.2 %all-to-all-start = ((s32[32,7,128]{2,1,0:T(8,128)}), s32[32,7,128]{2,1,0:T(8,128)S(1)}, u32[]{:S(2)}, u32[]{:S(2)}) async-start(s32[32,7,128]{2,1,0:T(8,128)} %get-tuple-element.66), calls=%async_computation | async-start | bytes 262144 | tf_op jit(solution)/shard_map/all_to_all | solution.py:975
  21.9 17.1 %collective-permute-start.4 = (bf16[4,16,3200]{2,1,0:T(8,128)(2,1)S(1)}, bf16[4,16,3200]{2,1,0:T(8,128)(2,1)S(1)}, u32[]{:S(2)}, u32[]{:S(2)}) collective-permute-start(bf16[4,16,3200]{2,1,0:T(8,128)(2,1)S(1)} %get-tuple-element.116), channel_id=1, source_target_pairs={{0,16},{8,24},{16,0},{24,8},{1,17},{9,25},{17,1},{25,9},{2,18},{10... | collective-permute-start | bytes 1228808 | tf_op jit(solution)/shard_map/ppermute | solution.py:1004
  23.5 15.5 %collective-permute-start.3 = (bf16[4,16,3200]{2,1,0:T(8,128)(2,1)S(1)}, bf16[4,16,3200]{2,1,0:T(8,128)(2,1)S(1)}, u32[]{:S(2)}, u32[]{:S(2)}) collective-permute-start(bf16[4,16,3200]{2,1,0:T(8,128)(2,1)S(1)} %get-tuple-element.116), channel_id=1, source_target_pairs={{0,8},{8,0},{16,24},{24,16},{1,9},{9,1},{17,25},{25,17},{2,10},{10... | collective-permute-start | bytes 1228808 | tf_op jit(solution)/shard_map/ppermute | solution.py:1004
  25.0 20.7 %collective-permute-start.5 = (bf16[4,16,3200]{2,1,0:T(8,128)(2,1)S(1)}, bf16[4,16,3200]{2,1,0:T(8,128)(2,1)S(1)}, u32[]{:S(2)}, u32[]{:S(2)}) collective-permute-start(bf16[4,16,3200]{2,1,0:T(8,128)(2,1)S(1)} %get-tuple-element.116), channel_id=1, source_target_pairs={{0,24},{8,16},{16,8},{24,0},{1,25},{9,17},{17,9},{25,1},{2,26},{10... | collective-permute-start | bytes 1228808 | tf_op jit(solution)/shard_map/ppermute | solution.py:1004
  35.8 33.7 %all-to-all-start.2 = ((bf16[32,144,128]{2,1,0:T(8,128)(2,1)}), bf16[32,144,128]{2,1,0:T(8,128)(2,1)S(1)}, u32[]{:S(2)}, u32[]{:S(2)}) async-start(bf16[32,144,128]{2,1,0:T(8,128)(2,1)} %lookup.3), calls=%async_computation.2 | async-start | bytes 2359296 | tf_op jit(solution)/shard_map/all_to_all | solution.py:975
  39.1 6.7 %copy-start.5 = (bf16[4,16,3200]{2,1,0:T(8,128)(2,1)}, bf16[4,16,3200]{2,1,0:T(8,128)(2,1)S(1)}, u32[]{:S(2)}) copy-start(bf16[4,16,3200]{2,1,0:T(8,128)(2,1)S(1)} %collective-permute-done.4) | copy-start | bytes 1228804
  39.1 6.6 %copy-start.6 = (bf16[4,16,3200]{2,1,0:T(8,128)(2,1)}, bf16[4,16,3200]{2,1,0:T(8,128)(2,1)S(1)}, u32[]{:S(2)}) copy-start(bf16[4,16,3200]{2,1,0:T(8,128)(2,1)S(1)} %collective-permute-done.3) | copy-start | bytes 1228804
  48.0 9.2 %copy-start = (bf16[4,4,16,3200]{3,2,1,0:T(8,128)(2,1)}, bf16[4,4,16,3200]{3,2,1,0:T(8,128)(2,1)S(1)}, u32[]{:S(2)}) copy-start(bf16[4,4,16,3200]{3,2,1,0:T(8,128)(2,1)S(1)} %pad_maximum_fusion) | copy-start | bytes 4915204
  48.0 24.8 %collective-permute-start.6 = (bf16[16,16,3200]{2,1,0:T(8,128)(2,1)S(1)}, bf16[16,16,3200]{2,1,0:T(8,128)(2,1)}, u32[]{:S(2)}, u32[]{:S(2)}) collective-permute-start(bf16[16,16,3200]{2,1,0:T(8,128)(2,1)S(1)} %bitcast.36), channel_id=1, source_target_pairs={{0,1},{1,0},{2,3},{3,2},{4,5},{5,4},{6,7},{7,6},{8,9},{9,8},{10,11... | collective-permute-start | bytes 4915208 | tf_op jit(solution)/shard_map/ppermute | solution.py:1079
  69.4 68.2 %all-to-all-start.1 = ((bf16[32,144,128]{2,1,0:T(8,128)(2,1)}), bf16[32,144,128]{2,1,0:T(8,128)(2,1)}, u32[]{:S(2)}, u32[]{:S(2)}) async-start(bf16[32,144,128]{2,1,0:T(8,128)(2,1)} %lookup.2), calls=%async_computation.1 | async-start | bytes 2359296 | tf_op jit(solution)/shard_map/all_to_all | solution.py:975
  137.7 32.5 %all-to-all-start.3 = ((bf16[32,128,128]{2,1,0:T(8,128)(2,1)}), bf16[32,128,128]{2,1,0:T(8,128)(2,1)S(1)}, u32[]{:S(2)}, u32[]{:S(2)}) async-start(bf16[32,128,128]{2,1,0:T(8,128)(2,1)} %bitcast.43), calls=%async_computation.3 | async-start | bytes 2097152 | tf_op jit(solution)/shard_map/all_to_all | solution.py:975
  161.1 35.3 %collective-permute-start.7 = (bf16[256,3200]{1,0:T(8,128)(2,1)}, bf16[256,3200]{1,0:T(8,128)(2,1)S(1)}, u32[]{:S(2)}, u32[]{:S(2)}) collective-permute-start(bf16[256,3200]{1,0:T(8,128)(2,1)} %get-tuple-element.78), channel_id=1, source_target_pairs={{0,1},{1,0},{2,3},{3,2},{4,5},{5,4},{6,7},{7,6},{8,9},{9,8},{10,11... | collective-permute-start | bytes 4915208 | tf_op jit(solution)/shard_map/ppermute | solution.py:1012
  171.1 66.1 %all-to-all-start.4 = ((bf16[32,128,128]{2,1,0:T(8,128)(2,1)}), bf16[32,128,128]{2,1,0:T(8,128)(2,1)S(1)}, u32[]{:S(2)}, u32[]{:S(2)}) async-start(bf16[32,128,128]{2,1,0:T(8,128)(2,1)} %bitcast.40), calls=%async_computation.4 | async-start | bytes 2097152 | tf_op jit(solution)/shard_map/all_to_all | solution.py:975
  201.0 17.3 %collective-permute-start.8 = (bf16[64,3200]{1,0:T(8,128)(2,1)}, bf16[64,3200]{1,0:T(8,128)(2,1)S(1)}, u32[]{:S(2)}, u32[]{:S(2)}) collective-permute-start(bf16[64,3200]{1,0:T(8,128)(2,1)} %get-tuple-element.80), channel_id=1, source_target_pairs={{0,8},{8,0},{16,24},{24,16},{1,9},{9,1},{17,25},{25,17},{2,10},{10... | collective-permute-start | bytes 1228808 | tf_op jit(solution)/shard_map/ppermute | solution.py:1004
  202.7 16.6 %collective-permute-start.9 = (bf16[64,3200]{1,0:T(8,128)(2,1)}, bf16[64,3200]{1,0:T(8,128)(2,1)S(1)}, u32[]{:S(2)}, u32[]{:S(2)}) collective-permute-start(bf16[64,3200]{1,0:T(8,128)(2,1)} %get-tuple-element.82), channel_id=1, source_target_pairs={{0,16},{8,24},{16,0},{24,8},{1,17},{9,25},{17,1},{25,9},{2,18},{10... | collective-permute-start | bytes 1228808 | tf_op jit(solution)/shard_map/ppermute | solution.py:1004
  204.2 25.6 %collective-permute-start.10 = (bf16[64,3200]{1,0:T(8,128)(2,1)}, bf16[64,3200]{1,0:T(8,128)(2,1)S(1)}, u32[]{:S(2)}, u32[]{:S(2)}) collective-permute-start(bf16[64,3200]{1,0:T(8,128)(2,1)} %get-tuple-element.83), channel_id=1, source_target_pairs={{0,24},{8,16},{16,8},{24,0},{1,25},{9,17},{17,9},{25,1},{2,26},{10... | collective-permute-start | bytes 1228808 | tf_op jit(solution)/shard_map/ppermute | solution.py:1004
  218.3 11.4 %copy-start.8 = (bf16[64,3200]{1,0:T(8,128)(2,1)}, bf16[64,3200]{1,0:T(8,128)(2,1)S(1)}, u32[]{:S(2)}) copy-start(bf16[64,3200]{1,0:T(8,128)(2,1)S(1)} %collective-permute-done.8.refs_0_) | copy-start | bytes 1228804
  219.4 10.4 %copy-start.9 = (bf16[64,3200]{1,0:T(8,128)(2,1)}, bf16[64,3200]{1,0:T(8,128)(2,1)S(1)}, u32[]{:S(2)}) copy-start(bf16[64,3200]{1,0:T(8,128)(2,1)S(1)} %collective-permute-done.9.refs_1_) | copy-start | bytes 1228804
  232.9 14.5 %collective-permute-start.11 = (bf16[16,3200]{1,0:T(8,128)(2,1)}, bf16[16,3200]{1,0:T(8,128)(2,1)S(1)}, u32[]{:S(2)}, u32[]{:S(2)}) collective-permute-start(bf16[16,3200]{1,0:T(8,128)(2,1)} %get-tuple-element.85), channel_id=1, source_target_pairs={{0,2},{1,3},{2,0},{3,1},{4,6},{5,7},{6,4},{7,5},{8,10},{9,11},{10,... | collective-permute-start | bytes 307208 | tf_op jit(solution)/shard_map/ppermute | solution.py:1004
  233.7 13.7 %collective-permute-start.12 = (bf16[16,3200]{1,0:T(8,128)(2,1)}, bf16[16,3200]{1,0:T(8,128)(2,1)S(1)}, u32[]{:S(2)}, u32[]{:S(2)}) collective-permute-start(bf16[16,3200]{1,0:T(8,128)(2,1)} %get-tuple-element.86), channel_id=1, source_target_pairs={{0,4},{1,5},{2,6},{3,7},{4,0},{5,1},{6,2},{7,3},{8,12},{9,13},{10,... | collective-permute-start | bytes 307208 | tf_op jit(solution)/shard_map/ppermute | solution.py:1004
  236.3 11.1 %collective-permute-start.13 = (bf16[16,3200]{1,0:T(8,128)(2,1)}, bf16[16,3200]{1,0:T(8,128)(2,1)S(1)}, u32[]{:S(2)}, u32[]{:S(2)}) collective-permute-start(bf16[16,3200]{1,0:T(8,128)(2,1)} %get-tuple-element.87), channel_id=1, source_target_pairs={{0,6},{1,7},{2,4},{3,5},{4,2},{5,3},{6,0},{7,1},{8,14},{9,15},{10,... | collective-permute-start | bytes 307208 | tf_op jit(solution)/shard_map/ppermute | solution.py:1004
  (11 other events, 12.5 us)
